TPU v7x, 128 devices: a whole 4x4x4 slice. The times are simulated.
128 devices in a mesh: ctx: 32 (over y, x, core), tp: 4 (over z).
Axes of the slice: x: 4, y: 4, z: 4, core: 2. Of those that a mesh axis runs over, the one named last changes fastest.
Arguments:
- block_input: float32 [8192, 1536], P('ctx'), may hold values from -6 to 6
- gain_in: bfloat16 [1536], replicated, may hold values from 0.5 to 1.5
- w_query: bfloat16 [1536, 1536], P(None, 'tp'), may hold values from -0.15625 to 0.15625
- w_key: bfloat16 [1536, 1536], P(None, 'tp'), may hold values from -0.15625 to 0.15625
- w_value: bfloat16 [1536, 1536], P(None, 'tp'), may hold values from -0.15625 to 0.15625
- w_path: bfloat16 [1536, 1536], P(None, 'tp'), may hold values from -0.15625 to 0.15625
- w_beta: bfloat16 [1536, 12], P(None, 'tp'), may hold values from -0.15625 to 0.15625
- w_out: bfloat16 [1536, 1536], P('tp'), may hold values from -0.15625 to 0.15625
- gain_mid: bfloat16 [1536], replicated, may hold values from 0.5 to 1.5
- w_gate: bfloat16 [1536, 4096], P(None, 'tp'), may hold values from -0.15625 to 0.15625
- w_up: bfloat16 [1536, 4096], P(None, 'tp'), may hold values from -0.15625 to 0.15625
- w_down: bfloat16 [4096, 1536], P('tp'), may hold values from -0.09375 to 0.09375
- out_grad: float32 [8192, 1536], P('ctx'), may hold values from -6 to 6
- lengths: int32 [3], replicated, may hold values from 1 to 8064, 8192 in all
Outputs:
- block_output: float32 [8192, 1536], P('ctx')
- input_grad: float32 [8192, 1536], P('ctx')
- gain_in_grad: float32 [1536], P('ctx')
- query_grad: float32 [1536, 1536], P('ctx', 'tp')
- key_grad: float32 [1536, 1536], P('ctx', 'tp')
- value_grad: float32 [1536, 1536], P('ctx', 'tp')
- path_grad: float32 [1536, 1536], P('ctx', 'tp')
- beta_grad: float32 [1536, 12], P('ctx', 'tp')
- out_proj_grad: float32 [1536, 1536], P('tp', 'ctx')
- gain_mid_grad: float32 [1536], P('ctx')
- gate_grad: float32 [1536, 4096], P('ctx', 'tp')
- up_grad: float32 [1536, 4096], P('ctx', 'tp')
- down_grad: float32 [4096, 1536], P('tp', 'ctx')
Inputs may be any that keep to these rules, and one draw needn't show every extreme that they name: `lengths`: the 3 sequences lie end to end and fill all 8192 tokens; the longest holds exactly 8064 tokens.
All inputs are finite; a program needn't handle non-finite values.
Results may differ from a plain program's by a relative error of at most 0.0085.
The roundings to bfloat16 on the way count: a program that leaves them out, or rounds other values in their place, can miss the bound.
Values sent between devices are 32-bit elements; how exact they have to be, the bound alone decides.
No kernel may reach another device: no remote copies, remote signals or barrier semaphores. Data moves between devices by JAX's collectives and lax.ppermute only.
A program may use at most 192 MiB of HBM per device.

v0:
```python
import jax
import jax.numpy as jnp
from jax import lax
from jax.sharding import PartitionSpec as P

EPSILON = 1e-06
HEAD_EPSILON = 0.01
HIGHEST = lax.Precision.HIGHEST


def prefix_2(part, axis, combine, identity, reverse):
    count = lax.axis_size(axis)
    place = lax.axis_index(axis)
    ahead = count - 1 - place if reverse else place
    gathered = jax.tree.map(lambda a: lax.all_gather(a, axis), part)
    state = jax.tree.map(lambda a, e: jnp.zeros_like(a) + jnp.asarray(e, a.dtype), part, identity)

    def one(lap, state):
        source = count - 1 - lap if reverse else lap
        return combine(
            state, jax.tree.map(lambda a: lax.dynamic_index_in_dim(a, source, 0, False), gathered)
        )

    return lax.fori_loop(0, ahead, one, state)


def rms_scale(values, gain_vec):
    return (
        values * lax.rsqrt(jnp.mean(values * values, axis=-1, keepdims=True) + EPSILON) * gain_vec
    )


def unit_rows(values):
    return values * lax.rsqrt(jnp.sum(values * values, axis=-1, keepdims=True) + EPSILON)


def segment_of(positions, lengths):
    starts = jnp.cumsum(lengths) - lengths
    return jnp.sum((starts[None, :] <= positions[:, None]).astype(jnp.int32), axis=1) - 1


def masks_of(segment, previous, dtype):
    carry_in = (segment == previous).astype(dtype)
    same_seq = segment[:, None] == segment[None, :]
    last_seq = (segment == segment[-1]).astype(dtype)
    return (carry_in, same_seq, last_seq)


def upper_inverse(left_side, diagonal_part):
    length = left_side.shape[0]
    indices = jnp.arange(length)
    inverse = jnp.diag(1.0 / diagonal_part)
    width = 1
    while width < length:
        same_pair = indices[:, None] // (2 * width) == indices[None, :] // (2 * width)
        lower_half = indices[:, None] // width < indices[None, :] // width
        linking = jnp.where(same_pair & lower_half, left_side, 0.0)
        inverse = inverse - jnp.dot(
            inverse, jnp.dot(linking, inverse, precision=HIGHEST), precision=HIGHEST
        )
        width = width * 2
    return inverse


def block_parts(query, keys, values, paths, strength, same_seq, last_seq, carry_all):
    length = query.shape[0]
    head_width = query.shape[1]
    indices = jnp.arange(length)
    up_to = indices[:, None] <= indices[None, :]
    later_mask = indices[:, None] < indices[None, :]
    gram_matrix = jnp.dot(paths, paths.T, precision=HIGHEST)
    left_side = jnp.where(later_mask, gram_matrix, 0.0)
    inverse = upper_inverse(left_side, 1.0 / strength)
    paths_query = jnp.where(up_to, jnp.dot(paths, query.T, precision=HIGHEST), 0.0)
    coefficient = jnp.dot(inverse, paths_query, precision=HIGHEST)
    turned_query = query - jnp.dot(coefficient.T, paths, precision=HIGHEST)
    keys_paths = jnp.where(later_mask, jnp.dot(keys, paths.T, precision=HIGHEST), 0.0)
    folded = jnp.dot(keys_paths, inverse, precision=HIGHEST)
    turned_keys = keys - jnp.dot(folded, paths, precision=HIGHEST)
    scores = jnp.dot(keys, query.T, precision=HIGHEST) - jnp.dot(
        folded, paths_query, precision=HIGHEST
    )
    scores = jnp.where(up_to & same_seq, scores, 0.0)
    inside = jnp.dot(scores.T, values, precision=HIGHEST)
    product = jnp.dot(paths.T, jnp.dot(inverse, paths, precision=HIGHEST), precision=HIGHEST)
    transition = carry_all * (jnp.eye(head_width, dtype=query.dtype) - product)
    update = jnp.dot(values.T, turned_keys * last_seq[:, None], precision=HIGHEST)
    return (inside, turned_query, transition, update)


def heads_pieces(query_raw, keys_raw, values, paths_raw, beta_raw, same_seq, last_seq, carry_all):
    query = unit_rows(query_raw)
    keys = unit_rows(keys_raw)
    paths = unit_rows(paths_raw)
    strength = 1.0 + jax.nn.sigmoid(beta_raw)
    mapped = jax.vmap(block_parts, in_axes=(1, 1, 1, 1, 1, None, None, None), out_axes=(1, 1, 0, 0))
    return mapped(query, keys, values, paths, strength, same_seq, last_seq, carry_all)


def heads_finish(inside, turned_query, carry_in, carried):
    mixed = inside + carry_in[:, None, None] * jnp.einsum(
        "lhs,hvs->lhv", turned_query, carried, precision=HIGHEST
    )
    return mixed * lax.rsqrt(jnp.mean(mixed * mixed, axis=-1, keepdims=True) + HEAD_EPSILON)


def compose(earlier, latter):
    joined = jnp.einsum("hab,hbc->hac", earlier[0], latter[0], precision=HIGHEST)
    moved = jnp.einsum("hab,hbc->hac", earlier[1], latter[0], precision=HIGHEST) + latter[1]
    return (joined, moved)


def contract_rows(left, right):
    return lax.dot_general(
        left, right, (((0,), (0,)), ((), ())), preferred_element_type=jnp.float32
    )


def contract_cols(left, right):
    return lax.dot_general(
        left, right, (((1,), (1,)), ((), ())), preferred_element_type=jnp.float32
    )


def local(
    block_input,
    gain_in,
    w_query,
    w_key,
    w_value,
    w_path,
    w_beta,
    w_out,
    gain_mid,
    w_gate,
    w_up,
    w_down,
    out_grad,
    lengths,
):
    tokens_here = block_input.shape[0]
    heads_here = w_beta.shape[1]
    head_width = w_query.shape[1] // heads_here
    positions = lax.axis_index("ctx") * tokens_here + jnp.arange(tokens_here, dtype=jnp.int32)
    segment = segment_of(positions, lengths)
    previous = segment_of(positions[:1] - 1, lengths)[0]
    carry_in, same_seq, last_seq = masks_of(segment, previous, jnp.float32)
    gain_first = gain_in.astype(jnp.float32)
    gain_second = gain_mid.astype(jnp.float32)
    identity = (
        jnp.broadcast_to(
            jnp.eye(head_width, dtype=jnp.float32), (heads_here, head_width, head_width)
        ),
        jnp.zeros((heads_here, head_width, head_width), jnp.float32),
    )

    def local_pieces(query_raw, keys_raw, values, paths_raw, beta_local):
        return heads_pieces(
            query_raw, keys_raw, values, paths_raw, beta_local, same_seq, last_seq, carry_in[-1]
        )

    def local_finish(inside_part, turned_part, state):
        return heads_finish(inside_part, turned_part, carry_in, state)

    first_low = rms_scale(block_input, gain_first).astype(jnp.bfloat16)
    head_weights = (w_query, w_key, w_value, w_path)
    raw_list = [
        jnp.dot(first_low, weight, preferred_element_type=jnp.float32).reshape(
            tokens_here, heads_here, head_width
        )
        for weight in head_weights
    ]
    beta_raw = jnp.dot(first_low, w_beta, preferred_element_type=jnp.float32)
    pieces, pieces_pull = jax.vjp(
        local_pieces, raw_list[0], raw_list[1], raw_list[2], raw_list[3], beta_raw
    )
    inside, turned_query, transition, update = pieces
    prefix = prefix_2((transition, update), "ctx", compose, identity, False)
    carried = prefix[1]
    normed, finish_pull = jax.vjp(local_finish, inside, turned_query, carried)
    normed_low = normed.reshape(tokens_here, heads_here * head_width).astype(jnp.bfloat16)
    residual = block_input + lax.psum(
        jnp.dot(normed_low, w_out, preferred_element_type=jnp.float32), "tp"
    )
    second_low = rms_scale(residual, gain_second).astype(jnp.bfloat16)
    gate_val = jnp.dot(second_low, w_gate, preferred_element_type=jnp.float32)
    up_val = jnp.dot(second_low, w_up, preferred_element_type=jnp.float32)
    hidden_low = (jax.nn.silu(gate_val) * up_val).astype(jnp.bfloat16)
    block_output = residual + lax.psum(
        jnp.dot(hidden_low, w_down, preferred_element_type=jnp.float32), "tp"
    )
    ffn_low = out_grad.astype(jnp.bfloat16)
    down_term = contract_rows(hidden_low, ffn_low)
    hidden_grad = contract_cols(ffn_low, w_down)
    sigmoid_gate = jax.nn.sigmoid(gate_val)
    silu_gate = gate_val * sigmoid_gate
    gate_low = (
        hidden_grad * up_val * sigmoid_gate * (1.0 + gate_val * (1.0 - sigmoid_gate))
    ).astype(jnp.bfloat16)
    up_low = (hidden_grad * silu_gate).astype(jnp.bfloat16)
    gate_term = contract_rows(second_low, gate_low)
    up_term = contract_rows(second_low, up_low)
    second_grad = lax.psum(contract_cols(gate_low, w_gate) + contract_cols(up_low, w_up), "tp")
    _, second_pull = jax.vjp(rms_scale, residual, gain_second)
    residual_norm_grad, gain_second_term = second_pull(second_grad)
    residual_grad = out_grad + residual_norm_grad
    attn_low = residual_grad.astype(jnp.bfloat16)
    out_term = contract_rows(normed_low, attn_low)
    normed_grad = contract_cols(attn_low, w_out).reshape(tokens_here, heads_here, head_width)
    inside_grad, turned_grad, state_grad = finish_pull(normed_grad)
    flipped = jnp.swapaxes(transition, 1, 2)
    suffix = prefix_2((flipped, state_grad), "ctx", compose, identity, True)
    later_grad = suffix[1]
    transition_grad = jnp.einsum("hvs,hvt->hst", carried, later_grad, precision=HIGHEST)
    raw_grads = pieces_pull((inside_grad, turned_grad, transition_grad, later_grad))
    grad_lows = [
        raw_grads[index].reshape(tokens_here, -1).astype(jnp.bfloat16) for index in range(5)
    ]
    query_term = contract_rows(first_low, grad_lows[0])
    key_term = contract_rows(first_low, grad_lows[1])
    value_term = contract_rows(first_low, grad_lows[2])
    path_term = contract_rows(first_low, grad_lows[3])
    beta_term = contract_rows(first_low, grad_lows[4])
    first_partial = contract_cols(grad_lows[0], w_query) + contract_cols(grad_lows[1], w_key)
    first_partial = (
        first_partial + contract_cols(grad_lows[2], w_value) + contract_cols(grad_lows[3], w_path)
    )
    first_partial = first_partial + contract_cols(grad_lows[4], w_beta)
    first_grad = lax.psum(first_partial, "tp")
    _, first_norm_pull = jax.vjp(rms_scale, block_input, gain_first)
    input_norm_grad, gain_first_term = first_norm_pull(first_grad)
    input_grad = residual_grad + input_norm_grad
    summed = (
        lax.psum_scatter(gain_first_term, "ctx", scatter_dimension=0, tiled=True),
        lax.psum_scatter(query_term, "ctx", scatter_dimension=0, tiled=True),
        lax.psum_scatter(key_term, "ctx", scatter_dimension=0, tiled=True),
        lax.psum_scatter(value_term, "ctx", scatter_dimension=0, tiled=True),
        lax.psum_scatter(path_term, "ctx", scatter_dimension=0, tiled=True),
        lax.psum_scatter(beta_term, "ctx", scatter_dimension=0, tiled=True),
        lax.psum_scatter(out_term, "ctx", scatter_dimension=1, tiled=True),
        lax.psum_scatter(gain_second_term, "ctx", scatter_dimension=0, tiled=True),
        lax.psum_scatter(gate_term, "ctx", scatter_dimension=0, tiled=True),
        lax.psum_scatter(up_term, "ctx", scatter_dimension=0, tiled=True),
        lax.psum_scatter(down_term, "ctx", scatter_dimension=1, tiled=True),
    )
    return (
        block_output,
        input_grad,
        summed[0],
        summed[1],
        summed[2],
        summed[3],
        summed[4],
        summed[5],
        summed[6],
        summed[7],
        summed[8],
        summed[9],
        summed[10],
    )


def solution(mesh):
    in_specs = (
        P("ctx", None),
        P(),
        P(None, "tp"),
        P(None, "tp"),
        P(None, "tp"),
        P(None, "tp"),
        P(None, "tp"),
        P("tp", None),
        P(),
        P(None, "tp"),
        P(None, "tp"),
        P("tp", None),
        P("ctx", None),
        P(),
    )
    out_specs = (
        P("ctx", None),
        P("ctx", None),
        P("ctx"),
        P("ctx", "tp"),
        P("ctx", "tp"),
        P("ctx", "tp"),
        P("ctx", "tp"),
        P("ctx", "tp"),
        P("tp", "ctx"),
        P("ctx"),
        P("ctx", "tp"),
        P("ctx", "tp"),
        P("tp", "ctx"),
    )
    return jax.shard_map(local, mesh=mesh, in_specs=in_specs, out_specs=out_specs, check_vma=False)
```

profile of v0, /device:TPU:0, one launch (start us, length us, event | category | flops | bytes accessed | tf_op | source)
XLA Modules:
  0.0 1596.6 jit_solution(935526015053818873)
XLA Ops:
  78.8 25.5 %all-gather.9.cloned.1.call-done = f32[96,128,128]{2,1,0:T(8,128)} async-done(((f32[3,128,128]{2,1,0:T(8,128)}), f32[96,128,128]{2,1,0:T(8,128)}) %all-gather.9.cloned.1.call-update) | async-done | bytes 6291472 | tf_op jit(solution)/shard_map/all_gather | solution.py:15
  104.4 50.9 %all-gather.11.cloned.1.call-done = f32[96,128,128]{2,1,0:T(8,128)} async-done(((f32[3,128,128]{2,1,0:T(8,128)}), f32[96,128,128]{2,1,0:T(8,128)}) %all-gather.11.cloned.1.call-update) | async-done | bytes 6291472 | tf_op jit(solution)/shard_map/all_gather | solution.py:15
  164.4 272.4 %all-reduce.8.cloned.1.call-done = f32[256,1536]{1,0:T(8,128)} async-done(((f32[256,1536]{1,0:T(8,128)}), f32[256,1536]{1,0:T(8,128)}) %all-reduce.8.cloned.1.call-update) | async-done | bytes 1572880 | tf_op jit(solution)/shard_map/psum | solution.py:182
  450.5 48.9 %all-reduce.10.cloned.1.call-done = f32[256,1536]{1,0:T(8,128)} async-done(((f32[256,1536]{1,0:T(8,128)}), f32[256,1536]{1,0:T(8,128)}) %all-reduce.10.cloned.1.call-update) | async-done | bytes 1572880 | tf_op jit(solution)/shard_map/psum | solution.py:203
  499.4 3.0 multiply_reduce_fusion
  508.1 3.2 fusion.249
  525.0 3.1 fusion.81
  532.1 18.4 %all-gather.13.cloned.1.call-done = f32[96,128,128]{2,1,0:T(8,128)} async-done(((f32[3,128,128]{2,1,0:T(8,128)}), f32[96,128,128]{2,1,0:T(8,128)}) %all-gather.13.cloned.1.call-update) | async-done | bytes 6291472 | tf_op jit(solution)/shard_map/all_gather | solution.py:15
  550.5 50.2 %all-gather.15.cloned.1.call-done = f32[96,128,128]{2,1,0:T(8,128)} async-done(((f32[3,128,128]{2,1,0:T(8,128)}), f32[96,128,128]{2,1,0:T(8,128)}) %all-gather.15.cloned.1.call-update) | async-done | bytes 6291472 | tf_op jit(solution)/shard_map/all_gather | solution.py:15
  600.7 79.6 %while.27 = (s32[]{:T(128)}, f32[3,128,128]{1,2,0:T(8,128)S(1)}, s32[]{:T(128)}, f32[32,3,128,128]{3,2,1,0:T(8,128)}, f32[32,3,128,128]{3,2,1,0:T(8,128)}, /*index=5*/s32[]{:T(128)}, s32[]{:T(128)}, s32[]{:T(128)}, s32[]{:T(128)}) while((s32[]{:T(128)}, f32[3,128,128]{1,2,0:T(8,128)S(1)}, s32[]{:T(128)}, f32[32,3,128,128]{3,2,1,0:T(8,128)}, ...), condition=%wide.region_18.19_spmd, body=%wide.region_17.18_spmd.sunk | while | flops 75546632 | bytes 1966235 | solution.py:24
  767.4 3.7 fusion.133
  772.4 3.7 fusion.261
  777.1 3.6 fusion.260
  791.5 35.6 %reduce-scatter.28.cloned.1.call-done = f32[48,3]{1,0:T(8,128)} async-done(((f32[1536,3]{1,0:T(8,128)}), f32[48,3]{1,0:T(8,128)}) %reduce-scatter.28.cloned.1.call-update) | async-done | bytes 592
  828.4 77.3 %all-reduce.12.cloned.1.call-done = (f32[256,1536]{1,0:T(8,128)}, f32[256,1536]{1,0:T(8,128)}) async-done(((f32[256,1536]{1,0:T(8,128)}, f32[256,1536]{1,0:T(8,128)}), (f32[256,1536]{1,0:T(8,128)}, f32[256,1536]{1,0:T(8,128)})) %all-reduce.12.cloned.1.call-update) | async-done | bytes 3145744 | tf_op jit(solution)/shard_map/psum | solution.py:189
  909.4 128.0 %all-reduce.2 = (f32[1536]{0:T(1024)S(1)}, f32[1536]{0:T(1024)S(1)}) all-reduce(f32[1536]{0:T(1024)S(1)} %get-tuple-element.185, f32[1536]{0:T(1024)S(1)} %copy-done.190), channel_id=6, replica_groups=mesh['ctx'=32,'tp'=4] {'ctx'}, use_global_device_ids=true, to_apply=%region_25.26.clone | all-reduce | flops 3072 | bytes 24576
  1038.6 4.0 fusion.17
  1042.6 29.0 %reduce-scatter.12.cloned.1.call-done = f32[48,384]{1,0:T(8,128)} async-done(((f32[1536,384]{1,0:T(8,128)}), f32[48,384]{1,0:T(8,128)}) %reduce-scatter.12.cloned.1.call-update) | async-done | bytes 73744 | tf_op jit(solution)/shard_map/reduce_scatter | solution.py:235
  1071.6 89.9 %reduce-scatter.26.cloned.1.call-done = f32[1024,48]{0,1:T(8,128)} async-done(((f32[1024,1536]{0,1:T(8,128)}), f32[1024,48]{0,1:T(8,128)}) %reduce-scatter.26.cloned.1.call-update) | async-done | bytes 196624 | tf_op jit(solution)/shard_map/reduce_scatter | solution.py:244
  1161.5 90.2 %reduce-scatter.24.cloned.1.call-done = f32[48,1024]{1,0:T(8,128)} async-done(((f32[1536,1024]{1,0:T(8,128)}), f32[48,1024]{1,0:T(8,128)}) %reduce-scatter.24.cloned.1.call-update) | async-done | bytes 196624 | tf_op jit(solution)/shard_map/reduce_scatter | solution.py:243
  1251.7 89.8 %reduce-scatter.22.cloned.1.call-done = f32[48,1024]{1,0:T(8,128)} async-done(((f32[1536,1024]{1,0:T(8,128)}), f32[48,1024]{1,0:T(8,128)}) %reduce-scatter.22.cloned.1.call-update) | async-done | bytes 196624 | tf_op jit(solution)/shard_map/reduce_scatter | solution.py:242
  1341.5 82.9 %reduce-scatter.18.cloned.1.call-done = f32[48,384]{1,0:T(8,128)} async-done(((f32[1536,384]{1,0:T(8,128)}), f32[48,384]{1,0:T(8,128)}) %reduce-scatter.18.cloned.1.call-update) | async-done | bytes 73744 | tf_op jit(solution)/shard_map/reduce_scatter | solution.py:238
  1424.4 82.5 %reduce-scatter.16.cloned.1.call-done = f32[48,384]{1,0:T(8,128)} async-done(((f32[1536,384]{1,0:T(8,128)}), f32[48,384]{1,0:T(8,128)}) %reduce-scatter.16.cloned.1.call-update) | async-done | bytes 73744 | tf_op jit(solution)/shard_map/reduce_scatter | solution.py:237
  1506.9 83.0 %reduce-scatter.14.cloned.1.call-done = f32[48,384]{1,0:T(8,128)} async-done(((f32[1536,384]{1,0:T(8,128)}), f32[48,384]{1,0:T(8,128)}) %reduce-scatter.14.cloned.1.call-update) | async-done | bytes 73744 | tf_op jit(solution)/shard_map/reduce_scatter | solution.py:236
  (765 shorter events, 297.1 us)
Async XLA Ops:
  7.2 435.8 %copy-start = (bf16[1024,1536]{1,0:T(8,128)(2,1)S(1)}, bf16[1024,1536]{1,0:T(8,128)(2,1)}, u32[]{:S(2)}) copy-start(bf16[1024,1536]{1,0:T(8,128)(2,1)} %param.29) | copy-start | bytes 9437188
  7.2 13.1 copy-start.213
  7.2 97.2 %all-gather.9.cloned.1.call-start = ((), (), s32[]{:S(2)}) async-start(), calls=%async_computation.19 | async-start | bytes 6488064 | tf_op jit(solution)/shard_map/all_gather | solution.py:15
  25.0 15.7 copy-start.2
  26.3 14.4 copy-start.164
  52.8 102.5 %all-gather.11.cloned.1.call-start = ((), (), s32[]{:S(2)}) async-start(), calls=%async_computation.20 | async-start | bytes 6488064 | tf_op jit(solution)/shard_map/all_gather | solution.py:15
  62.8 374.1 %all-reduce.8.cloned.1.call-start = ((), (), s32[]{:S(2)}) async-start(), calls=%async_computation.9 | async-start | bytes 3145728 | tf_op jit(solution)/shard_map/psum | solution.py:182
  162.7 336.7 %all-reduce.10.cloned.1.call-start = ((), (), s32[]{:S(2)}) async-start(), calls=%async_computation.10 | async-start | bytes 3145728 | tf_op jit(solution)/shard_map/psum | solution.py:203
  448.7 101.8 %all-gather.13.cloned.1.call-start = ((), (), s32[]{:S(2)}) async-start(), calls=%async_computation.21 | async-start | bytes 6488064 | tf_op jit(solution)/shard_map/all_gather | solution.py:15
  450.5 150.2 %all-gather.15.cloned.1.call-start = ((), (), s32[]{:S(2)}) async-start(), calls=%async_computation.22 | async-start | bytes 6488064 | tf_op jit(solution)/shard_map/all_gather | solution.py:15
  507.9 319.2 %reduce-scatter.28.cloned.1.call-start = ((), (), s32[]{:S(2)}) async-start(), calls=%async_computation.23 | async-start | bytes 811008
  600.7 81.3 %copy-start.51 = (f32[3,128,128]{1,2,0:T(8,128)S(1)}, f32[3,128,128]{1,2,0:T(8,128)}, u32[]{:S(2)}) copy-start(f32[3,128,128]{1,2,0:T(8,128)} %get-tuple-element.141) | copy-start | bytes 589828
  753.3 152.5 %all-reduce.12.cloned.1.call-start = ((), (), s32[]{:S(2)}) async-start(), calls=%async_computation.24 | async-start | bytes 6291456 | tf_op jit(solution)/shard_map/psum | solution.py:189
  759.4 283.3 %reduce-scatter.20.cloned.1.call-start = ((), (), s32[]{:S(2)}) async-start(), calls=%async_computation.15 | async-start | bytes 2433024 | tf_op jit(solution)/shard_map/reduce_scatter | solution.py:240
  762.9 308.8 %reduce-scatter.12.cloned.1.call-start = ((), (), s32[]{:S(2)}) async-start(), calls=%async_computation.11 | async-start | bytes 2433024 | tf_op jit(solution)/shard_map/reduce_scatter | solution.py:235
  765.9 395.6 %reduce-scatter.26.cloned.1.call-start = ((), (), s32[]{:S(2)}) async-start(), calls=%async_computation.18 | async-start | bytes 6488064 | tf_op jit(solution)/shard_map/reduce_scatter | solution.py:244
  771.1 480.6 %reduce-scatter.24.cloned.1.call-start = ((), (), s32[]{:S(2)}) async-start(), calls=%async_computation.17 | async-start | bytes 6488064 | tf_op jit(solution)/shard_map/reduce_scatter | solution.py:243
  776.1 565.4 %reduce-scatter.22.cloned.1.call-start = ((), (), s32[]{:S(2)}) async-start(), calls=%async_computation.16 | async-start | bytes 6488064 | tf_op jit(solution)/shard_map/reduce_scatter | solution.py:242
  780.8 643.6 %reduce-scatter.18.cloned.1.call-start = ((), (), s32[]{:S(2)}) async-start(), calls=%async_computation.14 | async-start | bytes 2433024 | tf_op jit(solution)/shard_map/reduce_scatter | solution.py:238
  783.7 723.2 %reduce-scatter.16.cloned.1.call-start = ((), (), s32[]{:S(2)}) async-start(), calls=%async_computation.13 | async-start | bytes 2433024 | tf_op jit(solution)/shard_map/reduce_scatter | solution.py:237
  786.7 803.2 %reduce-scatter.14.cloned.1.call-start = ((), (), s32[]{:S(2)}) async-start(), calls=%async_computation.12 | async-start | bytes 2433024 | tf_op jit(solution)/shard_map/reduce_scatter | solution.py:236
  789.6 116.1 %copy-start.11 = (f32[256,1536]{1,0:T(8,128)S(1)}, f32[256,1536]{1,0:T(8,128)}, u32[]{:S(2)}) copy-start(f32[256,1536]{1,0:T(8,128)} %copy-done.9) | copy-start | bytes 4718596
  908.7 129.9 %copy-start.212 = (f32[256]{0:T(256)S(1)}, f32[256]{0:T(256)}, u32[]{:S(2)}) copy-start(f32[256]{0:T(256)} %copy-done.211) | copy-start | bytes 3076
  1038.6 551.3 %copy-start.1 = (bf16[1024,1536]{1,0:T(8,128)(2,1)S(1)}, bf16[1024,1536]{1,0:T(8,128)(2,1)}, u32[]{:S(2)}) copy-start(bf16[1024,1536]{1,0:T(8,128)(2,1)} %param.29) | copy-start | bytes 9437188
  (207 other events, 409.4 us)
Sparse Core Ops, SparseCore 0:
  52.9 51.4 all-gather.8
  107.2 47.9 all-gather.10
  162.8 274.0 all-reduce.7
  448.8 50.6 all-reduce.9
  501.5 48.9 all-gather.12
  552.6 48.0 all-gather.14
  753.4 73.6 reduce-scatter.27
  830.0 75.6 all-reduce.11
  909.9 78.7 reduce-scatter.19
  993.1 78.5 reduce-scatter.11
  1076.0 85.4 reduce-scatter.25
  1166.1 85.5 reduce-scatter.23
  1256.0 85.4 reduce-scatter.21
  1345.9 78.4 reduce-scatter.17
  1428.4 78.4 reduce-scatter.15
  1511.3 78.5 reduce-scatter.13
where the time goes:
time: 1600 us
  waiting for transfers between devices  1130 us (71%)
  matrix products  209 us (13%)
  blocking collectives  128 us (8%)
  local copies, waits for them, and re-layouts  78.2 us (5%)
  other arithmetic  32.7 us (2%)
  between operations  19.2 us (1%)
    psum x1, waiting for transfers between devices, local(): lax.psum(jnp.dot(normed_low, w_out, preferred_element_type=jnp.float32),...  272 us
    all_gather x4, waiting for transfers between devices, prefix_2(): gathered = jax.tree.map(lambda a: lax.all_gather(a, axis), part)  145 us
    unnamed x1, blocking collectives  128 us
    reduce_scatter x1, waiting for transfers between devices, local(): lax.psum_scatter(up_term, 'ctx', scatter_dimension=0, tiled=True)  90.2 us
    reduce_scatter x1, waiting for transfers between devices, local(): lax.psum_scatter(down_term, 'ctx', scatter_dimension=1, tiled=True)  89.9 us
    reduce_scatter x1, waiting for transfers between devices, local(): lax.psum_scatter(gate_term, 'ctx', scatter_dimension=0, tiled=True)  89.8 us
    reduce_scatter x1, waiting for transfers between devices, local(): lax.psum_scatter(key_term, 'ctx', scatter_dimension=0, tiled=True)  83 us
    reduce_scatter x1, waiting for transfers between devices, local(): lax.psum_scatter(path_term, 'ctx', scatter_dimension=0, tiled=True)  82.9 us
  transfers between devices with their start and end apart: 16, of which 15 were waited for; matrix products, arithmetic and copies ran while one was open for 6% of the time, Pallas kernels for 0%

commit v1 on v0

v1 whole, which is shorter than its diff:
```python
import jax
import jax.numpy as jnp
from jax import lax
from jax.sharding import Mesh
from jax.sharding import PartitionSpec as P

EPSILON = 1e-06
HEAD_EPSILON = 0.01
HIGHEST = lax.Precision.HIGHEST
F32 = jnp.float32
BF16 = jnp.bfloat16
CTX = ("y", "x", "c")


def swap(value):
    return lax.ppermute(value, "c", [(0, 1), (1, 0)])


def shift(value, axis, step):
    count = lax.axis_size(axis)
    return lax.ppermute(value, axis, [(i, (i + step) % count) for i in range(count)])


def gather_all(value, axis):
    count = lax.axis_size(axis)
    spread = jnp.broadcast_to(value[None], (count,) + value.shape)
    return lax.all_to_all(spread, axis, 0, 0)


def pick(array, index, dim=0):
    return lax.dynamic_index_in_dim(array, index, dim, False)


def rms_scale(values, gain_vec):
    return (
        values * lax.rsqrt(jnp.mean(values * values, axis=-1, keepdims=True) + EPSILON) * gain_vec
    )


def unit_rows(values):
    return values * lax.rsqrt(jnp.sum(values * values, axis=-1, keepdims=True) + EPSILON)


def segment_of(positions, lengths):
    starts = jnp.cumsum(lengths) - lengths
    return jnp.sum((starts[None, :] <= positions[:, None]).astype(jnp.int32), axis=1) - 1


def masks_of(segment, previous, dtype):
    carry_in = (segment == previous).astype(dtype)
    same_seq = segment[:, None] == segment[None, :]
    last_seq = (segment == segment[-1]).astype(dtype)
    return (carry_in, same_seq, last_seq)


def upper_inverse(left_side, diagonal_part):
    length = left_side.shape[0]
    indices = jnp.arange(length)
    inverse = jnp.diag(1.0 / diagonal_part)
    width = 1
    while width < length:
        same_pair = indices[:, None] // (2 * width) == indices[None, :] // (2 * width)
        lower_half = indices[:, None] // width < indices[None, :] // width
        linking = jnp.where(same_pair & lower_half, left_side, 0.0)
        inverse = inverse - jnp.dot(
            inverse, jnp.dot(linking, inverse, precision=HIGHEST), precision=HIGHEST
        )
        width = width * 2
    return inverse


def block_parts(query, keys, values, paths, strength, same_seq, last_seq, carry_all):
    length = query.shape[0]
    head_width = query.shape[1]
    indices = jnp.arange(length)
    up_to = indices[:, None] <= indices[None, :]
    later_mask = indices[:, None] < indices[None, :]
    gram_matrix = jnp.dot(paths, paths.T, precision=HIGHEST)
    left_side = jnp.where(later_mask, gram_matrix, 0.0)
    inverse = upper_inverse(left_side, 1.0 / strength)
    paths_query = jnp.where(up_to, jnp.dot(paths, query.T, precision=HIGHEST), 0.0)
    coefficient = jnp.dot(inverse, paths_query, precision=HIGHEST)
    turned_query = query - jnp.dot(coefficient.T, paths, precision=HIGHEST)
    keys_paths = jnp.where(later_mask, jnp.dot(keys, paths.T, precision=HIGHEST), 0.0)
    folded = jnp.dot(keys_paths, inverse, precision=HIGHEST)
    turned_keys = keys - jnp.dot(folded, paths, precision=HIGHEST)
    scores = jnp.dot(keys, query.T, precision=HIGHEST) - jnp.dot(
        folded, paths_query, precision=HIGHEST
    )
    scores = jnp.where(up_to & same_seq, scores, 0.0)
    inside = jnp.dot(scores.T, values, precision=HIGHEST)
    product = jnp.dot(paths.T, jnp.dot(inverse, paths, precision=HIGHEST), precision=HIGHEST)
    transition = carry_all * (jnp.eye(head_width, dtype=query.dtype) - product)
    update = jnp.dot(values.T, turned_keys * last_seq[:, None], precision=HIGHEST)
    return (inside, turned_query, transition, update)


def heads_pieces(query_raw, keys_raw, values, paths_raw, beta_raw, same_seq, last_seq, carry_all):
    query = unit_rows(query_raw)
    keys = unit_rows(keys_raw)
    paths = unit_rows(paths_raw)
    strength = 1.0 + jax.nn.sigmoid(beta_raw)
    mapped = jax.vmap(block_parts, in_axes=(1, 1, 1, 1, 1, None, None, None), out_axes=(1, 1, 0, 0))
    return mapped(query, keys, values, paths, strength, same_seq, last_seq, carry_all)


def heads_finish(inside, turned_query, carry_in, carried):
    mixed = inside + carry_in[:, None, None] * jnp.einsum(
        "lhs,hvs->lhv", turned_query, carried, precision=HIGHEST
    )
    return mixed * lax.rsqrt(jnp.mean(mixed * mixed, axis=-1, keepdims=True) + HEAD_EPSILON)


def mul(left, right):
    return jnp.einsum("hab,hbc->hac", left, right, precision=HIGHEST)


def mul_t(left, right):
    return jnp.einsum("hab,hcb->hac", left, right, precision=HIGHEST)


def join_rows(mine, other, core):
    return jnp.where(
        core == 0,
        jnp.concatenate([mine, other], axis=-2),
        jnp.concatenate([other, mine], axis=-2),
    )


def rows_of(array, core):
    half = array.shape[-2] // 2
    return lax.dynamic_slice_in_dim(array, core * half, half, array.ndim - 2)


def forward_state(transition, update, place):
    row, col, core = place
    mate = swap(jnp.stack([transition, update]))
    first = core == 0
    t_0 = jnp.where(first, transition, mate[0])
    t_1 = jnp.where(first, mate[0], transition)
    u_0 = rows_of(jnp.where(first, update, mate[1]), core)
    u_1 = rows_of(jnp.where(first, mate[1], update), core)
    chip_t = rows_of(mul(t_0, t_1), core)
    chip_u = mul(u_0, t_1) + u_1
    along_x = gather_all(jnp.stack([chip_t, chip_u]), "x")
    t_x = join_rows(along_x[:, 0], swap(along_x[:, 0]), core)
    u_x = along_x[:, 1]
    t_23 = mul(t_x[2], t_x[3])
    row_t = rows_of(mul(mul(t_x[0], t_x[1]), t_23), core)
    row_u = mul(mul(u_x[0], t_x[1]) + u_x[1], t_23) + mul(u_x[2], t_x[3]) + u_x[3]
    along_y = gather_all(jnp.stack([row_t, row_u]), "y")
    t_y = join_rows(along_y[:, 0], swap(along_y[:, 0]), core)
    u_y = along_y[:, 1]
    state = jnp.zeros_like(u_0)
    for at in range(3):
        state = jnp.where(at < row, mul(state, t_y[at]) + u_y[at], state)
    for at in range(3):
        state = jnp.where(at < col, mul(state, t_x[at]) + u_x[at], state)
    state_1 = mul(state, t_0) + u_0
    other = swap(jnp.where(first, state_1, state))
    carried = join_rows(jnp.where(first, state, state_1), other, core)
    return carried, (t_0, t_1, t_x, t_y)


def backward_state(state_grad, kept, place):
    row, col, core = place
    t_0, t_1, t_x, t_y = kept
    first = core == 0
    mate = swap(rows_of(state_grad, 1 - core))
    mine = rows_of(state_grad, core)
    g_0 = jnp.where(first, mine, mate)
    g_1 = jnp.where(first, mate, mine)
    chip_g = mul_t(g_1, t_0) + g_0
    g_x = gather_all(chip_g, "x")
    row_g = g_x[3]
    for at in (2, 1, 0):
        row_g = mul_t(row_g, t_x[at]) + g_x[at]
    g_y = gather_all(row_g, "y")
    later = jnp.zeros_like(g_0)
    for at in (3, 2, 1):
        later = jnp.where(at > row, mul_t(later, t_y[at]) + g_y[at], later)
    for at in (3, 2, 1):
        later = jnp.where(at > col, mul_t(later, t_x[at]) + g_x[at], later)
    later_0 = mul_t(later, t_1) + g_1
    other = swap(jnp.where(first, later, later_0))
    return join_rows(jnp.where(first, later_0, later), other, core)


def contract_cols(left, right):
    return lax.dot_general(
        left, right, (((1,), (1,)), ((), ())), preferred_element_type=jnp.float32
    )


def dot32(left, right):
    return jnp.dot(left, right, preferred_element_type=jnp.float32)


def direct_sum(blocks, axis, dim):
    count = lax.axis_size(axis)
    me = lax.axis_index(axis)
    total = pick(blocks, me, dim)
    arrived = [
        shift(pick(blocks, (me + step) % count, dim), axis, step) for step in (1, count - 1, 2)
    ]
    for one in arrived:
        total = total + one
    return total


def scatter_ctx(groups, place):
    core = place[2]
    sums = []
    for rows, columns in groups:
        parts = rows.reshape(4, 4, 2, rows.shape[0] // 32, rows.shape[1])
        shape = (4, 4, rows.shape[0] // 32, columns.shape[1])
        theirs = dot32(pick(parts, 1 - core, 2).reshape(-1, rows.shape[1]), columns)
        mine = dot32(pick(parts, core, 2).reshape(-1, rows.shape[1]), columns)
        sums.append((mine + swap(theirs)).reshape(shape))
    return sums


def spread_xy(first, second):
    a = direct_sum(first, "x", 1)
    b = direct_sum(second, "y", 0)
    a = direct_sum(a, "y", 0)
    b = direct_sum(b, "x", 0)
    return a, b


def local(
    block_input,
    gain_in,
    w_query,
    w_key,
    w_value,
    w_path,
    w_beta,
    w_out,
    gain_mid,
    w_gate,
    w_up,
    w_down,
    out_grad,
    lengths,
):
    tokens_here, width = block_input.shape
    heads_here = w_beta.shape[1]
    head_width = w_query.shape[1] // heads_here
    head_cols = w_query.shape[1]
    place = tuple(lax.axis_index(name) for name in CTX)
    core = place[2]
    rank = lax.axis_index("z")
    ranks = lax.axis_size("z")
    part = tokens_here // ranks
    positions = lax.axis_index(CTX) * tokens_here + jnp.arange(tokens_here, dtype=jnp.int32)
    segment = segment_of(positions, lengths)
    previous = segment_of(positions[:1] - 1, lengths)[0]
    carry_in, same_seq, last_seq = masks_of(segment, previous, jnp.float32)
    gain_first = gain_in.astype(jnp.float32)
    gain_second = gain_mid.astype(jnp.float32)

    unity = (lengths[0] > 0).astype(F32)

    def part_of(array):
        return lax.dynamic_slice_in_dim(array, rank * part, part, 0)

    out_half = lax.dynamic_slice_in_dim(w_out, core * (head_cols // 2), head_cols // 2, 0)
    out_mine = lax.all_gather(out_half.astype(F32), "z", axis=0)
    out_other = swap(out_mine)
    out_pair = jnp.where(
        core == 0,
        jnp.stack([out_mine, out_other], axis=1),
        jnp.stack([out_other, out_mine], axis=1),
    )
    w_out_all = (out_pair * unity).reshape(width, width).astype(BF16)

    def local_pieces(query_raw, keys_raw, values, paths_raw, beta_local):
        return heads_pieces(
            query_raw, keys_raw, values, paths_raw, beta_local, same_seq, last_seq, carry_in[-1]
        )

    def local_finish(inside_part, turned_part, state):
        return heads_finish(inside_part, turned_part, carry_in, state)

    first_low = rms_scale(block_input, gain_first).astype(jnp.bfloat16)
    raw_list = [
        dot32(first_low, weight).reshape(tokens_here, heads_here, head_width)
        for weight in (w_query, w_key, w_value, w_path)
    ]
    beta_raw = dot32(first_low, w_beta)
    pieces, pieces_pull = jax.vjp(local_pieces, *raw_list, beta_raw)
    inside, turned_query, transition, update = pieces
    carried, kept = forward_state(transition, update, place)
    normed, finish_pull = jax.vjp(local_finish, inside, turned_query, carried)
    normed_low = normed.reshape(tokens_here, head_cols).astype(jnp.bfloat16)
    normed_all = gather_all(normed_low.astype(F32), "z") * unity
    normed_all = jnp.swapaxes(normed_all.astype(BF16), 0, 1).reshape(tokens_here, width)
    residual = block_input + dot32(normed_all, w_out_all)
    second_low = rms_scale(residual, gain_second).astype(jnp.bfloat16)
    gate_val = dot32(second_low, w_gate)
    up_val = dot32(second_low, w_up)
    hidden_low = (jax.nn.silu(gate_val) * up_val).astype(jnp.bfloat16)
    ffn_low = out_grad.astype(jnp.bfloat16)
    hidden_grad = contract_cols(ffn_low, w_down)
    sigmoid_gate = jax.nn.sigmoid(gate_val)
    silu_gate = gate_val * sigmoid_gate
    gate_low = (
        hidden_grad * up_val * sigmoid_gate * (1.0 + gate_val * (1.0 - sigmoid_gate))
    ).astype(jnp.bfloat16)
    up_low = (hidden_grad * silu_gate).astype(jnp.bfloat16)
    second_partial = contract_cols(gate_low, w_gate) + contract_cols(up_low, w_up)
    second_grad = jnp.sum(
        lax.all_to_all(second_partial.reshape(ranks, part, width), "z", 0, 0), axis=0
    )
    middle_part = part_of(residual)
    _, second_pull = jax.vjp(rms_scale, middle_part, gain_second)
    middle_norm_grad, gain_second_term = second_pull(second_grad)
    middle_grad = part_of(out_grad) + middle_norm_grad
    attn_low = middle_grad.astype(jnp.bfloat16)
    normed_grad = contract_cols(attn_low, w_out_all).reshape(part, ranks, head_cols)
    normed_grad = lax.all_to_all(jnp.swapaxes(normed_grad, 0, 1), "z", 0, 0)
    normed_grad = normed_grad.reshape(tokens_here, heads_here, head_width)
    inside_grad, turned_grad, state_grad = finish_pull(normed_grad)
    later_grad = backward_state(state_grad, kept, place)
    transition_grad = jnp.einsum("hvs,hvt->hst", carried, later_grad, precision=HIGHEST)
    raw_grads = pieces_pull((inside_grad, turned_grad, transition_grad, later_grad))
    grad_lows = [
        raw_grads[index].reshape(tokens_here, -1).astype(jnp.bfloat16) for index in range(5)
    ]
    first_partial = contract_cols(grad_lows[0], w_query) + contract_cols(grad_lows[1], w_key)
    first_partial = (
        first_partial + contract_cols(grad_lows[2], w_value) + contract_cols(grad_lows[3], w_path)
    )
    first_partial = first_partial + contract_cols(grad_lows[4], w_beta)
    first_grad = jnp.sum(
        lax.all_to_all(first_partial.reshape(ranks, part, width), "z", 0, 0), axis=0
    )
    _, first_norm_pull = jax.vjp(rms_scale, part_of(block_input), gain_first)
    input_norm_grad, gain_first_term = first_norm_pull(first_grad)
    input_grad = gather_all(middle_grad + input_norm_grad, "z").reshape(tokens_here, width)

    down_partial = dot32(hidden_low, w_down)
    down_partial, _ = lax.optimization_barrier((down_partial, second_grad))
    block_output = residual + lax.psum(down_partial, "z")

    second_t = second_low.T
    ffn_t = ffn_low.T
    first_t = first_low.T
    both_low = jnp.concatenate([gate_low, up_low], axis=1)
    cut = (both_low.shape[1] + hidden_low.shape[1]) // 2
    sums = scatter_ctx(
        [(second_t, both_low[:, :cut]), (second_t, both_low[:, cut:]), (ffn_t, hidden_low)], place
    )
    ffn_a, ffn_b = spread_xy(sums[0], jnp.concatenate(sums[1:], axis=-1))
    ffn_sum = jnp.concatenate([ffn_a, ffn_b], axis=-1)
    hidden_cols = w_gate.shape[1]
    gate_out = ffn_sum[:, :hidden_cols]
    up_out = ffn_sum[:, hidden_cols : 2 * hidden_cols]
    down_out = ffn_sum[:, 2 * hidden_cols :].T

    attn_all = lax.all_gather(attn_low.astype(F32), "z", axis=0, tiled=True)
    attn_t = (attn_all * unity).astype(BF16).T
    sums = scatter_ctx([(first_t, grad_lows[0]), (attn_t, normed_low)], place)
    query_out, out_out = spread_xy(sums[0], sums[1])
    tail = jnp.concatenate(
        grad_lows[1:] + [jnp.zeros((tokens_here, 128 - heads_here), BF16)], axis=1
    )
    cut = tail.shape[1] // 2
    sums = scatter_ctx([(first_t, tail[:, :cut]), (first_t, tail[:, cut:])], place)
    tail_sum = jnp.concatenate(spread_xy(sums[0], sums[1]), axis=-1)
    key_out = tail_sum[:, :head_cols]
    value_out = tail_sum[:, head_cols : 2 * head_cols]
    path_out = tail_sum[:, 2 * head_cols : 3 * head_cols]
    beta_out = tail_sum[:, 3 * head_cols : 3 * head_cols + heads_here]

    gains = jnp.stack([gain_first_term, gain_second_term]).reshape(2, 32, width // 32)
    gains = jnp.sum(lax.all_to_all(jnp.swapaxes(gains, 0, 1), CTX, 0, 0), axis=0)
    gains = jnp.sum(gather_all(gains, "z"), axis=0)
    return (
        block_output,
        input_grad,
        gains[0],
        query_out,
        key_out,
        value_out,
        path_out,
        beta_out,
        out_out.T,
        gains[1],
        gate_out,
        up_out,
        down_out,
    )


def solution(mesh):
    fine = Mesh(mesh.devices.reshape(4, 4, 2, 4), ("y", "x", "c", "z"))
    in_specs = (
        P(CTX, None),
        P(),
        P(None, "z"),
        P(None, "z"),
        P(None, "z"),
        P(None, "z"),
        P(None, "z"),
        P("z", None),
        P(),
        P(None, "z"),
        P(None, "z"),
        P("z", None),
        P(CTX, None),
        P(),
    )
    out_specs = (
        P(CTX, None),
        P(CTX, None),
        P(CTX),
        P(CTX, "z"),
        P(CTX, "z"),
        P(CTX, "z"),
        P(CTX, "z"),
        P(CTX, "z"),
        P("z", CTX),
        P(CTX),
        P(CTX, "z"),
        P(CTX, "z"),
        P("z", CTX),
    )
    return jax.shard_map(local, mesh=fine, in_specs=in_specs, out_specs=out_specs, check_vma=False)
```

time: 1600 us -> 662 us (0.41)
  waiting for transfers between devices: 1130 us -> 186 us
  blocking collectives: 128 us -> 0 us
  starting transfers between devices: 1.67 us -> 100 us
  other arithmetic: 32.7 us -> 69.7 us
    reduce_scatter x8 -> x0, waiting for transfers between devices: 547 us -> none  [the longest x1 90.2 us: local(): lax.psum_scatter(up_term, 'ctx', scatter_dimension=0, tiled=True)]
    psum x3 -> x1, waiting for transfers between devices: 399 us -> 0.01 us  [local(): block_output = residual + lax.psum(down_partial, 'z')]
    all_gather x4 -> x2, waiting for transfers between devices: 145 us -> 0.01 us  [the longest x1 0.01 us: local(): out_mine = lax.all_gather(out_half.astype(F32), 'z', axis=0)]
    unnamed x1 -> x0, blocking collectives: 128 us -> none
    all_to_all x0 -> x11, waiting for transfers between devices: none -> 95.2 us  [the longest x7 40.8 us: gather_all(): return lax.all_to_all(spread, axis, 0, 0)]
    ppermute x0 -> x50, waiting for transfers between devices: none -> 90.6 us  [the longest x36 88.5 us: shift(): lax.ppermute(value, axis, [(i, (i + step) % count) for i in range(count)])]
    ppermute x0 -> x50, starting transfers between devices: none -> 51.1 us  [the longest x36 48.3 us: shift(): lax.ppermute(value, axis, [(i, (i + step) % count) for i in range(count)])]
    all_to_all x0 -> x11, starting transfers between devices: none -> 49 us  [the longest x7 30.9 us: gather_all(): return lax.all_to_all(spread, axis, 0, 0)]
  transfers between devices with their start and end apart: 16 -> 64, of which waited for: 15 -> 27; matrix products, arithmetic and copies ran while one was open for 6% -> 47% of each run, Pallas kernels for 0% -> 0%
where the time goes in v1:
time: 662 us; the launch traced here: 655 us
  matrix products  209 us (32%)
  waiting for transfers between devices  186 us (28%)
  starting transfers between devices  100 us (15%)
  other arithmetic  69.7 us (11%)
  local copies, waits for them, and re-layouts  69.4 us (10%)
  between operations  20.7 us (3%)
    ppermute x36, waiting for transfers between devices, shift(): lax.ppermute(value, axis, [(i, (i + step) % count) for i in range(count)])  88.5 us
    ppermute x36, starting transfers between devices, shift(): lax.ppermute(value, axis, [(i, (i + step) % count) for i in range(count)])  48.3 us
    dot_general x23, matrix products, dot32(): return jnp.dot(left, right, preferred_element_type=jnp.float32)  44.2 us
    all_to_all x7, waiting for transfers between devices, gather_all(): return lax.all_to_all(spread, axis, 0, 0)  40.8 us
    all_to_all x1, waiting for transfers between devices, local(): lax.all_to_all(jnp.swapaxes(gains, 0, 1), CTX, 0, 0)  40.5 us
    dot_general x24, matrix products, upper_inverse(): jnp.dot(linking, inverse, precision=HIGHEST)  33.7 us
    all_to_all x7, starting transfers between devices, gather_all(): return lax.all_to_all(spread, axis, 0, 0)  30.9 us
    dot_general x24, matrix products, upper_inverse(): jnp.dot(inverse, jnp.dot(linking, inverse, precision=HIGHEST), precision=...  28.8 us
  transfers between devices with their start and end apart: 64, of which 27 were waited for; matrix products, arithmetic and copies ran while one was open for 47% of the time, Pallas kernels for 0%

profile of v1, /device:TPU:0, one launch (start us, length us, event | category | flops | bytes accessed | tf_op | source)
XLA Modules:
  0.0 654.5 jit_solution(2856627697034900928)
XLA Ops:
  66.7 4.4 all-to-all-start
  74.0 9.9 %all-to-all-done = f32[4,2,3,64,128]{4,3,2,1,0:T(8,128)} async-done(((f32[4,2,3,64,128]{4,3,2,1,0:T(8,128)}), f32[4,2,3,64,128]{4,3,2,1,0:T(8,128)}, u32[]{:S(2)}, u32[]{:S(2)}) %all-to-all-start) | async-done | bytes 786464 | tf_op jit(solution)/shard_map/all_to_all | solution.py:27
  95.9 4.6 all-to-all-start.1
  106.2 7.3 %all-to-all-done.1 = f32[4,2,3,64,128]{4,3,2,1,0:T(8,128)} async-done(((f32[4,2,3,64,128]{4,3,2,1,0:T(8,128)}), f32[4,2,3,64,128]{4,3,2,1,0:T(8,128)}, u32[]{:S(2)}, u32[]{:S(2)}) %all-to-all-start.1) | async-done | bytes 786464 | tf_op jit(solution)/shard_map/all_to_all | solution.py:27
  134.8 5.5 all-to-all-start.2
  149.8 12.1 %all-to-all-done.2 = f32[4,256,384]{1,2,0:T(8,128)} async-done(((f32[4,256,384]{1,2,0:T(8,128)}), f32[4,256,384]{1,2,0:T(8,128)}, u32[]{:S(2)}, u32[]{:S(2)}) %all-to-all-start.2) | async-done | bytes 1572896 | tf_op jit(solution)/shard_map/all_to_all | solution.py:27
  163.5 7.8 %fusion.1 = bf16[4,2,192,1536]{3,2,1,0:T(8,128)(2,1)S(1)} fusion(f32[4,1,192,1536]{3,2,1,0:T(8,128)} %bitcast.47, f32[4,1,192,1536]{3,2,1,0:T(8,128)} %bitcast.668, f32[]{:T(128)} %bitcast.42, pred[]{:T(512)S(6)} %eq.330), kind=kLoop, calls=%fused_computation.2 | loop fusion | flops 11796480 | bytes 14155781 | tf_op jit(solution)/shard_map/convert_element_type | solution.py:276
  183.9 4.4 all-to-all-start.3
  201.2 7.6 %all-to-all-done.3 = f32[4,64,1536]{2,1,0:T(8,128)} async-done(((f32[4,64,1536]{2,1,0:T(8,128)}), f32[4,64,1536]{2,1,0:T(8,128)}, u32[]{:S(2)}, u32[]{:S(2)}) %all-to-all-start.3) | async-done | bytes 1572896 | tf_op jit(solution)/shard_map/all_to_all | solution.py:314
  214.8 4.7 convolution_bitcast_fusion.7
  228.3 6.4 all-to-all-done.4
  264.8 4.4 all-to-all-start.5
  283.5 4.3 all-to-all-start.6
  290.8 5.0 all-to-all-done.6
  390.1 4.5 all-to-all-start.7
  396.9 4.4 collective-permute-done.9
  428.9 5.1 all-to-all-start.9
  434.7 40.5 %all-to-all-done.9 = f32[32,2,48]{2,1,0:T(2,128)} async-done(((f32[32,2,48]{2,1,0:T(2,128)}), f32[32,2,48]{2,1,0:T(2,128)}, u32[]{:S(2)}, u32[]{:S(2)}) %all-to-all-start.9) | async-done | bytes 12320 | tf_op jit(solution)/shard_map/all_to_all | solution.py:378
  487.4 4.4 all-to-all-start.8
  507.7 20.7 %collective-permute-done.44 = f32[4,48,1536]{2,1,0:T(8,128)S(1)} collective-permute-done((f32[4,48,1536]{2,1,0:T(8,128)S(1)}, f32[4,48,1536]{2,1,0:T(8,128)S(1)}, u32[]{:S(2)}, u32[]{:S(2)}) %collective-permute-start.44) | collective-permute-done | bytes 1179680 | tf_op jit(solution)/shard_map/ppermute | solution.py:21
  549.9 7.3 %collective-permute-done.16 = f32[4,48,640]{2,1,0:T(8,128)S(1)} collective-permute-done((f32[4,48,640]{2,1,0:T(8,128)S(1)}, f32[4,48,640]{2,1,0:T(8,128)S(1)}, u32[]{:S(2)}, u32[]{:S(2)}) %collective-permute-start.16) | collective-permute-done | bytes 491552 | tf_op jit(solution)/shard_map/ppermute | solution.py:21
  578.6 7.3 %collective-permute-done.18 = f32[48,640]{1,0:T(8,128)S(1)} collective-permute-done((f32[48,640]{1,0:T(8,128)S(1)}, f32[48,640]{1,0:T(8,128)S(1)}, u32[]{:S(2)}, u32[]{:S(2)}) %collective-permute-start.18) | collective-permute-done | bytes 122912 | tf_op jit(solution)/shard_map/ppermute | solution.py:21
  605.2 18.8 %collective-permute-done.37 = f32[4,48,1536]{2,1,0:T(8,128)} collective-permute-done((f32[4,48,1536]{2,1,0:T(8,128)}, f32[4,48,1536]{2,1,0:T(8,128)}, u32[]{:S(2)}, u32[]{:S(2)}) %collective-permute-start.37) | collective-permute-done | bytes 1179680 | tf_op jit(solution)/shard_map/ppermute | solution.py:21
  631.9 6.6 %collective-permute-done.41 = f32[48,1536]{1,0:T(8,128)} collective-permute-done((f32[48,1536]{1,0:T(8,128)S(1)}, f32[48,1536]{1,0:T(8,128)}, u32[]{:S(2)}, u32[]{:S(2)}) %collective-permute-start.41) | collective-permute-done | bytes 294944 | tf_op jit(solution)/shard_map/ppermute | solution.py:21
  (922 shorter events, 425.8 us)
Async XLA Ops:
  7.2 112.0 %all-gather.6.cloned.1.call-start = ((), (), s32[]{:S(2)}) async-start(), calls=%async_computation.13 | async-start | bytes 5898240 | tf_op jit(solution)/shard_map/all_gather | solution.py:269
  119.2 44.2 %collective-permute-start.4 = (f32[4,192,1536]{2,1,0:T(8,128)}, f32[4,192,1536]{2,1,0:T(8,128)}, u32[]{:S(2)}, u32[]{:S(2)}) collective-permute-start(f32[4,192,1536]{2,1,0:T(8,128)} %bitcast.667), channel_id=1, source_target_pairs={{0,4},{4,0},{1,5},{5,1},{2,6},{6,2},{3,7},{7,3},{8,12},{12,8},{9,1... | collective-permute-start | bytes 14155784 | tf_op jit(solution)/shard_map/ppermute | solution.py:16
  188.3 221.5 %all-reduce.2.cloned.1.call-start = ((), (), s32[]{:S(2)}) async-start(), calls=%async_computation.11 | async-start | bytes 3145728 | tf_op jit(solution)/shard_map/psum | solution.py:345
  191.8 223.3 %collective-permute-start.43 = (f32[768,1024]{1,0:T(8,128)}, f32[768,1024]{1,0:T(8,128)}, u32[]{:S(2)}, u32[]{:S(2)}) collective-permute-start(f32[768,1024]{1,0:T(8,128)} %fusion.325), channel_id=1, source_target_pairs={{0,4},{4,0},{1,5},{5,1},{2,6},{6,2},{3,7},{7,3},{8,12},{12,8},{9,1... | collective-permute-start | bytes 9437192 | tf_op jit(solution)/shard_map/ppermute | solution.py:16
  212.0 93.4 %collective-permute-start.42 = (f32[768,512]{1,0:T(8,128)}, f32[768,512]{1,0:T(8,128)}, u32[]{:S(2)}, u32[]{:S(2)}) collective-permute-start(f32[768,512]{1,0:T(8,128)} %fusion.226), channel_id=1, source_target_pairs={{0,4},{4,0},{1,5},{5,1},{2,6},{6,2},{3,7},{7,3},{8,12},{12,8},{9,1... | collective-permute-start | bytes 4718600 | tf_op jit(solution)/shard_map/ppermute | solution.py:16
  223.6 268.7 %all-gather.4.cloned.1.call-start = ((), (), s32[]{:S(2)}) async-start(), calls=%async_computation.12 | async-start | bytes 1966080 | tf_op jit(solution)/shard_map/all_gather | solution.py:362
  226.7 303.9 %collective-permute-start.35 = (f32[768,1536]{1,0:T(8,128)}, f32[768,1536]{1,0:T(8,128)}, u32[]{:S(2)}, u32[]{:S(2)}) collective-permute-start(f32[768,1536]{1,0:T(8,128)} %fusion.200), channel_id=1, source_target_pairs={{0,4},{4,0},{1,5},{5,1},{2,6},{6,2},{3,7},{7,3},{8,12},{12,8},{9,1... | collective-permute-start | bytes 14155784 | tf_op jit(solution)/shard_map/ppermute | solution.py:16
  272.2 109.8 %collective-permute-start.7 = (f32[768,384]{1,0:T(8,128)}, f32[768,384]{1,0:T(8,128)}, u32[]{:S(2)}, u32[]{:S(2)}) collective-permute-start(f32[768,384]{1,0:T(8,128)} %fusion.323), channel_id=1, source_target_pairs={{0,4},{4,0},{1,5},{5,1},{2,6},{6,2},{3,7},{7,3},{8,12},{12,8},{9,1... | collective-permute-start | bytes 3538952 | tf_op jit(solution)/shard_map/ppermute | solution.py:16
  390.1 32.6 %all-to-all-start.7 = ((f32[4,64,1536]{2,1,0:T(8,128)}), f32[4,64,1536]{2,1,0:T(8,128)}, u32[]{:S(2)}, u32[]{:S(2)}) async-start(f32[4,64,1536]{2,1,0:T(8,128)} %bitcast.78), calls=%async_computation.7 | async-start | bytes 3145728 | tf_op jit(solution)/shard_map/all_to_all | solution.py:337
  412.6 85.8 %collective-permute-start.21 = (f32[768,640]{1,0:T(8,128)}, f32[768,640]{1,0:T(8,128)}, u32[]{:S(2)}, u32[]{:S(2)}) collective-permute-start(f32[768,640]{1,0:T(8,128)} %fusion.300), channel_id=1, source_target_pairs={{0,4},{4,0},{1,5},{5,1},{2,6},{6,2},{3,7},{7,3},{8,12},{12,8},{9,1... | collective-permute-start | bytes 5898248 | tf_op jit(solution)/shard_map/ppermute | solution.py:16
  412.6 88.9 %collective-permute-start.14 = (f32[768,640]{1,0:T(8,128)}, f32[768,640]{1,0:T(8,128)}, u32[]{:S(2)}, u32[]{:S(2)}) collective-permute-start(f32[768,640]{1,0:T(8,128)} %fusion.242), channel_id=1, source_target_pairs={{0,4},{4,0},{1,5},{5,1},{2,6},{6,2},{3,7},{7,3},{8,12},{12,8},{9,1... | collective-permute-start | bytes 5898248 | tf_op jit(solution)/shard_map/ppermute | solution.py:16
  419.6 84.2 %collective-permute-start.46 = (f32[4,48,1536]{2,1,0:T(8,128)}, f32[4,48,1536]{2,1,0:T(8,128)}, u32[]{:S(2)}, u32[]{:S(2)}) collective-permute-start(f32[4,48,1536]{2,1,0:T(8,128)} %get-tuple-element.103), channel_id=1, source_target_pairs={{0,64},{32,96},{64,0},{96,32},{1,65},{33,97},{65,1},{97,33},{2,66}... | collective-permute-start | bytes 3538952 | tf_op jit(solution)/shard_map/ppermute | solution.py:21
  421.5 86.2 %collective-permute-start.45 = (f32[4,48,1536]{2,1,0:T(8,128)}, f32[4,48,1536]{2,1,0:T(8,128)}, u32[]{:S(2)}, u32[]{:S(2)}) collective-permute-start(f32[4,48,1536]{2,1,0:T(8,128)} %get-tuple-element.102), channel_id=1, source_target_pairs={{0,96},{32,0},{64,32},{96,64},{1,97},{33,1},{65,33},{97,65},{2,98}... | collective-permute-start | bytes 3538952 | tf_op jit(solution)/shard_map/ppermute | solution.py:21
  428.9 46.3 %all-to-all-start.9 = ((f32[32,2,48]{2,1,0:T(2,128)}), f32[32,2,48]{2,1,0:T(2,128)}, u32[]{:S(2)}, u32[]{:S(2)}) async-start(f32[32,2,48]{2,1,0:T(2,128)} %maximum_bitcast_fusion), calls=%async_computation.9 | async-start | bytes 65536 | tf_op jit(solution)/shard_map/all_to_all | solution.py:378
  487.4 91.1 %all-to-all-start.8 = ((f32[4,64,1536]{2,1,0:T(8,128)}), f32[4,64,1536]{2,1,0:T(8,128)}, u32[]{:S(2)}, u32[]{:S(2)}) async-start(f32[4,64,1536]{2,1,0:T(8,128)} %broadcast_in_dim.261), calls=%async_computation.8 | async-start | bytes 3145728 | tf_op jit(solution)/shard_map/all_to_all | solution.py:27
  498.6 29.9 %collective-permute-start.44 = (f32[4,48,1536]{2,1,0:T(8,128)S(1)}, f32[4,48,1536]{2,1,0:T(8,128)S(1)}, u32[]{:S(2)}, u32[]{:S(2)}) collective-permute-start(f32[4,48,1536]{2,1,0:T(8,128)S(1)} %copy-done.177), channel_id=1, source_target_pairs={{0,32},{32,64},{64,96},{96,0},{1,33},{33,65},{65,97},{97,1},{2,34}... | collective-permute-start | bytes 3538952 | tf_op jit(solution)/shard_map/ppermute | solution.py:21
  501.5 37.2 %collective-permute-start.28 = (f32[768,384]{1,0:T(8,128)S(1)}, f32[768,384]{1,0:T(8,128)S(1)}, u32[]{:S(2)}, u32[]{:S(2)}) collective-permute-start(f32[768,384]{1,0:T(8,128)S(1)} %fusion.324), channel_id=1, source_target_pairs={{0,4},{4,0},{1,5},{5,1},{2,6},{6,2},{3,7},{7,3},{8,12},{12,8},{9,1... | collective-permute-start | bytes 3538952 | tf_op jit(solution)/shard_map/ppermute | solution.py:16
  503.8 36.3 %collective-permute-start.24 = (f32[4,48,640]{2,1,0:T(8,128)S(1)}, f32[4,48,640]{2,1,0:T(8,128)S(1)}, u32[]{:S(2)}, u32[]{:S(2)}) collective-permute-start(f32[4,48,640]{2,1,0:T(8,128)S(1)} %get-tuple-element.111), channel_id=1, source_target_pairs={{0,64},{32,96},{64,0},{96,32},{1,65},{33,97},{65,1},{97,33},{2,66}... | collective-permute-start | bytes 1474568 | tf_op jit(solution)/shard_map/ppermute | solution.py:21
  507.7 33.4 %collective-permute-start.23 = (f32[4,48,640]{2,1,0:T(8,128)S(1)}, f32[4,48,640]{2,1,0:T(8,128)S(1)}, u32[]{:S(2)}, u32[]{:S(2)}) collective-permute-start(f32[4,48,640]{2,1,0:T(8,128)S(1)} %get-tuple-element.112), channel_id=1, source_target_pairs={{0,96},{32,0},{64,32},{96,64},{1,97},{33,1},{65,33},{97,65},{2,98}... | collective-permute-start | bytes 1474568 | tf_op jit(solution)/shard_map/ppermute | solution.py:21
  572.9 30.8 %collective-permute-start.38 = (f32[4,48,1536]{2,1,0:T(8,128)}, f32[4,48,1536]{2,1,0:T(8,128)}, u32[]{:S(2)}, u32[]{:S(2)}) collective-permute-start(f32[4,48,1536]{2,1,0:T(8,128)} %get-tuple-element.105), channel_id=1, source_target_pairs={{0,16},{8,24},{16,0},{24,8},{1,17},{9,25},{17,1},{25,9},{2,18},{10... | collective-permute-start | bytes 3538952 | tf_op jit(solution)/shard_map/ppermute | solution.py:21
  575.1 48.9 %collective-permute-start.37 = (f32[4,48,1536]{2,1,0:T(8,128)}, f32[4,48,1536]{2,1,0:T(8,128)}, u32[]{:S(2)}, u32[]{:S(2)}) collective-permute-start(f32[4,48,1536]{2,1,0:T(8,128)} %get-tuple-element.106), channel_id=1, source_target_pairs={{0,24},{8,0},{16,8},{24,16},{1,25},{9,1},{17,9},{25,17},{2,26},{10... | collective-permute-start | bytes 3538952 | tf_op jit(solution)/shard_map/ppermute | solution.py:21
  577.2 46.9 %collective-permute-start.36 = (f32[4,48,1536]{2,1,0:T(8,128)}, f32[4,48,1536]{2,1,0:T(8,128)}, u32[]{:S(2)}, u32[]{:S(2)}) collective-permute-start(f32[4,48,1536]{2,1,0:T(8,128)} %get-tuple-element.104), channel_id=1, source_target_pairs={{0,8},{8,16},{16,24},{24,0},{1,9},{9,17},{17,25},{25,1},{2,10},{10... | collective-permute-start | bytes 3538952 | tf_op jit(solution)/shard_map/ppermute | solution.py:21
  595.2 34.3 %collective-permute-start.34 = (f32[48,384]{1,0:T(8,128)S(1)}, f32[48,384]{1,0:T(8,128)S(1)}, u32[]{:S(2)}, u32[]{:S(2)}) collective-permute-start(f32[48,384]{1,0:T(8,128)S(1)} %get-tuple-element.148), channel_id=1, source_target_pairs={{0,16},{8,24},{16,0},{24,8},{1,17},{9,25},{17,1},{25,9},{2,18},{10... | collective-permute-start | bytes 221192 | tf_op jit(solution)/shard_map/ppermute | solution.py:21
  597.2 34.0 %collective-permute-start.33 = (f32[48,384]{1,0:T(8,128)S(1)}, f32[48,384]{1,0:T(8,128)S(1)}, u32[]{:S(2)}, u32[]{:S(2)}) collective-permute-start(f32[48,384]{1,0:T(8,128)S(1)} %get-tuple-element.149), channel_id=1, source_target_pairs={{0,24},{8,0},{16,8},{24,16},{1,25},{9,1},{17,9},{25,17},{2,26},{10... | collective-permute-start | bytes 221192 | tf_op jit(solution)/shard_map/ppermute | solution.py:21
  (307 other events, 1677.5 us)
Sparse Core Ops, SparseCore 0:
  10.3 55.3 all-gather.5
  210.5 50.2 all-reduce.1
  262.5 26.6 all-gather.3

commit v2 on v0

v2 whole, which is shorter than its diff:
```python
import jax
import jax.numpy as jnp
from jax import lax
from jax.experimental import pallas as pl
from jax.experimental.pallas import tpu as pltpu
from jax.sharding import Mesh
from jax.sharding import PartitionSpec as P

EPSILON = 1e-06
HEAD_EPSILON = 0.01
F32 = jnp.float32
BF16 = jnp.bfloat16
HEADS = 3
HW = 128
LEN = 256
RANKS = 4
PART = LEN // RANKS
SIDE = 4
CTX = ("y", "x", "c")
VMEM_LIMIT = 56 * 1024 * 1024


def split(value):
    high = value.astype(BF16)
    return high, (value - high.astype(F32)).astype(BF16)


def dg(left, right, ta, tb):
    dims = (((0 if ta else 1,), (1 if tb else 0,)), ((), ()))
    return lax.dot_general(left, right, dims, preferred_element_type=F32)


def mm(left, right, ta=False, tb=False):
    left = left if isinstance(left, tuple) else split(left)
    right = right if isinstance(right, tuple) else split(right)
    return dg(left[0], right[0], ta, tb) + (
        dg(left[0], right[1], ta, tb) + dg(left[1], right[0], ta, tb)
    )


def iota(shape, dim):
    return lax.broadcasted_iota(jnp.int32, shape, dim)


def cols(head):
    return slice(head * HW, (head + 1) * HW)


def segments(spot, scal):
    second = scal[1]
    third = second + scal[2]
    return (spot >= second).astype(jnp.int32) + (spot >= third).astype(jnp.int32)


def small_inverses(scaled):
    row = iota((HW, HW), 0)
    lane = iota((HW, HW), 1)
    same = (row // 8) == (lane // 8)
    packed = []
    for one in scaled:
        for half in range(2):
            block = jnp.where(same, one[half * HW : (half + 1) * HW, half * HW : (half + 1) * HW], 0.0)
            packed.append(jnp.sum(block.reshape(HW // 8, 8, HW), axis=0))
    count = len(packed)
    high, low = split(jnp.concatenate(packed, axis=0))
    lane_8 = iota((8, HW), 1) % 8
    spread = {}
    for k in range(1, 8):
        unit = ((row // 8 == lane // 8) & (row % 8 == k)).astype(BF16)
        both = dg(high, unit, False, False) + dg(low, unit, False, False)
        spread[k] = both.reshape(count, 8, HW)
    rows = {}
    for i in range(7, -1, -1):
        value = jnp.broadcast_to((lane_8[:1] == i).astype(F32)[None], (count, 1, HW))
        for k in range(i + 1, 8):
            value = value - spread[k][:, i : i + 1, :] * rows[k]
        rows[i] = value
    done = jnp.concatenate([rows[i] for i in range(8)], axis=1)
    out = []
    zero = jnp.zeros((HW, HW), F32)
    for head in range(count // 2):
        halves = [
            jnp.where(same, jnp.concatenate([done[2 * head + half]] * (HW // 8), axis=0), 0.0)
            for half in range(2)
        ]
        out.append(
            jnp.concatenate(
                [
                    jnp.concatenate([halves[0], zero], axis=1),
                    jnp.concatenate([zero, halves[1]], axis=1),
                ],
                axis=0,
            )
        )
    return out


def upper_rows(value, width):
    return jnp.concatenate(
        [value[at : at + width] for at in range(0, value.shape[0], 2 * width)], axis=0
    )


def put_upper(value, upper, width):
    pieces = []
    for n, at in enumerate(range(0, value.shape[0], 2 * width)):
        pieces.append(upper[n * width : (n + 1) * width])
        pieces.append(value[at + width : at + 2 * width])
    return jnp.concatenate(pieces, axis=0)


def inverses(scaled):
    out = small_inverses(scaled)
    row = iota((LEN, LEN), 0)
    lane = iota((LEN, LEN), 1)
    width = 8
    while width < LEN:
        pair = (row // (2 * width) == lane // (2 * width)) & (row // width < lane // width)
        link = [upper_rows(jnp.where(pair, one, 0.0), width) for one in scaled]
        parts = [split(one) for one in out]
        first = [mm(a, b) for a, b in zip(link, parts)]
        empty = jnp.zeros((LEN, LEN), F32)
        wide = [put_upper(empty, one, width) for one in first]
        tops = [
            (upper_rows(a, width), upper_rows(b, width)) for a, b in parts
        ]
        second = [mm(a, b) for a, b in zip(tops, wide)]
        out = [
            put_upper(one, upper_rows(one, width) - new, width) for one, new in zip(out, second)
        ]
        width *= 2
    return out


def unit_rows(value):
    scale = lax.rsqrt(jnp.sum(value * value, axis=-1, keepdims=True) + EPSILON)
    return value * scale, scale


def a1_body(
    scal_ref, x_ref, gain_ref, wq_ref, wk_ref, wv_ref, ww_ref, wb_ref,
    h1_ref, q_ref, k_ref, v_ref, w_ref, aux_ref, inv_ref, kp_ref, b_ref, kt_ref, tu_ref,
):
    x = x_ref[...]
    scale = lax.rsqrt(jnp.mean(x * x, axis=-1, keepdims=True) + EPSILON)
    h1 = (x * scale * gain_ref[...].astype(F32)).astype(BF16)
    h1_ref[...] = h1.astype(F32)
    start = scal_ref[0]
    token = iota((LEN, 1), 0) + start
    segment = segments(token, scal_ref)
    end_segment = segments(jnp.full((1, 1), LEN - 1, jnp.int32) + start, scal_ref)
    before = start - 1
    before_segment = jnp.where(start == 0, -1, segments(jnp.full((1, 1), 0, jnp.int32) + before, scal_ref))
    last = (segment == end_segment).astype(F32)
    carry_all = (end_segment == before_segment).astype(F32)
    row = iota((LEN, LEN), 0)
    lane = iota((LEN, LEN), 1)
    later = row < lane
    bl = dg(h1, wb_ref[...], False, False)
    sig = jax.nn.sigmoid(bl)
    beta = 1.0 + sig
    beta_rows = beta.T
    pr = dg(h1, ww_ref[...], False, False)
    kr = dg(h1, wk_ref[...], False, False)
    w_all, k_all, aux = [], [], []
    for head in range(HEADS):
        w, w_scale = unit_rows(pr[:, cols(head)])
        k, k_scale = unit_rows(kr[:, cols(head)])
        w_ref[:, cols(head)] = w
        k_ref[:, cols(head)] = k
        w_all.append(w)
        k_all.append(k)
        aux.append((w_scale, k_scale))
    w_split = [split(w) for w in w_all]
    k_split = [split(k) for k in k_all]
    scaled = [
        jnp.where(later, mm(w_split[h], w_split[h], tb=True), 0.0) * beta[:, h : h + 1]
        for h in range(HEADS)
    ]
    inverse = [
        one * beta_rows[h : h + 1, :] for h, one in enumerate(inverses(scaled))
    ]
    vr = dg(h1, wv_ref[...], False, False)
    qr = dg(h1, wq_ref[...], False, False)
    v_ref[...] = vr
    lane_aux = iota((LEN, HW), 1)
    packed = jnp.where(lane_aux < HEADS, beta, 0.0)
    eye = (iota((HW, HW), 0) == iota((HW, HW), 1)).astype(F32)
    for head in range(HEADS):
        q, q_scale = unit_rows(qr[:, cols(head)])
        q_ref[:, cols(head)] = q
        for at, value in ((8 + head, q_scale), (16 + head, aux[head][1]), (24 + head, aux[head][0])):
            packed = jnp.where(lane_aux == at, value, packed)
        inv_ref[head] = inverse[head]
        inv_split = split(inverse[head])
        folded = mm(inv_split, w_split[head])
        b_ref[:, cols(head)] = folded
        folded_split = split(folded)
        kp = jnp.where(later, mm(k_split[head], w_split[head], tb=True), 0.0)
        kp_ref[head] = kp
        kt = k_all[head] - mm(kp, folded_split)
        kt_ref[:, cols(head)] = kt
        tu_ref[0, head] = carry_all * (eye - mm(w_split[head], folded_split, ta=True))
        tu_ref[1, head] = mm(vr[:, cols(head)], kt * last, ta=True)
    aux_ref[...] = packed


def shape(*dims, dtype=F32):
    return jax.ShapeDtypeStruct(dims, dtype)


def call(body, outs, name, flops, moved, scratch=()):
    smem = pl.BlockSpec(memory_space=pltpu.SMEM)
    vmem = pl.BlockSpec(memory_space=pltpu.VMEM)

    def run(*operands):
        return pl.pallas_call(
            body,
            out_shape=outs,
            in_specs=[smem] + [vmem] * (len(operands) - 1),
            out_specs=[vmem] * len(outs),
            scratch_shapes=list(scratch),
            name=name,
            cost_estimate=pl.CostEstimate(flops=flops, bytes_accessed=moved, transcendentals=0),
            compiler_params=pltpu.CompilerParams(vmem_limit_bytes=VMEM_LIMIT),
        )(*operands)

    return run


WIDE = HEADS * HW


def run_a1(*operands):
    outs = [
        shape(LEN, operands[1].shape[1]),
        shape(LEN, WIDE), shape(LEN, WIDE), shape(LEN, WIDE), shape(LEN, WIDE),
        shape(LEN, HW),
        shape(HEADS, LEN, LEN), shape(HEADS, LEN, LEN),
        shape(LEN, WIDE), shape(LEN, WIDE),
        shape(2, HEADS, HW, HW),
    ]
    return call(a1_body, outs, "local_parts", 8 * 10**9, 12 * 10**6)(*operands)


def a2_body(
    scal_ref, q_ref, k_ref, v_ref, w_ref, inv_ref, kp_ref,
    c_ref, sc_ref, qt_ref, in_ref,
):
    start = scal_ref[0]
    segment = segments(iota((LEN, LEN), 0) + start, scal_ref)
    segment_t = segments(iota((LEN, LEN), 1) + start, scal_ref)
    row = iota((LEN, LEN), 0)
    lane = iota((LEN, LEN), 1)
    up_to = row <= lane
    seen = up_to & (segment == segment_t)
    for head in range(HEADS):
        q = q_ref[:, cols(head)]
        q_split = split(q)
        w_split = split(w_ref[:, cols(head)])
        pq = jnp.where(up_to, mm(w_split, q_split, tb=True), 0.0)
        c = mm(inv_ref[head], pq)
        c_ref[head] = c
        c_split = split(c)
        qt_ref[:, cols(head)] = q - mm(c_split, w_split, ta=True)
        scores = mm(k_ref[:, cols(head)], q_split, tb=True) - mm(kp_ref[head], c_split)
        scores = jnp.where(seen, scores, 0.0)
        sc_ref[head] = scores
        in_ref[:, cols(head)] = mm(scores, v_ref[:, cols(head)], ta=True)


def run_a2(*operands):
    outs = [shape(HEADS, LEN, LEN), shape(HEADS, LEN, LEN), shape(LEN, WIDE), shape(LEN, WIDE)]
    return call(a2_body, outs, "inside_parts", 4 * 10**9, 6 * 10**6)(*operands)


def carry_of(start, scal_ref):
    token = iota((LEN, 1), 0) + start
    before = jnp.full((1, 1), 0, jnp.int32) + (start - 1)
    before_segment = jnp.where(start == 0, -1, segments(before, scal_ref))
    return (segments(token, scal_ref) == before_segment).astype(F32)


def pair_of(ref, core, head):
    return jnp.concatenate([ref[0, core, head], ref[1, core, head]], axis=0)


def a3_body(scal_ref, in_ref, qt_ref, states_ref, mixed_ref, normed_ref, spread_ref, carried_ref):
    carry = carry_of(scal_ref[0], scal_ref)
    core = scal_ref[5]
    for head in range(HEADS):
        carried = pair_of(states_ref, core, head)
        carried_ref[head] = carried
        mixed = in_ref[:, cols(head)] + carry * mm(qt_ref[:, cols(head)], carried, tb=True)
        mixed_ref[:, cols(head)] = mixed
        scale = lax.rsqrt(jnp.mean(mixed * mixed, axis=-1, keepdims=True) + HEAD_EPSILON)
        low = (mixed * scale).astype(BF16).astype(F32)
        normed_ref[:, cols(head)] = low
        for at in range(RANKS):
            spread_ref[at, :, cols(head)] = low


def run_a3(*operands):
    outs = [shape(LEN, WIDE), shape(LEN, WIDE), shape(RANKS, LEN, WIDE), shape(HEADS, HW, HW)]
    return call(a3_body, outs, "normed_heads", 10**8, 2 * 10**6)(*operands)


def b1_body(scal_ref, dn_ref, mixed_ref, qt_ref, dm_ref, sg_ref):
    carry = carry_of(scal_ref[0], scal_ref)
    for head in range(HEADS):
        mixed = mixed_ref[:, cols(head)]
        dn = dn_ref[:, cols(head)]
        scale = lax.rsqrt(jnp.mean(mixed * mixed, axis=-1, keepdims=True) + HEAD_EPSILON)
        drift = jnp.mean(dn * mixed, axis=-1, keepdims=True) * (scale * scale)
        dm = scale * (dn - mixed * drift)
        dm_ref[:, cols(head)] = dm
        sg_ref[head] = mm(dm * carry, qt_ref[:, cols(head)], ta=True)


def run_b1(*operands):
    outs = [shape(LEN, WIDE), shape(HEADS, HW, HW)]
    return call(b1_body, outs, "state_gradient", 10**8, 2 * 10**6)(*operands)


def unit_pull(unit, scale, grad):
    return scale * (grad - unit * jnp.sum(unit * grad, axis=-1, keepdims=True))


def b2_body(
    scal_ref, dm_ref, carried_ref, q_ref, k_ref, v_ref, w_ref, aux_ref, inv_ref, kp_ref,
    c_ref, sc_ref,
    dq_ref, dk_ref, dv_ref, dw_ref, dkp_ref, xc_ref,
):
    start = scal_ref[0]
    carry = carry_of(start, scal_ref)
    row = iota((LEN, LEN), 0)
    lane = iota((LEN, LEN), 1)
    up_to = row <= lane
    seen = up_to & (
        segments(row + start, scal_ref) == segments(lane + start, scal_ref)
    )
    for head in range(HEADS):
        q = q_ref[:, cols(head)]
        q_split = split(q)
        w_split = split(w_ref[:, cols(head)])
        k_split = split(k_ref[:, cols(head)])
        c_split = split(c_ref[head])
        kp_split = split(kp_ref[head])
        dm = dm_ref[:, cols(head)]
        dm_split = split(dm)
        dqt = mm(dm * carry, carried_ref[head])
        dqt_split = split(dqt)
        ds = jnp.where(seen, mm(v_ref[:, cols(head)], dm_split, tb=True), 0.0)
        ds_split = split(ds)
        dv_ref[:, cols(head)] = mm(sc_ref[head], dm_split)
        dk = mm(ds_split, q_split)
        dq = dqt + mm(ds_split, k_split, ta=True)
        dkp_ref[head] = mm(ds_split, c_split, tb=True)
        dc = mm(kp_split, ds_split, ta=True) + mm(w_split, dqt_split, tb=True)
        dw = mm(c_split, dqt_split)
        x = mm(inv_ref[head], dc, ta=True)
        xc_ref[head] = mm(x, c_split, tb=True)
        dpq_split = split(jnp.where(up_to, x, 0.0))
        dw_ref[:, cols(head)] = dw + mm(dpq_split, q_split)
        dq = dq - mm(dpq_split, w_split, ta=True)
        dk_ref[:, cols(head)] = dk
        scale = aux_ref[:, 8 + head : 9 + head]
        dq_ref[:, cols(head)] = unit_pull(q, scale, dq).astype(BF16).astype(F32)


def run_b2(*operands):
    outs = [
        shape(LEN, WIDE), shape(LEN, WIDE), shape(LEN, WIDE), shape(LEN, WIDE),
        shape(HEADS, LEN, LEN), shape(HEADS, LEN, LEN),
    ]
    return call(b2_body, outs, "inside_gradients", 8 * 10**9, 8 * 10**6)(*operands)


def b3_body(
    scal_ref, x_ref, gain_mid_ref, states_ref, carried_ref, k_ref, v_ref, w_ref, aux_ref,
    inv_ref, kp_ref, b_ref, kt_ref, dq_ref, dk_ref, dv_ref, dw_ref, dkp_ref, xc_ref,
    wq_ref, wk_ref, wv_ref, ww_ref, wb_ref,
    low_ref, dh_ref,
):
    start = scal_ref[0]
    core = scal_ref[5]
    segment = segments(iota((LEN, 1), 0) + start, scal_ref)
    end_segment = segments(jnp.full((1, 1), LEN - 1, jnp.int32) + start, scal_ref)
    before = jnp.full((1, 1), 0, jnp.int32) + (start - 1)
    before_segment = jnp.where(start == 0, -1, segments(before, scal_ref))
    last = (segment == end_segment).astype(F32)
    carry_all = (end_segment == before_segment).astype(F32)
    row = iota((LEN, LEN), 0)
    lane = iota((LEN, LEN), 1)
    later_mask = row < lane
    lane_aux = iota((LEN, HW), 1)
    d_beta = jnp.zeros((LEN, HW), F32)
    for head in range(HEADS):
        later = pair_of(states_ref, core, head)
        later_split = split(later)
        dt_split = split(carry_all * mm(carried_ref[head], later_split, ta=True))
        w = w_ref[:, cols(head)]
        w_split = split(w)
        k = k_ref[:, cols(head)]
        v = v_ref[:, cols(head)]
        b_split = split(b_ref[:, cols(head)])
        kp_split = split(kp_ref[head])
        dv = dv_ref[:, cols(head)] + last * mm(kt_ref[:, cols(head)], later_split, tb=True)
        dkt = last * mm(v, later_split)
        dkt_split = split(dkt)
        db = mm(w_split, dt_split) + mm(kp_split, dkt_split, ta=True)
        y = mm(inv_ref[head], db, ta=True)
        y_split = split(y)
        dw = dw_ref[:, cols(head)] + mm(b_split, dt_split, tb=True) + y
        dkp = jnp.where(later_mask, dkp_ref[head] + mm(dkt_split, b_split, tb=True), 0.0)
        dkp_split = split(dkp)
        dk = dk_ref[:, cols(head)] + dkt - mm(dkp_split, w_split)
        dw = dw + mm(dkp_split, split(k), ta=True)
        dm = xc_ref[head] + mm(y_split, b_split, tb=True)
        dn_split = split(jnp.where(later_mask, dm, 0.0))
        dw = mm(dn_split, w_split) + mm(dn_split, w_split, ta=True) - dw
        diagonal = jnp.sum(jnp.where(row == lane, dm, 0.0), axis=-1, keepdims=True)
        beta = aux_ref[:, head : head + 1]
        sig = beta - 1.0
        dbl = -diagonal / (beta * beta) * sig * (1.0 - sig)
        d_beta = jnp.where(lane_aux == head, dbl, d_beta)
        low_ref[:, cols(head)] = unit_pull(k, aux_ref[:, 16 + head : 17 + head], dk).astype(BF16).astype(F32)
        low_ref[:, WIDE + head * HW : WIDE + (head + 1) * HW] = dv.astype(BF16).astype(F32)
        low_ref[:, 2 * WIDE + head * HW : 2 * WIDE + (head + 1) * HW] = unit_pull(
            w, aux_ref[:, 24 + head : 25 + head], dw
        ).astype(BF16).astype(F32)
    low_ref[:, 3 * WIDE :] = d_beta.astype(BF16).astype(F32)
    total = dg(dq_ref[...].astype(BF16), wq_ref[...], False, True)
    for at, ref in enumerate((wk_ref, wv_ref, ww_ref, wb_ref)):
        low = low_ref[:, at * WIDE : at * WIDE + ref.shape[1]].astype(BF16)
        total = total + dg(low, ref[...], False, True)
    for at in range(RANKS):
        dh_ref[at, :PART, :] = total[at * PART : (at + 1) * PART]
    x = x_ref[...]
    scale = lax.rsqrt(jnp.mean(x * x, axis=-1, keepdims=True) + EPSILON)
    gain_in = jnp.sum(total * x * scale, axis=0, keepdims=True)
    rows = iota((8, x.shape[1]), 0)
    both = jnp.where(rows == 0, gain_in, jnp.where(rows == 1, gain_mid_ref[...], 0.0))
    for at in range(RANKS):
        dh_ref[at, PART:, :] = both


def run_b3(*operands):
    outs = [shape(LEN, 3 * WIDE + HW), shape(RANKS, PART + 8, operands[1].shape[1])]
    return call(b3_body, outs, "late_gradients", 9 * 10**9, 16 * 10**6)(*operands)


def half_of(core):
    return pl.ds(pl.multiple_of(core * (HW // 2), HW // 2), HW // 2)


def s1_body(scal_ref, both_ref, u_ref, out_ref):
    rows = half_of(scal_ref[5])
    for head in range(HEADS):
        t_1 = split(both_ref[1, 0, head])
        u_0 = both_ref[0, 1, head, rows, :]
        u_1 = both_ref[1, 1, head, rows, :]
        u_ref[0, head] = u_0
        u_ref[1, head] = u_1
        chip_t = mm(both_ref[0, 0, head, rows, :], t_1)
        chip_u = mm(u_0, t_1) + u_1
        for at in range(SIDE):
            out_ref[at, 0, head] = chip_t
            out_ref[at, 1, head] = chip_u


def run_s1(*operands):
    outs = [shape(2, HEADS, HW // 2, HW), shape(SIDE, 2, HEADS, HW // 2, HW)]
    return call(s1_body, outs, "chip_state", 10**8, 2 * 10**6)(*operands)


def s2_body(scal_ref, pair_ref, t_ref, u_ref, out_ref):
    core = scal_ref[5]
    rows = half_of(core)
    for head in range(HEADS):
        for at in range(SIDE):
            t_ref[at, head] = jnp.concatenate(
                [pair_ref[0, at, 0, head], pair_ref[1, at, 0, head]], axis=0
            )
            u_ref[at, head] = pair_ref[core, at, 1, head]
    for head in range(HEADS):
        t_1 = split(t_ref[1, head])
        t_3 = split(t_ref[3, head])
        t_23 = split(mm(t_ref[2, head], t_3))
        row_t = mm(mm(t_ref[0, head, rows, :], t_1), t_23)
        row_u = mm(mm(u_ref[0, head], t_1) + u_ref[1, head], t_23)
        row_u = row_u + mm(u_ref[2, head], t_3) + u_ref[3, head]
        for at in range(SIDE):
            out_ref[at, 0, head] = row_t
            out_ref[at, 1, head] = row_u


def run_s2(*operands):
    outs = [
        shape(SIDE, HEADS, HW, HW),
        shape(SIDE, HEADS, HW // 2, HW),
        shape(SIDE, 2, HEADS, HW // 2, HW),
    ]
    return call(s2_body, outs, "row_state", 10**8, 2 * 10**6)(*operands)


def s3_body(scal_ref, pair_ref, tx_ref, ux_ref, both_ref, uc_ref, ty_ref, out_ref):
    row, col, core = scal_ref[3], scal_ref[4], scal_ref[5]
    for head in range(HEADS):
        for at in range(SIDE):
            ty_ref[at, head] = jnp.concatenate(
                [pair_ref[0, at, 0, head], pair_ref[1, at, 0, head]], axis=0
            )
    for head in range(HEADS):
        state = jnp.where(row > 0, pair_ref[core, 0, 1, head], 0.0)
        for at in range(1, SIDE - 1):
            new = mm(state, ty_ref[at, head]) + pair_ref[core, at, 1, head]
            state = jnp.where(at < row, new, state)
        for at in range(SIDE - 1):
            new = mm(state, tx_ref[at, head]) + ux_ref[at, head]
            state = jnp.where(at < col, new, state)
        out_ref[0, head] = state
        out_ref[1, head] = mm(state, both_ref[0, 0, head]) + uc_ref[0, head]


def run_s3(*operands):
    outs = [shape(SIDE, HEADS, HW, HW), shape(2, HEADS, HW // 2, HW)]
    return call(s3_body, outs, "block_state", 10**8, 2 * 10**6)(*operands)


def t1_body(scal_ref, pair_ref, both_ref, g_ref, out_ref):
    rows = half_of(scal_ref[5])
    for head in range(HEADS):
        g_1 = pair_ref[1, head, rows, :]
        g_ref[head] = g_1
        chip = mm(g_1, both_ref[0, 0, head], tb=True) + pair_ref[0, head, rows, :]
        for at in range(SIDE):
            out_ref[at, head] = chip


def run_t1(*operands):
    outs = [shape(HEADS, HW // 2, HW), shape(SIDE, HEADS, HW // 2, HW)]
    return call(t1_body, outs, "chip_gradient", 10**8, 10**6)(*operands)


def t2_body(scal_ref, g_ref, t_ref, out_ref):
    for head in range(HEADS):
        total = g_ref[3, head]
        for at in (2, 1, 0):
            total = mm(total, t_ref[at, head], tb=True) + g_ref[at, head]
        for at in range(SIDE):
            out_ref[at, head] = total


def run_t2(*operands):
    outs = [shape(SIDE, HEADS, HW // 2, HW)]
    return call(t2_body, outs, "row_gradient", 10**8, 10**6)(*operands)[0]


def t3_body(scal_ref, gy_ref, gx_ref, ty_ref, tx_ref, both_ref, g_ref, out_ref):
    row, col = scal_ref[3], scal_ref[4]
    for head in range(HEADS):
        later = jnp.where(row < SIDE - 1, gy_ref[3, head], 0.0)
        for at in (2, 1):
            new = mm(later, ty_ref[at, head], tb=True) + gy_ref[at, head]
            later = jnp.where(at > row, new, later)
        for at in (3, 2, 1):
            new = mm(later, tx_ref[at, head], tb=True) + gx_ref[at, head]
            later = jnp.where(at > col, new, later)
        out_ref[1, head] = later
        out_ref[0, head] = mm(later, both_ref[1, 0, head], tb=True) + g_ref[head]


def run_t3(*operands):
    outs = [shape(2, HEADS, HW // 2, HW)]
    return call(t3_body, outs, "block_gradient", 10**8, 2 * 10**6)(*operands)[0]


def ffn_body(
    scal_ref, normed_ref, out_mine_ref, out_other_ref, x_ref, gain_ref, grad_ref,
    gate_ref, up_ref, down_ref,
    middle_ref, sent_ref, dh_ref, down_part_ref, h_ref, d_ref,
):
    step = pl.program_id(0)
    units = gate_ref.shape[1]
    hidden_all = units * pl.num_programs(0)

    @pl.when(step == 0)
    def _():
        core = scal_ref[5]
        half = x_ref.shape[1] // 2
        for ref, at in ((out_mine_ref, core), (out_other_ref, 1 - core)):
            spot = pl.ds(pl.multiple_of(at * half, half), half)
            total = x_ref[:, spot]
            for rank in range(RANKS):
                total = total + dg(normed_ref[rank].astype(BF16), ref[rank], False, False)
            middle_ref[:, spot] = total
        middle = middle_ref[...]
        scale = lax.rsqrt(jnp.mean(middle * middle, axis=-1, keepdims=True) + EPSILON)
        h2 = (middle * scale * gain_ref[...].astype(F32)).astype(BF16)
        h_ref[...] = h2
        sent_ref[:, 3 * hidden_all :] = h2.astype(F32)
        d_ref[...] = grad_ref[...].astype(BF16)

    h2 = h_ref[...]
    gate = dg(h2, gate_ref[...], False, False)
    up = dg(h2, up_ref[...], False, False)
    sig = jax.nn.sigmoid(gate)
    silu = gate * sig
    hidden = (silu * up).astype(BF16)
    d_hidden = dg(d_ref[...], down_ref[...], False, True)
    d_gate = (d_hidden * up * sig * (1.0 + gate * (1.0 - sig))).astype(BF16)
    d_up = (d_hidden * silu).astype(BF16)
    for n, value in enumerate((d_gate, d_up, hidden)):
        spot = pl.ds(pl.multiple_of(n * hidden_all + step * units, units), units)
        sent_ref[:, spot] = value.astype(F32)
    d_h = dg(d_gate, gate_ref[...], False, True) + dg(d_up, up_ref[...], False, True)
    down = dg(hidden, down_ref[...], False, False)

    @pl.when(step == 0)
    def _():
        dh_ref[...] = d_h
        down_part_ref[...] = down

    @pl.when(step > 0)
    def _():
        dh_ref[...] += d_h
        down_part_ref[...] += down


def run_ffn(scal, normed, out_mine, out_other, x, gain, grad, w_gate, w_up, w_down):
    tokens, width = x.shape
    hidden = w_gate.shape[1]
    steps = 4
    units = hidden // steps

    def whole(array):
        dims = array.shape
        return pl.BlockSpec(dims, lambda i: (0,) * len(dims))

    outs = [
        shape(tokens, width),
        shape(tokens, 3 * hidden + width),
        shape(tokens, width),
        shape(tokens, width),
    ]
    across = pl.BlockSpec((width, units), lambda i: (0, i))
    return pl.pallas_call(
        ffn_body,
        grid=(steps,),
        out_shape=outs,
        in_specs=[pl.BlockSpec(memory_space=pltpu.SMEM)]
        + [whole(a) for a in (normed, out_mine, out_other, x, gain, grad)]
        + [across, across, pl.BlockSpec((units, width), lambda i: (i, 0))],
        out_specs=[whole(a) for a in outs],
        scratch_shapes=[pltpu.VMEM((tokens, width), BF16)] * 2,
        name="feed_forward",
        cost_estimate=pl.CostEstimate(
            flops=6 * 10**9, bytes_accessed=36 * 10**6, transcendentals=tokens * hidden
        ),
        compiler_params=pltpu.CompilerParams(
            vmem_limit_bytes=VMEM_LIMIT, dimension_semantics=("arbitrary",)
        ),
    )(scal, normed, out_mine, out_other, x, gain, grad, w_gate, w_up, w_down)


def norm_pull(grad, values, gain):
    scale = lax.rsqrt(jnp.mean(values * values, axis=-1, keepdims=True) + EPSILON)
    turned = gain * grad
    drift = jnp.mean(turned * values, axis=-1, keepdims=True) * (scale * scale * scale)
    return scale * turned - values * drift, grad * values * scale


def k5_body(
    scal_ref, second_ref, middle_ref, grad_ref, gain_ref, out_mine_ref, out_other_ref,
    d_middle_ref, attn_ref, gain_out_ref, normed_ref,
):
    core = scal_ref[5]
    rows = pl.ds(pl.multiple_of(scal_ref[6] * PART, PART), PART)
    second = second_ref[0] + second_ref[1] + second_ref[2] + second_ref[3]
    pulled, summed = norm_pull(second, middle_ref[rows, :], gain_ref[...].astype(F32))
    d_middle = grad_ref[rows, :] + pulled
    d_middle_ref[...] = d_middle
    gain_out_ref[...] = jnp.sum(summed, axis=0, keepdims=True)
    attn_ref[...] = d_middle.astype(BF16).astype(F32)
    half = d_middle.shape[1] // 2
    mine = attn_ref[:, pl.ds(pl.multiple_of(core * half, half), half)].astype(BF16)
    other = attn_ref[:, pl.ds(pl.multiple_of((1 - core) * half, half), half)].astype(BF16)
    for rank in range(RANKS):
        normed_ref[rank] = dg(mine, out_mine_ref[rank], False, True) + dg(
            other, out_other_ref[rank], False, True
        )


def run_k5(*operands):
    width = operands[2].shape[1]
    outs = [shape(PART, width), shape(PART, width), shape(1, width), shape(RANKS, PART, WIDE)]
    return call(k5_body, outs, "middle_gradient", 10**9, 8 * 10**6)(*operands)


def n_body(scal_ref, first_ref, x_ref, gain_ref, d_middle_ref, out_ref, gains_ref):
    rows = pl.ds(pl.multiple_of(scal_ref[6] * PART, PART), PART)
    total = first_ref[0] + first_ref[1] + first_ref[2] + first_ref[3]
    pulled, _ = norm_pull(total[:PART], x_ref[rows, :], gain_ref[...].astype(F32))
    done = d_middle_ref[...] + pulled
    for at in range(RANKS):
        out_ref[at] = done
    gains_ref[...] = total[PART:]


def run_n(*operands):
    width = operands[2].shape[1]
    outs = [shape(RANKS, PART, width), shape(8, width)]
    return call(n_body, outs, "input_gradient", 10**7, 5 * 10**6)(*operands)


def turn(ref, turned_ref, spot):
    width = ref.shape[1]
    for at in range(0, width, 256):
        turned_ref[at : at + 256, spot] = ref[:, at : at + 256].T.astype(BF16)


def parts_of(turned_ref, scal_ref, along_x, step):
    row, col, core = scal_ref[3], scal_ref[4], scal_ref[5]
    rows = turned_ref.shape[0] // (2 * SIDE * SIDE)
    pieces = []
    for at in range(SIDE):
        if along_x:
            place = (at * SIDE + lax.rem(col + step, SIDE)) * 2 + core
        else:
            place = (lax.rem(row + step, SIDE) * SIDE + at) * 2 + core
        pieces.append(turned_ref[pl.ds(pl.multiple_of(place * rows, rows), rows), :])
    return jnp.concatenate(pieces, axis=0)


def put(ref, value, start):
    rows = value.shape[0] // SIDE
    for at in range(SIDE):
        ref[at, :, start : start + value.shape[1]] = value[at * rows : (at + 1) * rows]


def w1_body(scal_ref, mine_ref, other_ref, grad_ref, grad_other_ref, *rest):
    outs, (cols_ref, h_ref, d_ref) = rest[:8], rest[8:]
    tokens = mine_ref.shape[0]
    wide = cols_ref.shape[1]
    cut = wide // 2
    up_end = 2 * (wide // 3)
    for n, (ref, grad) in enumerate(((mine_ref, grad_ref), (other_ref, grad_other_ref))):
        spot = slice(n * tokens, (n + 1) * tokens)
        cols_ref[spot, :] = ref[:, :wide].astype(BF16)
        turn(ref.at[:, wide:], h_ref, spot)
        turn(grad, d_ref, spot)
    for step in range(SIDE):
        put(outs[step], dg(parts_of(h_ref, scal_ref, True, step), cols_ref[:, :cut], False, False), 0)
    for step in range(SIDE):
        out = outs[SIDE + step]
        rows = parts_of(h_ref, scal_ref, False, step)
        put(out, dg(rows, cols_ref[:, cut:up_end], False, False), 0)
        rows = parts_of(d_ref, scal_ref, False, step)
        put(out, dg(rows, cols_ref[:, up_end:], False, False), up_end - cut)


def run_w1(scal, mine, other, grad, grad_other):
    tokens, width = grad.shape
    wide = mine.shape[1] - width
    outs = [shape(SIDE, width // 32, wide // 2)] * 8
    scratch = [
        pltpu.VMEM((2 * tokens, wide), BF16),
        pltpu.VMEM((width, 2 * tokens), BF16),
        pltpu.VMEM((width, 2 * tokens), BF16),
    ]
    return call(w1_body, outs, "ffn_weight_sums", 3 * 10**9, 24 * 10**6, scratch)(
        scal, mine, other, grad, grad_other
    )


def w2_body(
    scal_ref, low_ref, low_other_ref, dq_ref, dq_other_ref, n_ref, n_other_ref,
    h1_ref, h1_other_ref, attn_ref, attn_other_ref, *rest,
):
    outs, (cols_ref, h_ref, d_ref) = rest[:8], rest[8:]
    tokens = low_ref.shape[0]
    late = low_ref.shape[1]
    cut = cols_ref.shape[1] // 2
    query_end = late + WIDE
    sides = (
        (low_ref, dq_ref, n_ref, h1_ref, attn_ref),
        (low_other_ref, dq_other_ref, n_other_ref, h1_other_ref, attn_other_ref),
    )
    for n, (low, dq, normed, h1, attn) in enumerate(sides):
        spot = slice(n * tokens, (n + 1) * tokens)
        cols_ref[spot, :late] = low[...].astype(BF16)
        cols_ref[spot, late:query_end] = dq[...].astype(BF16)
        cols_ref[spot, query_end:] = normed[...].astype(BF16)
        turn(h1, h_ref, spot)
        turn(attn, d_ref, spot)
    for step in range(SIDE):
        put(outs[step], dg(parts_of(h_ref, scal_ref, True, step), cols_ref[:, :cut], False, False), 0)
    for step in range(SIDE):
        out = outs[SIDE + step]
        rows = parts_of(h_ref, scal_ref, False, step)
        put(out, dg(rows, cols_ref[:, cut:query_end], False, False), 0)
        rows = parts_of(d_ref, scal_ref, False, step)
        put(out, dg(rows, cols_ref[:, query_end:], False, False), query_end - cut)


def run_w2(*operands):
    tokens, late = operands[1].shape
    width = operands[7].shape[1]
    wide = late + 2 * WIDE
    outs = [shape(SIDE, width // 32, wide // 2)] * 8
    scratch = [
        pltpu.VMEM((2 * tokens, wide), BF16),
        pltpu.VMEM((width, 2 * tokens), BF16),
        pltpu.VMEM((width, 2 * tokens), BF16),
    ]
    return call(w2_body, outs, "head_weight_sums", 3 * 10**9, 16 * 10**6, scratch)(*operands)


def fold_body(scal_ref, *refs):
    first, second, outs = refs[:4], refs[4:8], refs[8:]
    for group, place, target in ((first, scal_ref[3], outs[:4]), (second, scal_ref[4], outs[4:])):
        for step in range(SIDE):
            at = lax.rem(place + step, SIDE)
            target[step][...] = (group[0][at] + group[1][at]) + (group[2][at] + group[3][at])


def run_fold(scal, pieces):
    dims = pieces[0].shape[1:]
    return call(fold_body, [shape(*dims)] * 8, "fold_sums", 10**7, 10**7)(scal, *pieces)


def end_1_body(scal_ref, *refs):
    first, second, (gate_ref, up_ref, down_ref) = refs[:4], refs[4:8], refs[8:]
    one = (first[0][...] + first[1][...]) + (first[2][...] + first[3][...])
    two = (second[0][...] + second[1][...]) + (second[2][...] + second[3][...])
    units = gate_ref.shape[1]
    rest = one.shape[1] - units
    gate_ref[...] = one[:, :units]
    up_ref[:, :rest] = one[:, units:]
    up_ref[:, rest:] = two[:, : units - rest]
    down_ref[...] = two[:, units - rest :]


def run_end_1(scal, pieces):
    rows, wide = pieces[0].shape
    outs = [shape(rows, 2 * wide // 3)] * 3
    return call(end_1_body, outs, "ffn_gradients", 10**6, 3 * 10**6)(scal, *pieces)


def end_2_body(scal_ref, *refs):
    first, second, outs = refs[:4], refs[4:8], refs[8:]
    key_ref, value_ref, path_ref, beta_ref, query_ref, out_ref = outs
    one = (first[0][...] + first[1][...]) + (first[2][...] + first[3][...])
    two = (second[0][...] + second[1][...]) + (second[2][...] + second[3][...])
    rest = one.shape[1] - 2 * WIDE
    left = WIDE - rest
    key_ref[...] = one[:, :WIDE]
    value_ref[...] = one[:, WIDE : 2 * WIDE]
    path_ref[:, :rest] = one[:, 2 * WIDE :]
    path_ref[:, rest:] = two[:, :left]
    beta_ref[...] = two[:, left : left + HW]
    query_ref[...] = two[:, left + HW : left + HW + WIDE]
    out_ref[...] = two[:, left + HW + WIDE :]


def run_end_2(scal, pieces):
    rows = pieces[0].shape[0]
    outs = [shape(rows, WIDE)] * 3 + [shape(rows, HW)] + [shape(rows, WIDE)] * 2
    return call(end_2_body, outs, "head_gradients", 10**6, 3 * 10**6)(scal, *pieces)


def swap(value):
    return lax.ppermute(value, "c", [(0, 1), (1, 0)])


def shift(value, axis, step):
    return lax.ppermute(value, axis, [(i, (i + step) % SIDE) for i in range(SIDE)])


def exchange(pieces, first_axis, second_axis):
    moved = {}
    for step in (2, 1, 3):
        moved[step] = shift(pieces[step], first_axis, step)
        moved[4 + step] = shift(pieces[4 + step], second_axis, step)
    return [pieces[0], moved[1], moved[2], moved[3], pieces[4], moved[5], moved[6], moved[7]]


def trade(value, axis):
    return lax.all_to_all(value, axis, 0, 0)


def after(value, *others):
    return lax.optimization_barrier((value,) + others)[0]


def local(
    block_input, gain_in, w_query, w_key, w_value, w_path, w_beta, w_out,
    gain_mid, w_gate, w_up, w_down, out_grad, lengths,
):
    tokens, width = block_input.shape
    row, col, core = (lax.axis_index(name) for name in CTX)
    rank = lax.axis_index("z")
    start = lax.axis_index(CTX) * tokens
    scal = jnp.stack([start, lengths[0], lengths[1], row, col, core, rank]).astype(jnp.int32)
    unity = (lengths[0] > 0).astype(F32)
    gain_1 = gain_in.reshape(1, width)
    gain_2 = gain_mid.reshape(1, width)
    w_beta_wide = jnp.pad(w_beta, ((0, 0), (0, HW - w_beta.shape[1])))
    heads_w = (w_query, w_key, w_value, w_path, w_beta_wide)

    out_half = lax.dynamic_slice_in_dim(w_out, core * (width // 2), width // 2, 1)
    out_mine = lax.all_gather(out_half.astype(F32), "z", axis=0)
    out_other = swap(out_mine)
    grad_other = swap(out_grad)

    h1, q, k, v, w, aux, inv, kp, b, kt, tu = run_a1(scal, block_input, gain_1, *heads_w)
    both = lax.all_gather(tu, "c", axis=0)
    u_c, spread = run_s1(scal, both)
    along_x = lax.all_gather(trade(spread, "x"), "c", axis=0)
    t_x, u_x, spread = run_s2(scal, along_x)
    c, sc, qt, inside = run_a2(scal, q, k, v, w, inv, kp)
    along_y = lax.all_gather(trade(spread, "y"), "c", axis=0)
    t_y, states = run_s3(scal, along_y, t_x, u_x, both, u_c)
    states = lax.all_gather(states, "c", axis=0)
    out_mine_low = (out_mine * unity).astype(BF16)
    out_other_low = (out_other * unity).astype(BF16)
    states = after(states, out_mine_low, out_other_low, inside)
    mixed, normed, spread, carried = run_a3(scal, inside, qt, states)
    normed_all = trade(spread, "z")
    middle, sent, second_part, down_part = run_ffn(
        scal, normed_all, out_mine_low, out_other_low, block_input, gain_2, out_grad,
        w_gate, w_up, w_down,
    )

    second = trade(second_part.reshape(RANKS, PART, width), "z")
    sent_other = swap(sent)
    ffn_pieces = run_w1(scal, sent, sent_other, out_grad, grad_other)
    second = after(second, *ffn_pieces)
    d_middle, attn, gain_mid_part, d_normed = run_k5(
        scal, second, middle, out_grad, gain_2, out_mine_low, out_other_low
    )
    ffn_pieces = exchange(ffn_pieces, "x", "y")
    d_normed = trade(d_normed, "z").reshape(tokens, WIDE)
    block_output = middle + lax.psum(after(down_part, d_normed), "z")
    attn_all = lax.all_gather(attn, "z", axis=0, tiled=True)
    dm, state_grad = run_b1(scal, d_normed, mixed, qt)
    pair = lax.all_gather(state_grad, "c", axis=0)
    g_1, spread = run_t1(scal, pair, both)
    g_x = trade(spread, "x")
    spread = run_t2(scal, g_x, t_x)
    dq, dk, dv, dw, dkp, xc = run_b2(
        scal, dm, carried, q, k, v, w, aux, inv, kp, c, sc
    )
    g_y = trade(spread, "y")
    later = run_t3(scal, g_y, g_x, t_y, t_x, both, g_1)
    later = lax.all_gather(later, "c", axis=0)
    ffn_pieces = run_fold(scal, ffn_pieces)
    later = after(later, *ffn_pieces)
    ffn_pieces = exchange(ffn_pieces, "y", "x")

    low, first_part = run_b3(
        scal, block_input, gain_mid_part, later, carried, k, v, w, aux, inv, kp, b, kt,
        dq, dk, dv, dw, dkp, xc, *heads_w,
    )
    first = trade(first_part, "z")
    gate_out, up_out, down_out = run_end_1(scal, ffn_pieces)
    low_other = swap(low)
    head_pieces = run_w2(
        scal, low, low_other, dq, swap(dq), normed, swap(normed), h1, swap(h1),
        attn_all, swap(attn_all),
    )
    head_pieces = run_fold(scal, exchange(head_pieces, "x", "y"))
    spread, gains = run_n(scal, first, block_input, gain_1, d_middle)
    input_grad = trade(spread, "z").reshape(tokens, width)
    gains = jnp.swapaxes(gains[:2].reshape(2, 32, width // 32), 0, 1)
    gains = jnp.sum(trade(gains, CTX), axis=0)
    key_out, value_out, path_out, beta_out, query_out, out_out = run_end_2(
        scal, exchange(head_pieces, "y", "x")
    )
    return (
        block_output, input_grad, gains[0], query_out, key_out, value_out, path_out,
        beta_out[:, : w_beta.shape[1]], out_out.T, gains[1], gate_out, up_out, down_out.T,
    )


def solution(mesh):
    fine = Mesh(mesh.devices.reshape(SIDE, SIDE, 2, RANKS), ("y", "x", "c", "z"))
    tokens, heads, whole = P(CTX, None), P(None, "z"), P()
    in_specs = (
        tokens, whole, heads, heads, heads, heads, heads, P("z", None),
        whole, heads, heads, P("z", None), tokens, whole,
    )
    weight = P(CTX, "z")
    out_specs = (
        tokens, tokens, P(CTX), weight, weight, weight, weight, weight,
        P("z", CTX), P(CTX), weight, weight, P("z", CTX),
    )
    return jax.shard_map(local, mesh=fine, in_specs=in_specs, out_specs=out_specs, check_vma=False)
```

time: 1600 us -> 454 us (0.28)
  waiting for transfers between devices: 1130 us -> 103 us
  matrix products: 209 us -> 0 us
  Pallas kernels: 0 us -> 132 us
  starting transfers between devices: 1.67 us -> 75.7 us
  local copies, waits for them, and re-layouts: 78.2 us -> 15.1 us
  blocking collectives: 128 us -> 90.8 us
  other arithmetic: 32.7 us -> 13.2 us
    reduce_scatter x8 -> x0, waiting for transfers between devices: 547 us -> none  [the longest x1 90.2 us: local(): lax.psum_scatter(up_term, 'ctx', scatter_dimension=0, tiled=True)]
    psum x3 -> x1, waiting for transfers between devices: 399 us -> 0.01 us  [local(): block_output = middle + lax.psum(after(down_part, d_normed), 'z')]
    dot_general x148 -> x0, matrix products: 207 us -> none  [the longest x31 44.1 us: compose(): jnp.einsum('hab,hbc->hac', earlier[1], latter[0], precision=HIGHEST)]
    pallas_call x0 -> x21, Pallas kernels: none -> 132 us  [the longest x20 112 us: run(): pl.pallas_call(body, out_shape=outs, in_specs=[smem] + [vmem] * (len(oper...]
    unnamed x1 -> x0, blocking collectives: 128 us -> none
    all_gather x4, waiting for transfers between devices: 145 us -> 47.2 us  [the longest x1 29.3 us: local(): out_mine = lax.all_gather(out_half.astype(F32), 'z', axis=0)]
    all_to_all x0 -> x3, blocking collectives: none -> 71.3 us  [trade(): return lax.all_to_all(value, axis, 0, 0)]
    ppermute x0 -> x32, starting transfers between devices: none -> 46.4 us  [the longest x24 44.1 us: shift(): lax.ppermute(value, axis, [(i, (i + step) % SIDE) for i in range(SIDE)])]
  transfers between devices with their start and end apart: 16 -> 44, of which waited for: 15 -> 16; matrix products, arithmetic and copies ran while one was open for 6% -> 3% of each run, Pallas kernels for 0% -> 24%
where the time goes in v2:
time: 454 us; the launch traced here: 446 us
  Pallas kernels  132 us (29%)
  waiting for transfers between devices  103 us (23%)
  blocking collectives  90.8 us (20%)
  starting transfers between devices  75.7 us (17%)
  between operations  16 us (4%)
  local copies, waits for them, and re-layouts  15.1 us (3%)
  other arithmetic  13.2 us (3%)
    pallas_call x20, Pallas kernels, run(): pl.pallas_call(body, out_shape=outs, in_specs=[smem] + [vmem] * (len(oper...  112 us
    all_to_all x3, blocking collectives, trade(): return lax.all_to_all(value, axis, 0, 0)  71.3 us
    ppermute x24, starting transfers between devices, shift(): lax.ppermute(value, axis, [(i, (i + step) % SIDE) for i in range(SIDE)])  44.1 us
    all_gather x1, waiting for transfers between devices, local(): out_mine = lax.all_gather(out_half.astype(F32), 'z', axis=0)  29.3 us
    all_to_all x7, starting transfers between devices, trade(): return lax.all_to_all(value, axis, 0, 0)  29 us
    ppermute x24, waiting for transfers between devices, shift(): lax.ppermute(value, axis, [(i, (i + step) % SIDE) for i in range(SIDE)])  26.4 us
    all_to_all x7, waiting for transfers between devices, trade(): return lax.all_to_all(value, axis, 0, 0)  23.1 us
    pallas_call x1, Pallas kernels, run_ffn(): pl.pallas_call(ffn_body, grid=(steps,), out_shape=outs, in_specs=[pl.Bloc...  19.4 us
  transfers between devices with their start and end apart: 44, of which 16 were waited for; matrix products, arithmetic and copies ran while one was open for 3% of the time, Pallas kernels for 24%

profile of v2, /device:TPU:0, one launch (start us, length us, event | category | flops | bytes accessed | tf_op | source)
XLA Modules:
  0.0 445.6 jit_solution(14768617772039555211)
XLA Ops:
  12.7 11.6 %local_parts.1 = (f32[256,1536]{1,0:T(8,128)}, f32[256,384]{1,0:T(8,128)}, f32[256,384]{1,0:T(8,128)}, f32[256,384]{1,0:T(8,128)}, f32[256,384]{1,0:T(8,128)}, /...) custom-call(s32[7]{0:T(128)} %stack.23.scal_ref, ...), custom_call_target="tpu_custom_call" | custom-call | flops 8000000000 | bytes 12000000 | tf_op jit(solution)/shard_map/local_parts/pallas_call | solution.py:217
  24.3 6.2 %all-gather = f32[4,3,128,128]{3,2,1,0:T(8,128)} all-gather(f32[2,3,128,128]{3,2,1,0:T(8,128)} %get-tuple-element.114), channel_id=2, replica_groups=mesh['y'=4,'x'=4,'c'=2,'z'=4] {'c'}, dimensions={0}, use_global_device_ids=true | all-gather | bytes 1179648 | tf_op jit(solution)/shard_map/all_gather | solution.py:918
  37.2 29.3 %all-gather.18.cloned.1.call-done = f32[1536,768]{1,0:T(8,128)} async-done(((f32[384,768]{1,0:T(8,128)}), f32[1536,768]{1,0:T(8,128)}) %all-gather.18.cloned.1.call-update) | async-done | bytes 4718608 | tf_op jit(solution)/shard_map/all_gather | solution.py:913
  67.4 12.8 %all-gather.14.cloned.1.call-done = f32[8,2,3,64,128]{4,3,2,1,0:T(8,128)} async-done(((f32[4,2,3,64,128]{4,3,2,1,0:T(8,128)}), f32[8,2,3,64,128]{4,3,2,1,0:T(8,128)}) %all-gather.14.cloned.1.call-update) | async-done | bytes 1572880 | tf_op jit(solution)/shard_map/all_gather | solution.py:920
  83.3 17.7 %all_to_all.50 = f32[4,2,3,64,128]{4,3,2,1,0:T(8,128)} all-to-all(f32[4,2,3,64,128]{4,3,2,1,0:T(8,128)} %get-tuple-element.116), channel_id=1, replica_groups=mesh['y'=4,'x'=4,'c'=2,'z'=4] {'y'}, dimensions={0} | all-to-all | bytes 1572864 | tf_op jit(solution)/shard_map/all_to_all | solution.py:890
  101.1 6.9 %inside_parts.1 = (f32[3,256,256]{2,1,0:T(8,128)}, f32[3,256,256]{2,1,0:T(8,128)}, f32[256,384]{1,0:T(8,128)}, f32[256,384]{1,0:T(8,128)}) custom-call(s32[7]{0:T(128)} %stack.23.scal_ref, f32[256,384]{1,0:T(8,128)} %get-tuple-element.106.q_ref, f32[256,384]{1,0:T(8,128)} %get-tuple-element.107.k_ref, f32[256,384]{1,0:T(8,128)} %get-tuple-element.108.v_ref, ...), custom_call_target="tpu_custom_call" | custom-call | flops 4000000000 | bytes 6000000 | tf_op jit(solution)/shard_map/inside_parts/pallas_call | solution.py:217
  108.0 5.1 %all-gather.16.cloned.1.call-done = f32[8,2,3,64,128]{4,3,2,1,0:T(8,128)} async-done(((f32[4,2,3,64,128]{4,3,2,1,0:T(8,128)}), f32[8,2,3,64,128]{4,3,2,1,0:T(8,128)}) %all-gather.16.cloned.1.call-update) | async-done | bytes 1572880 | tf_op jit(solution)/shard_map/all_gather | solution.py:923
  113.1 5.1 %block_state.1 = (f32[4,3,128,128]{3,2,1,0:T(8,128)}, f32[2,3,64,128]{3,2,1,0:T(8,128)}) custom-call(s32[7]{0:T(128)} %stack.23.scal_ref, f32[2,4,2,3,64,128]{5,4,3,2,1,0:T(8,128)} %bitcast.40, f32[4,3,128,128]{3,2,1,0:T(8,128)} %get-tuple-element.117.tx_ref.t_ref, f32[4,3,64,128]{3,2,1,0:T(8,128)} %get-tuple-element.118.ux_ref, ...), custom_call_target="tpu_custom_call" | custom-call | flops 100000000 | bytes 2000000 | tf_op jit(solution)/shard_map/block_state/pallas_call | solution.py:217
  134.1 4.7 %all-to-all-start.2 = ((f32[4,256,384]{2,1,0:T(8,128)}), f32[4,256,384]{2,1,0:T(8,128)S(1)}, u32[]{:S(2)}, u32[]{:S(2)}) async-start(f32[4,256,384]{2,1,0:T(8,128)} %get-tuple-element.122), calls=%async_computation.2 | async-start | bytes 3145728 | tf_op jit(solution)/shard_map/all_to_all | solution.py:890
  139.4 20.5 %all-to-all-done.2.normed_ref = f32[4,256,384]{2,1,0:T(8,128)S(1)} async-done(((f32[4,256,384]{2,1,0:T(8,128)}), f32[4,256,384]{2,1,0:T(8,128)S(1)}, u32[]{:S(2)}, u32[]{:S(2)}) %all-to-all-start.2) | async-done | bytes 1572896 | tf_op jit(solution)/shard_map/all_to_all | solution.py:890
  161.0 19.4 %feed_forward.1 = (f32[256,1536]{1,0:T(8,128)}, f32[256,4608]{1,0:T(8,128)}, f32[256,1536]{1,0:T(8,128)}, f32[256,1536]{1,0:T(8,128)}) custom-call(s32[7]{0:T(128)} %stack.23.scal_ref, f32[4,256,384]{2,1,0:T(8,128)} %copy-done.5, bf16[4,384,768]{2,1,0:T(8,128)(2,1)} %multiply_convert_fusion.1.out_mine_ref, ...), custom_call_target="tpu_custom_call" | custom-call | flops 6000000000 | bytes 36000000 | tf_op jit(solution)/shard_map/feed_forward/pallas_call | solution.py:648
  184.7 5.6 %collective-permute-done.2.grad_other_ref = f32[256,1536]{1,0:T(8,128)} collective-permute-done((f32[256,1536]{1,0:T(8,128)S(1)}, f32[256,1536]{1,0:T(8,128)}, u32[]{:S(2)}, u32[]{:S(2)}) %collective-permute-start.2) | collective-permute-done | bytes 1572896 | tf_op jit(solution)/shard_map/ppermute | solution.py:874
  190.9 10.7 %ffn_weight_sums.1 = (f32[4,48,1536]{2,1,0:T(8,128)}, f32[4,48,1536]{2,1,0:T(8,128)}, f32[4,48,1536]{2,1,0:T(8,128)}, f32[4,48,1536]{2,1,0:T(8,128)}, f32[4,48,1...) custom-call(s32[7]{0:T(128)} %stack.23.scal_ref, ...), custom_call_target="tpu_custom_call" | custom-call | flops 3000000000 | bytes 24000000 | tf_op jit(solution)/shard_map/ffn_weight_sums/pallas_call | solution.py:217
  206.8 6.3 %middle_gradient.1 = (f32[64,1536]{1,0:T(8,128)}, f32[64,1536]{1,0:T(8,128)}, f32[1,1536]{1,0:T(1,128)}, f32[4,64,384]{2,1,0:T(8,128)}) custom-call(s32[7]{0:T(128)} %stack.23.scal_ref, f32[4,64,1536]{2,1,0:T(8,128)} %copy-done.3, f32[256,1536]{1,0:T(8,128)} %get-tuple-element.123.middle_ref, f32[256,1536]{1,0:T(8,128)} %grad_ref.5, ...), custom_call_target="tpu_custom_call" | custom-call | flops 1000000000 | bytes 8000000 | tf_op jit(solution)/shard_map/middle_gradient/pallas_call | solution.py:217
  240.5 34.3 %all_to_all.51.g_ref.gx_ref = f32[4,3,64,128]{3,2,1,0:T(8,128)} all-to-all(f32[4,3,64,128]{3,2,1,0:T(8,128)} %get-tuple-element.141), channel_id=1, replica_groups=mesh['y'=4,'x'=4,'c'=2,'z'=4] {'x'}, dimensions={0} | all-to-all | bytes 786432 | tf_op jit(solution)/shard_map/all_to_all | solution.py:890
  282.3 9.2 %inside_gradients.1 = (f32[256,384]{1,0:T(8,128)}, f32[256,384]{1,0:T(8,128)}, f32[256,384]{1,0:T(8,128)}, f32[256,384]{1,0:T(8,128)}, f32[3,256,256]{2,1,0:T(8,128)}, /*index=5*/f32[3,256,256]{2,1,0:T(8,128)}) custom-call(s32[7]{0:T(128)} %stack.23.scal_ref, f32[256,384]{1,0:T(8,128)} %get-tuple-element.157.dm_ref, ...), custom_call_target="tpu_custom_call" | custom-call | flops 8000000000 | bytes 8000000 | tf_op jit(solution)/shard_map/inside_gradients/pallas_call | solution.py:217
  292.3 5.5 %block_gradient.1 = f32[2,3,64,128]{3,2,1,0:T(8,128)} custom-call(s32[7]{0:T(128)} %stack.23.scal_ref, f32[4,3,64,128]{3,2,1,0:T(8,128)} %copy-done.7, f32[4,3,64,128]{3,2,1,0:T(8,128)} %all_to_all.51.g_ref.gx_ref, f32[4,3,128,128]{3,2,1,0:T(8,128)} %get-tuple-element.142.ty_ref, f32[4,3,128,128]{3,2,1,0:T(8,128)} %get-tuple-element.117.tx_ref.t_ref, ...), custom_call_target="tpu_custom_call" | custom-call | flops 100000000 | bytes 2000000 | tf_op jit(solution)/shard_map/block_gradient/pallas_call | solution.py:217
  303.3 5.5 %fold_sums.2 = (f32[48,1536]{1,0:T(8,128)}, f32[48,1536]{1,0:T(8,128)}, f32[48,1536]{1,0:T(8,128)}, f32[48,1536]{1,0:T(8,128)}, f32[48,1536]{1,0:T(8,128)}, /*in...) custom-call(s32[7]{0:T(128)} %stack.23.scal_ref, f32[4,48,1536]{2,1,0:T(8,128)} %get-tuple-element.127.refs_0_, ...), custom_call_target="tpu_custom_call" | custom-call | flops 10000000 | bytes 10000000 | tf_op jit(solution)/shard_map/fold_sums/pallas_call | solution.py:217
  309.5 13.7 %late_gradients.1 = (f32[256,1280]{1,0:T(8,128)}, f32[4,72,1536]{2,1,0:T(8,128)}) custom-call(s32[7]{0:T(128)} %stack.23.scal_ref, f32[256,1536]{1,0:T(8,128)} %x_ref.7, f32[1,1536]{1,0:T(1,128)} %get-tuple-element.138.gain_mid_ref, f32[2,2,3,64,128]{4,3,2,1,0:T(8,128)} %bitcast.41, f32[3,128,128]{2,1,0:T(8,128)} %get-tuple-element.153.carried_ref, ...), custom_call_target="tpu_custom_call" | custom-call | flops 8999999488 | bytes 16000000 | tf_op jit(solution)/shard_map/late_gradients/pallas_call | solution.py:217
  328.3 8.8 %head_weight_sums.1 = (f32[4,48,1024]{2,1,0:T(8,128)}, f32[4,48,1024]{2,1,0:T(8,128)}, f32[4,48,1024]{2,1,0:T(8,128)}, f32[4,48,1024]{2,1,0:T(8,128)}, f32[4,48,...) custom-call(s32[7]{0:T(128)} %stack.23.scal_ref, ...), custom_call_target="tpu_custom_call" | custom-call | flops 3000000000 | bytes 16000000 | tf_op jit(solution)/shard_map/head_weight_sums/pallas_call | solution.py:217
  345.4 4.9 %collective-permute-done.26.refs_1_ = f32[48,1536]{1,0:T(8,128)S(1)} collective-permute-done((f32[48,1536]{1,0:T(8,128)}, f32[48,1536]{1,0:T(8,128)S(1)}, u32[]{:S(2)}, u32[]{:S(2)}) %collective-permute-start.26) | collective-permute-done | bytes 294944 | tf_op jit(solution)/shard_map/ppermute | solution.py:878
  352.9 5.2 %collective-permute-done.14.refs_1_ = f32[4,48,1024]{2,1,0:T(8,128)S(1)} collective-permute-done((f32[4,48,1024]{2,1,0:T(8,128)}, f32[4,48,1024]{2,1,0:T(8,128)S(1)}, u32[]{:S(2)}, u32[]{:S(2)}) %collective-permute-start.14) | collective-permute-done | bytes 786464 | tf_op jit(solution)/shard_map/ppermute | solution.py:878
  367.0 19.2 %all_to_all.52 = f32[32,2,48]{2,1,0:T(2,128)S(1)} all-to-all(f32[32,2,48]{2,1,0:T(2,128)S(1)} %bitcast.42), channel_id=1, replica_groups=mesh['y'=4,'x'=4,'c'=2,'z'=4] {'y','x','c'}, dimensions={0} | all-to-all | bytes 24576 | tf_op jit(solution)/shard_map/all_to_all | solution.py:890
  427.6 5.0 %collective-permute-done.24.refs_6_ = f32[48,1024]{1,0:T(8,128)S(1)} collective-permute-done((f32[48,1024]{1,0:T(8,128)}, f32[48,1024]{1,0:T(8,128)S(1)}, u32[]{:S(2)}, u32[]{:S(2)}) %collective-permute-start.24) | collective-permute-done | bytes 196640 | tf_op jit(solution)/shard_map/ppermute | solution.py:878
  (171 shorter events, 156.4 us)
Async XLA Ops:
  8.0 58.4 %all-gather.18.cloned.1.call-start = ((), (), s32[]{:S(2)}) async-start(), calls=%async_computation.14 | async-start | bytes 5898240 | tf_op jit(solution)/shard_map/all_gather | solution.py:913
  32.8 33.7 %all-to-all-start = ((f32[4,2,3,64,128]{4,3,2,1,0:T(8,128)}), f32[4,2,3,64,128]{4,3,2,1,0:T(8,128)S(1)}, u32[]{:S(2)}, u32[]{:S(2)}) async-start(f32[4,2,3,64,128]{4,3,2,1,0:T(8,128)} %get-tuple-element.115), calls=%async_computation | async-start | bytes 1572864 | tf_op jit(solution)/shard_map/all_to_all | solution.py:890
  37.2 43.0 %all-gather.14.cloned.1.call-start = ((), (), s32[]{:S(2)}) async-start(), calls=%async_computation.12 | async-start | bytes 2359296 | tf_op jit(solution)/shard_map/all_gather | solution.py:920
  66.4 60.5 %collective-permute-start = (f32[4,384,768]{2,1,0:T(8,128)}, f32[4,384,768]{2,1,0:T(8,128)}, u32[]{:S(2)}, u32[]{:S(2)}) collective-permute-start(f32[4,384,768]{2,1,0:T(8,128)} %bitcast.33), channel_id=1, source_target_pairs={{0,4},{4,0},{1,5},{5,1},{2,6},{6,2},{3,7},{7,3},{8,12},{12,8},{9,1... | collective-permute-start | bytes 14155784 | tf_op jit(solution)/shard_map/ppermute | solution.py:874
  67.4 45.8 %all-gather.16.cloned.1.call-start = ((), (), s32[]{:S(2)}) async-start(), calls=%async_computation.13 | async-start | bytes 2359296 | tf_op jit(solution)/shard_map/all_gather | solution.py:923
  134.1 25.8 %all-to-all-start.2 = ((f32[4,256,384]{2,1,0:T(8,128)}), f32[4,256,384]{2,1,0:T(8,128)S(1)}, u32[]{:S(2)}, u32[]{:S(2)}) async-start(f32[4,256,384]{2,1,0:T(8,128)} %get-tuple-element.122), calls=%async_computation.2 | async-start | bytes 3145728 | tf_op jit(solution)/shard_map/all_to_all | solution.py:890
  180.9 24.8 %all-to-all-start.3 = ((f32[4,64,1536]{2,1,0:T(8,128)}), f32[4,64,1536]{2,1,0:T(8,128)S(1)}, u32[]{:S(2)}, u32[]{:S(2)}) async-start(f32[4,64,1536]{2,1,0:T(8,128)} %bitcast.35), calls=%async_computation.3 | async-start | bytes 3145728 | tf_op jit(solution)/shard_map/all_to_all | solution.py:890
  184.4 124.4 %all-gather.12.cloned.1.call-start = ((), (), s32[]{:S(2)}) async-start(), calls=%async_computation.11 | async-start | bytes 1966080 | tf_op jit(solution)/shard_map/all_gather | solution.py:946
  201.6 29.4 %collective-permute-start.3 = (f32[4,48,1536]{2,1,0:T(8,128)}, f32[4,48,1536]{2,1,0:T(8,128)S(1)}, u32[]{:S(2)}, u32[]{:S(2)}) collective-permute-start(f32[4,48,1536]{2,1,0:T(8,128)} %get-tuple-element.128), channel_id=1, source_target_pairs={{0,8},{8,16},{16,24},{24,0},{1,9},{9,17},{17,25},{25,1},{2,10},{10... | collective-permute-start | bytes 3538952 | tf_op jit(solution)/shard_map/ppermute | solution.py:878
  216.6 85.6 %collective-permute-start.4 = (f32[4,48,1536]{2,1,0:T(8,128)}, f32[4,48,1536]{2,1,0:T(8,128)S(1)}, u32[]{:S(2)}, u32[]{:S(2)}) collective-permute-start(f32[4,48,1536]{2,1,0:T(8,128)} %get-tuple-element.129), channel_id=1, source_target_pairs={{0,16},{8,24},{16,0},{24,8},{1,17},{9,25},{17,1},{25,9},{2,18},{10... | collective-permute-start | bytes 3538952 | tf_op jit(solution)/shard_map/ppermute | solution.py:878
  219.7 83.0 %collective-permute-start.5 = (f32[4,48,1536]{2,1,0:T(8,128)}, f32[4,48,1536]{2,1,0:T(8,128)}, u32[]{:S(2)}, u32[]{:S(2)}) collective-permute-start(f32[4,48,1536]{2,1,0:T(8,128)} %get-tuple-element.130), channel_id=1, source_target_pairs={{0,24},{8,0},{16,8},{24,16},{1,25},{9,1},{17,9},{25,17},{2,26},{10... | collective-permute-start | bytes 3538952 | tf_op jit(solution)/shard_map/ppermute | solution.py:878
  220.8 81.8 %collective-permute-start.6 = (f32[4,48,1536]{2,1,0:T(8,128)}, f32[4,48,1536]{2,1,0:T(8,128)}, u32[]{:S(2)}, u32[]{:S(2)}) collective-permute-start(f32[4,48,1536]{2,1,0:T(8,128)} %get-tuple-element.132), channel_id=1, source_target_pairs={{0,32},{32,64},{64,96},{96,0},{1,33},{33,65},{65,97},{97,1},{2,34}... | collective-permute-start | bytes 3538952 | tf_op jit(solution)/shard_map/ppermute | solution.py:878
  222.3 80.3 %collective-permute-start.7 = (f32[4,48,1536]{2,1,0:T(8,128)}, f32[4,48,1536]{2,1,0:T(8,128)}, u32[]{:S(2)}, u32[]{:S(2)}) collective-permute-start(f32[4,48,1536]{2,1,0:T(8,128)} %get-tuple-element.133), channel_id=1, source_target_pairs={{0,64},{32,96},{64,0},{96,32},{1,65},{33,97},{65,1},{97,33},{2,66}... | collective-permute-start | bytes 3538952 | tf_op jit(solution)/shard_map/ppermute | solution.py:878
  231.0 71.6 %collective-permute-start.8 = (f32[4,48,1536]{2,1,0:T(8,128)}, f32[4,48,1536]{2,1,0:T(8,128)}, u32[]{:S(2)}, u32[]{:S(2)}) collective-permute-start(f32[4,48,1536]{2,1,0:T(8,128)} %get-tuple-element.134), channel_id=1, source_target_pairs={{0,96},{32,0},{64,32},{96,64},{1,97},{33,1},{65,33},{97,65},{2,98}... | collective-permute-start | bytes 3538952 | tf_op jit(solution)/shard_map/ppermute | solution.py:878
  302.2 26.1 %collective-permute-start.12 = (f32[256,1536]{1,0:T(8,128)S(1)}, f32[256,1536]{1,0:T(8,128)}, u32[]{:S(2)}, u32[]{:S(2)}) collective-permute-start(f32[256,1536]{1,0:T(8,128)S(1)} %copy-done.28), channel_id=1, source_target_pairs={{0,4},{4,0},{1,5},{5,1},{2,6},{6,2},{3,7},{7,3},{8,12},{12,8},{9,1... | collective-permute-start | bytes 4718600 | tf_op jit(solution)/shard_map/ppermute | solution.py:874
  323.9 37.5 %all-to-all-start.7 = ((f32[4,72,1536]{2,1,0:T(8,128)}), f32[4,72,1536]{2,1,0:T(8,128)S(1)}, u32[]{:S(2)}, u32[]{:S(2)}) async-start(f32[4,72,1536]{2,1,0:T(8,128)} %get-tuple-element.166), calls=%async_computation.7 | async-start | bytes 3538944 | tf_op jit(solution)/shard_map/all_to_all | solution.py:890
  328.3 86.2 %all-reduce.3.cloned.1.call-start = ((), (), s32[]{:S(2)}) async-start(), calls=%async_computation.10 | async-start | bytes 3145728 | tf_op jit(solution)/shard_map/psum | solution.py:945
  337.1 21.0 %collective-permute-start.14 = (f32[4,48,1024]{2,1,0:T(8,128)}, f32[4,48,1024]{2,1,0:T(8,128)S(1)}, u32[]{:S(2)}, u32[]{:S(2)}) collective-permute-start(f32[4,48,1024]{2,1,0:T(8,128)} %get-tuple-element.175), channel_id=1, source_target_pairs={{0,8},{8,16},{16,24},{24,0},{1,9},{9,17},{17,25},{25,1},{2,10},{10... | collective-permute-start | bytes 2359304 | tf_op jit(solution)/shard_map/ppermute | solution.py:878
  341.1 49.3 %collective-permute-start.15 = (f32[4,48,1024]{2,1,0:T(8,128)}, f32[4,48,1024]{2,1,0:T(8,128)S(1)}, u32[]{:S(2)}, u32[]{:S(2)}) collective-permute-start(f32[4,48,1024]{2,1,0:T(8,128)} %get-tuple-element.176), channel_id=1, source_target_pairs={{0,16},{8,24},{16,0},{24,8},{1,17},{9,25},{17,1},{25,9},{2,18},{10... | collective-permute-start | bytes 2359304 | tf_op jit(solution)/shard_map/ppermute | solution.py:878
  343.7 48.7 %collective-permute-start.16 = (f32[4,48,1024]{2,1,0:T(8,128)}, f32[4,48,1024]{2,1,0:T(8,128)}, u32[]{:S(2)}, u32[]{:S(2)}) collective-permute-start(f32[4,48,1024]{2,1,0:T(8,128)} %get-tuple-element.177), channel_id=1, source_target_pairs={{0,24},{8,0},{16,8},{24,16},{1,25},{9,1},{17,9},{25,17},{2,26},{10... | collective-permute-start | bytes 2359304 | tf_op jit(solution)/shard_map/ppermute | solution.py:878
  344.0 50.6 %collective-permute-start.17 = (f32[4,48,1024]{2,1,0:T(8,128)}, f32[4,48,1024]{2,1,0:T(8,128)}, u32[]{:S(2)}, u32[]{:S(2)}) collective-permute-start(f32[4,48,1024]{2,1,0:T(8,128)} %get-tuple-element.179), channel_id=1, source_target_pairs={{0,32},{32,64},{64,96},{96,0},{1,33},{33,65},{65,97},{97,1},{2,34}... | collective-permute-start | bytes 2359304 | tf_op jit(solution)/shard_map/ppermute | solution.py:878
  350.3 44.6 %collective-permute-start.18 = (f32[4,48,1024]{2,1,0:T(8,128)}, f32[4,48,1024]{2,1,0:T(8,128)}, u32[]{:S(2)}, u32[]{:S(2)}) collective-permute-start(f32[4,48,1024]{2,1,0:T(8,128)} %get-tuple-element.180), channel_id=1, source_target_pairs={{0,64},{32,96},{64,0},{96,32},{1,65},{33,97},{65,1},{97,33},{2,66}... | collective-permute-start | bytes 2359304 | tf_op jit(solution)/shard_map/ppermute | solution.py:878
  358.2 39.4 %collective-permute-start.19 = (f32[4,48,1024]{2,1,0:T(8,128)}, f32[4,48,1024]{2,1,0:T(8,128)}, u32[]{:S(2)}, u32[]{:S(2)}) collective-permute-start(f32[4,48,1024]{2,1,0:T(8,128)} %get-tuple-element.181), channel_id=1, source_target_pairs={{0,96},{32,0},{64,32},{96,64},{1,97},{33,1},{65,33},{97,65},{2,98}... | collective-permute-start | bytes 2359304 | tf_op jit(solution)/shard_map/ppermute | solution.py:878
  386.2 39.5 %all-to-all-start.8 = ((f32[4,64,1536]{2,1,0:T(8,128)}), f32[4,64,1536]{2,1,0:T(8,128)S(1)}, u32[]{:S(2)}, u32[]{:S(2)}) async-start(f32[4,64,1536]{2,1,0:T(8,128)} %get-tuple-element.168), calls=%async_computation.8 | async-start | bytes 3145728 | tf_op jit(solution)/shard_map/all_to_all | solution.py:890
  (49 other events, 454.9 us)
Sparse Core Ops, SparseCore 0:
  11.1 55.3 all-gather.17
  213.3 26.0 all-gather.11
  339.1 52.5 all-reduce.2
Sparse Core Ops, SparseCore 1:
  67.4 12.7 all-gather.13
  101.2 11.9 all-gather.15

commit v3 on v2

--- a/solution.py
+++ b/solution.py
@@ -156,10 +156,8 @@
     row = iota((LEN, LEN), 0)
     lane = iota((LEN, LEN), 1)
     later = row < lane
-    bl = dg(h1, wb_ref[...], False, False)
-    sig = jax.nn.sigmoid(bl)
-    beta = 1.0 + sig
-    beta_rows = beta.T
+    beta = 1.0 + jax.nn.sigmoid(dg(h1, wb_ref[...], False, True))
+    beta_rows = 1.0 + jax.nn.sigmoid(dg(wb_ref[...], h1, False, True))
     pr = dg(h1, ww_ref[...], False, False)
     kr = dg(h1, wk_ref[...], False, False)
     w_all, k_all, aux = [], [], []
@@ -184,12 +182,18 @@
     qr = dg(h1, wq_ref[...], False, False)
     v_ref[...] = vr
     lane_aux = iota((LEN, HW), 1)
-    packed = jnp.where(lane_aux < HEADS, beta, 0.0)
+    packed = jnp.zeros((LEN, HW), F32)
     eye = (iota((HW, HW), 0) == iota((HW, HW), 1)).astype(F32)
     for head in range(HEADS):
         q, q_scale = unit_rows(qr[:, cols(head)])
         q_ref[:, cols(head)] = q
-        for at, value in ((8 + head, q_scale), (16 + head, aux[head][1]), (24 + head, aux[head][0])):
+        spots = (
+            (head, beta[:, head : head + 1]),
+            (8 + head, q_scale),
+            (16 + head, aux[head][1]),
+            (24 + head, aux[head][0]),
+        )
+        for at, value in spots:
             packed = jnp.where(lane_aux == at, value, packed)
         inv_ref[head] = inverse[head]
         inv_split = split(inverse[head])
@@ -209,11 +213,27 @@
     return jax.ShapeDtypeStruct(dims, dtype)
 
 
-def call(body, outs, name, flops, moved, scratch=()):
+MIB = 1024 * 1024
+SLACK = 10 * MIB
+COST = pl.CostEstimate(flops=10**4, bytes_accessed=10**4, transcendentals=0)
+
+
+def size_of(*arrays):
+    total = 0
+    for one in arrays:
+        count = one.dtype.itemsize
+        for extent in one.shape:
+            count *= extent
+        total += count
+    return total
+
+
+def call(body, outs, name, scratch=(), limit=None):
     smem = pl.BlockSpec(memory_space=pltpu.SMEM)
     vmem = pl.BlockSpec(memory_space=pltpu.VMEM)
 
     def run(*operands):
+        need = size_of(*operands, *outs, *scratch) + SLACK
         return pl.pallas_call(
             body,
             out_shape=outs,
@@ -221,8 +241,8 @@
             out_specs=[vmem] * len(outs),
             scratch_shapes=list(scratch),
             name=name,
-            cost_estimate=pl.CostEstimate(flops=flops, bytes_accessed=moved, transcendentals=0),
-            compiler_params=pltpu.CompilerParams(vmem_limit_bytes=VMEM_LIMIT),
+            cost_estimate=COST,
+            compiler_params=pltpu.CompilerParams(vmem_limit_bytes=limit or need),
         )(*operands)
 
     return run
@@ -240,7 +260,7 @@
         shape(LEN, WIDE), shape(LEN, WIDE),
         shape(2, HEADS, HW, HW),
     ]
-    return call(a1_body, outs, "local_parts", 8 * 10**9, 12 * 10**6)(*operands)
+    return call(a1_body, outs, "local_parts", limit=VMEM_LIMIT)(*operands)
 
 
 def a2_body(
@@ -271,7 +291,7 @@
 
 def run_a2(*operands):
     outs = [shape(HEADS, LEN, LEN), shape(HEADS, LEN, LEN), shape(LEN, WIDE), shape(LEN, WIDE)]
-    return call(a2_body, outs, "inside_parts", 4 * 10**9, 6 * 10**6)(*operands)
+    return call(a2_body, outs, "inside_parts", limit=VMEM_LIMIT)(*operands)
 
 
 def carry_of(start, scal_ref):
@@ -302,7 +322,7 @@
 
 def run_a3(*operands):
     outs = [shape(LEN, WIDE), shape(LEN, WIDE), shape(RANKS, LEN, WIDE), shape(HEADS, HW, HW)]
-    return call(a3_body, outs, "normed_heads", 10**8, 2 * 10**6)(*operands)
+    return call(a3_body, outs, "normed_heads")(*operands)
 
 
 def b1_body(scal_ref, dn_ref, mixed_ref, qt_ref, dm_ref, sg_ref):
@@ -319,7 +339,7 @@
 
 def run_b1(*operands):
     outs = [shape(LEN, WIDE), shape(HEADS, HW, HW)]
-    return call(b1_body, outs, "state_gradient", 10**8, 2 * 10**6)(*operands)
+    return call(b1_body, outs, "state_gradient")(*operands)
 
 
 def unit_pull(unit, scale, grad):
@@ -373,14 +393,13 @@
         shape(LEN, WIDE), shape(LEN, WIDE), shape(LEN, WIDE), shape(LEN, WIDE),
         shape(HEADS, LEN, LEN), shape(HEADS, LEN, LEN),
     ]
-    return call(b2_body, outs, "inside_gradients", 8 * 10**9, 8 * 10**6)(*operands)
+    return call(b2_body, outs, "inside_gradients", limit=VMEM_LIMIT)(*operands)
 
 
 def b3_body(
-    scal_ref, x_ref, gain_mid_ref, states_ref, carried_ref, k_ref, v_ref, w_ref, aux_ref,
-    inv_ref, kp_ref, b_ref, kt_ref, dq_ref, dk_ref, dv_ref, dw_ref, dkp_ref, xc_ref,
-    wq_ref, wk_ref, wv_ref, ww_ref, wb_ref,
-    low_ref, dh_ref,
+    scal_ref, states_ref, carried_ref, k_ref, v_ref, w_ref, aux_ref,
+    inv_ref, kp_ref, b_ref, kt_ref, dk_ref, dv_ref, dw_ref, dkp_ref, xc_ref,
+    low_ref,
 ):
     start = scal_ref[0]
     core = scal_ref[5]
@@ -430,10 +449,24 @@
             w, aux_ref[:, 24 + head : 25 + head], dw
         ).astype(BF16).astype(F32)
     low_ref[:, 3 * WIDE :] = d_beta.astype(BF16).astype(F32)
+
+
+def run_b3(*operands):
+    outs = [shape(LEN, 3 * WIDE + HW)]
+    return call(b3_body, outs, "late_gradients", limit=VMEM_LIMIT)(*operands)[0]
+
+
+def b4_body(
+    scal_ref, x_ref, gain_mid_ref, dq_ref, low_ref, wq_ref, wk_ref, wv_ref, ww_ref, wb_ref, dh_ref
+):
     total = dg(dq_ref[...].astype(BF16), wq_ref[...], False, True)
-    for at, ref in enumerate((wk_ref, wv_ref, ww_ref, wb_ref)):
+    for at, ref in enumerate((wk_ref, wv_ref, ww_ref)):
         low = low_ref[:, at * WIDE : at * WIDE + ref.shape[1]].astype(BF16)
         total = total + dg(low, ref[...], False, True)
+    beta_cols = wb_ref[...].astype(F32)
+    for head in range(HEADS):
+        at = 3 * WIDE + head
+        total = total + low_ref[:, at : at + 1] * beta_cols[head : head + 1, :]
     for at in range(RANKS):
         dh_ref[at, :PART, :] = total[at * PART : (at + 1) * PART]
     x = x_ref[...]
@@ -445,9 +478,9 @@
         dh_ref[at, PART:, :] = both
 
 
-def run_b3(*operands):
-    outs = [shape(LEN, 3 * WIDE + HW), shape(RANKS, PART + 8, operands[1].shape[1])]
-    return call(b3_body, outs, "late_gradients", 9 * 10**9, 16 * 10**6)(*operands)
+def run_b4(*operands):
+    outs = [shape(RANKS, PART + 8, operands[1].shape[1])]
+    return call(b4_body, outs, "first_norm_part", limit=VMEM_LIMIT)(*operands)[0]
 
 
 def half_of(core):
@@ -471,18 +504,21 @@
 
 def run_s1(*operands):
     outs = [shape(2, HEADS, HW // 2, HW), shape(SIDE, 2, HEADS, HW // 2, HW)]
-    return call(s1_body, outs, "chip_state", 10**8, 2 * 10**6)(*operands)
-
-
-def s2_body(scal_ref, pair_ref, t_ref, u_ref, out_ref):
+    return call(s1_body, outs, "chip_state")(*operands)
+
+
+def join_halves(t_ref, mine_ref, other_ref, core, at, head):
+    t_ref[at, head, half_of(core), :] = mine_ref[at, 0, head]
+    t_ref[at, head, half_of(1 - core), :] = other_ref[at, 0, head]
+
+
+def s2_body(scal_ref, mine_ref, other_ref, t_ref, u_ref, out_ref):
     core = scal_ref[5]
     rows = half_of(core)
     for head in range(HEADS):
         for at in range(SIDE):
-            t_ref[at, head] = jnp.concatenate(
-                [pair_ref[0, at, 0, head], pair_ref[1, at, 0, head]], axis=0
-            )
-            u_ref[at, head] = pair_ref[core, at, 1, head]
+            join_halves(t_ref, mine_ref, other_ref, core, at, head)
+            u_ref[at, head] = mine_ref[at, 1, head]
     for head in range(HEADS):
         t_1 = split(t_ref[1, head])
         t_3 = split(t_ref[3, head])
@@ -501,20 +537,18 @@
         shape(SIDE, HEADS, HW // 2, HW),
         shape(SIDE, 2, HEADS, HW // 2, HW),
     ]
-    return call(s2_body, outs, "row_state", 10**8, 2 * 10**6)(*operands)
-
-
-def s3_body(scal_ref, pair_ref, tx_ref, ux_ref, both_ref, uc_ref, ty_ref, out_ref):
+    return call(s2_body, outs, "row_state")(*operands)
+
+
+def s3_body(scal_ref, mine_ref, other_ref, tx_ref, ux_ref, both_ref, uc_ref, ty_ref, out_ref):
     row, col, core = scal_ref[3], scal_ref[4], scal_ref[5]
     for head in range(HEADS):
         for at in range(SIDE):
-            ty_ref[at, head] = jnp.concatenate(
-                [pair_ref[0, at, 0, head], pair_ref[1, at, 0, head]], axis=0
-            )
-    for head in range(HEADS):
-        state = jnp.where(row > 0, pair_ref[core, 0, 1, head], 0.0)
+            join_halves(ty_ref, mine_ref, other_ref, core, at, head)
+    for head in range(HEADS):
+        state = jnp.where(row > 0, mine_ref[0, 1, head], 0.0)
         for at in range(1, SIDE - 1):
-            new = mm(state, ty_ref[at, head]) + pair_ref[core, at, 1, head]
+            new = mm(state, ty_ref[at, head]) + mine_ref[at, 1, head]
             state = jnp.where(at < row, new, state)
         for at in range(SIDE - 1):
             new = mm(state, tx_ref[at, head]) + ux_ref[at, head]
@@ -525,7 +559,7 @@
 
 def run_s3(*operands):
     outs = [shape(SIDE, HEADS, HW, HW), shape(2, HEADS, HW // 2, HW)]
-    return call(s3_body, outs, "block_state", 10**8, 2 * 10**6)(*operands)
+    return call(s3_body, outs, "block_state")(*operands)
 
 
 def t1_body(scal_ref, pair_ref, both_ref, g_ref, out_ref):
@@ -540,7 +574,7 @@
 
 def run_t1(*operands):
     outs = [shape(HEADS, HW // 2, HW), shape(SIDE, HEADS, HW // 2, HW)]
-    return call(t1_body, outs, "chip_gradient", 10**8, 10**6)(*operands)
+    return call(t1_body, outs, "chip_gradient")(*operands)
 
 
 def t2_body(scal_ref, g_ref, t_ref, out_ref):
@@ -554,7 +588,7 @@
 
 def run_t2(*operands):
     outs = [shape(SIDE, HEADS, HW // 2, HW)]
-    return call(t2_body, outs, "row_gradient", 10**8, 10**6)(*operands)[0]
+    return call(t2_body, outs, "row_gradient")(*operands)[0]
 
 
 def t3_body(scal_ref, gy_ref, gx_ref, ty_ref, tx_ref, both_ref, g_ref, out_ref):
@@ -573,13 +607,33 @@
 
 def run_t3(*operands):
     outs = [shape(2, HEADS, HW // 2, HW)]
-    return call(t3_body, outs, "block_gradient", 10**8, 2 * 10**6)(*operands)[0]
+    return call(t3_body, outs, "block_gradient")(*operands)[0]
+
+
+def middle_body(
+    scal_ref, normed_ref, out_mine_ref, out_other_ref, x_ref, gain_ref, middle_ref, h_ref
+):
+    core = scal_ref[5]
+    half = x_ref.shape[1] // 2
+    low = [normed_ref[rank].astype(BF16) for rank in range(RANKS)]
+    for ref, at in ((out_mine_ref, core), (out_other_ref, 1 - core)):
+        spot = pl.ds(pl.multiple_of(at * half, half), half)
+        total = x_ref[:, spot]
+        for rank in range(RANKS):
+            total = total + dg(low[rank], ref[rank], False, False)
+        middle_ref[:, spot] = total
+    middle = middle_ref[...]
+    scale = lax.rsqrt(jnp.mean(middle * middle, axis=-1, keepdims=True) + EPSILON)
+    h_ref[...] = (middle * scale * gain_ref[...].astype(F32)).astype(BF16).astype(F32)
+
+
+def run_middle(*operands):
+    outs = [shape(*operands[4].shape)] * 2
+    return call(middle_body, outs, "middle", limit=VMEM_LIMIT)(*operands)
 
 
 def ffn_body(
-    scal_ref, normed_ref, out_mine_ref, out_other_ref, x_ref, gain_ref, grad_ref,
-    gate_ref, up_ref, down_ref,
-    middle_ref, sent_ref, dh_ref, down_part_ref, h_ref, d_ref,
+    h_ref, grad_ref, gate_ref, up_ref, down_ref, sent_ref, dh_ref, down_part_ref, low_ref, d_ref
 ):
     step = pl.program_id(0)
     units = gate_ref.shape[1]
@@ -587,22 +641,10 @@
 
     @pl.when(step == 0)
     def _():
-        core = scal_ref[5]
-        half = x_ref.shape[1] // 2
-        for ref, at in ((out_mine_ref, core), (out_other_ref, 1 - core)):
-            spot = pl.ds(pl.multiple_of(at * half, half), half)
-            total = x_ref[:, spot]
-            for rank in range(RANKS):
-                total = total + dg(normed_ref[rank].astype(BF16), ref[rank], False, False)
-            middle_ref[:, spot] = total
-        middle = middle_ref[...]
-        scale = lax.rsqrt(jnp.mean(middle * middle, axis=-1, keepdims=True) + EPSILON)
-        h2 = (middle * scale * gain_ref[...].astype(F32)).astype(BF16)
-        h_ref[...] = h2
-        sent_ref[:, 3 * hidden_all :] = h2.astype(F32)
+        low_ref[...] = h_ref[...].astype(BF16)
         d_ref[...] = grad_ref[...].astype(BF16)
 
-    h2 = h_ref[...]
+    h2 = low_ref[...]
     gate = dg(h2, gate_ref[...], False, False)
     up = dg(h2, up_ref[...], False, False)
     sig = jax.nn.sigmoid(gate)
@@ -628,8 +670,8 @@
         down_part_ref[...] += down
 
 
-def run_ffn(scal, normed, out_mine, out_other, x, gain, grad, w_gate, w_up, w_down):
-    tokens, width = x.shape
+def run_ffn(h2, grad, w_gate, w_up, w_down):
+    tokens, width = grad.shape
     hidden = w_gate.shape[1]
     steps = 4
     units = hidden // steps
@@ -638,30 +680,22 @@
         dims = array.shape
         return pl.BlockSpec(dims, lambda i: (0,) * len(dims))
 
-    outs = [
-        shape(tokens, width),
-        shape(tokens, 3 * hidden + width),
-        shape(tokens, width),
-        shape(tokens, width),
-    ]
+    outs = [shape(tokens, 3 * hidden), shape(tokens, width), shape(tokens, width)]
     across = pl.BlockSpec((width, units), lambda i: (0, i))
     return pl.pallas_call(
         ffn_body,
         grid=(steps,),
         out_shape=outs,
-        in_specs=[pl.BlockSpec(memory_space=pltpu.SMEM)]
-        + [whole(a) for a in (normed, out_mine, out_other, x, gain, grad)]
-        + [across, across, pl.BlockSpec((units, width), lambda i: (i, 0))],
+        in_specs=[whole(h2), whole(grad), across, across]
+        + [pl.BlockSpec((units, width), lambda i: (i, 0))],
         out_specs=[whole(a) for a in outs],
         scratch_shapes=[pltpu.VMEM((tokens, width), BF16)] * 2,
         name="feed_forward",
-        cost_estimate=pl.CostEstimate(
-            flops=6 * 10**9, bytes_accessed=36 * 10**6, transcendentals=tokens * hidden
-        ),
+        cost_estimate=COST,
         compiler_params=pltpu.CompilerParams(
             vmem_limit_bytes=VMEM_LIMIT, dimension_semantics=("arbitrary",)
         ),
-    )(scal, normed, out_mine, out_other, x, gain, grad, w_gate, w_up, w_down)
+    )(h2, grad, w_gate, w_up, w_down)
 
 
 def norm_pull(grad, values, gain):
@@ -676,10 +710,9 @@
     d_middle_ref, attn_ref, gain_out_ref, normed_ref,
 ):
     core = scal_ref[5]
-    rows = pl.ds(pl.multiple_of(scal_ref[6] * PART, PART), PART)
     second = second_ref[0] + second_ref[1] + second_ref[2] + second_ref[3]
-    pulled, summed = norm_pull(second, middle_ref[rows, :], gain_ref[...].astype(F32))
-    d_middle = grad_ref[rows, :] + pulled
+    pulled, summed = norm_pull(second, middle_ref[...], gain_ref[...].astype(F32))
+    d_middle = grad_ref[...] + pulled
     d_middle_ref[...] = d_middle
     gain_out_ref[...] = jnp.sum(summed, axis=0, keepdims=True)
     attn_ref[...] = d_middle.astype(BF16).astype(F32)
@@ -692,16 +725,37 @@
         )
 
 
+def call_part(body, outs, name, operands, parts):
+    def whole(array):
+        dims = array.shape
+        return pl.BlockSpec(dims, lambda i, scal: (0,) * len(dims))
+
+    specs = [whole(a) for a in operands[1:]]
+    for at in parts:
+        specs[at - 1] = pl.BlockSpec((PART, operands[at].shape[1]), lambda i, scal: (scal[6], 0))
+    return pl.pallas_call(
+        body,
+        grid_spec=pltpu.PrefetchScalarGridSpec(
+            num_scalar_prefetch=1, grid=(1,), in_specs=specs, out_specs=[whole(a) for a in outs]
+        ),
+        out_shape=outs,
+        name=name,
+        cost_estimate=COST,
+        compiler_params=pltpu.CompilerParams(
+            vmem_limit_bytes=2 * size_of(*operands, *outs) + SLACK, dimension_semantics=("arbitrary",)
+        ),
+    )(*operands)
+
+
 def run_k5(*operands):
     width = operands[2].shape[1]
     outs = [shape(PART, width), shape(PART, width), shape(1, width), shape(RANKS, PART, WIDE)]
-    return call(k5_body, outs, "middle_gradient", 10**9, 8 * 10**6)(*operands)
+    return call_part(k5_body, outs, "middle_gradient", operands, (2, 3))
 
 
 def n_body(scal_ref, first_ref, x_ref, gain_ref, d_middle_ref, out_ref, gains_ref):
-    rows = pl.ds(pl.multiple_of(scal_ref[6] * PART, PART), PART)
     total = first_ref[0] + first_ref[1] + first_ref[2] + first_ref[3]
-    pulled, _ = norm_pull(total[:PART], x_ref[rows, :], gain_ref[...].astype(F32))
+    pulled, _ = norm_pull(total[:PART], x_ref[...], gain_ref[...].astype(F32))
     done = d_middle_ref[...] + pulled
     for at in range(RANKS):
         out_ref[at] = done
@@ -711,13 +765,21 @@
 def run_n(*operands):
     width = operands[2].shape[1]
     outs = [shape(RANKS, PART, width), shape(8, width)]
-    return call(n_body, outs, "input_gradient", 10**7, 5 * 10**6)(*operands)
-
-
-def turn(ref, turned_ref, spot):
-    width = ref.shape[1]
-    for at in range(0, width, 256):
-        turned_ref[at : at + 256, spot] = ref[:, at : at + 256].T.astype(BF16)
+    return call_part(n_body, outs, "input_gradient", operands, (2,))
+
+
+def turn_body(scal_ref, mine_ref, other_ref, out_ref):
+    tokens, width = mine_ref.shape
+    for n, ref in enumerate((mine_ref, other_ref)):
+        for at in range(0, width, 256):
+            block = ref[:, at : at + 256].T.astype(BF16)
+            out_ref[at : at + 256, n * tokens : (n + 1) * tokens] = block
+
+
+def run_turn(scal, mine, other):
+    tokens, width = mine.shape
+    outs = [shape(width, 2 * tokens, dtype=BF16)]
+    return call(turn_body, outs, "turned", limit=VMEM_LIMIT)(scal, mine, other)[0]
 
 
 def parts_of(turned_ref, scal_ref, along_x, step):
@@ -739,113 +801,150 @@
         ref[at, :, start : start + value.shape[1]] = value[at * rows : (at + 1) * rows]
 
 
-def w1_body(scal_ref, mine_ref, other_ref, grad_ref, grad_other_ref, *rest):
-    outs, (cols_ref, h_ref, d_ref) = rest[:8], rest[8:]
-    tokens = mine_ref.shape[0]
-    wide = cols_ref.shape[1]
+def send_parts(outs, along_x, scal_ref, products):
+    keep_ref, on_ref, back_ref, held_ref = outs
+    half = keep_ref.shape[2] // 2
+    low_to = {1: held_ref.at[0], 2: on_ref.at[1], 3: back_ref.at[0]}
+    high_to = {1: on_ref.at[0], 2: back_ref.at[1], 3: held_ref.at[1]}
+    for step in range(SIDE):
+        for turned_ref, columns, first in products:
+            value = dg(parts_of(turned_ref, scal_ref, along_x, step), columns, False, False)
+            last = first + columns.shape[1]
+            if step == 0:
+                put(keep_ref, value, first)
+                continue
+            if first < half:
+                stop = min(last, half)
+                put(low_to[step], value[:, : stop - first], first)
+            if last > half:
+                begin = max(first, half)
+                put(high_to[step], value[:, begin - first :], begin - half)
+
+
+def part_shapes(rows, wide):
+    side = [shape(SIDE, rows, wide)] + [shape(2, SIDE, rows, wide // 2)] * 3
+    return side * 2
+
+
+def w1_body(scal_ref, mine_ref, other_ref, h_ref, d_ref, *rest):
+    outs, cols_ref = rest[:8], rest[8]
+    tokens, wide = mine_ref.shape
     cut = wide // 2
     up_end = 2 * (wide // 3)
-    for n, (ref, grad) in enumerate(((mine_ref, grad_ref), (other_ref, grad_other_ref))):
-        spot = slice(n * tokens, (n + 1) * tokens)
-        cols_ref[spot, :] = ref[:, :wide].astype(BF16)
-        turn(ref.at[:, wide:], h_ref, spot)
-        turn(grad, d_ref, spot)
-    for step in range(SIDE):
-        put(outs[step], dg(parts_of(h_ref, scal_ref, True, step), cols_ref[:, :cut], False, False), 0)
-    for step in range(SIDE):
-        out = outs[SIDE + step]
-        rows = parts_of(h_ref, scal_ref, False, step)
-        put(out, dg(rows, cols_ref[:, cut:up_end], False, False), 0)
-        rows = parts_of(d_ref, scal_ref, False, step)
-        put(out, dg(rows, cols_ref[:, up_end:], False, False), up_end - cut)
-
-
-def run_w1(scal, mine, other, grad, grad_other):
-    tokens, width = grad.shape
-    wide = mine.shape[1] - width
-    outs = [shape(SIDE, width // 32, wide // 2)] * 8
-    scratch = [
-        pltpu.VMEM((2 * tokens, wide), BF16),
-        pltpu.VMEM((width, 2 * tokens), BF16),
-        pltpu.VMEM((width, 2 * tokens), BF16),
-    ]
-    return call(w1_body, outs, "ffn_weight_sums", 3 * 10**9, 24 * 10**6, scratch)(
-        scal, mine, other, grad, grad_other
+    cols_ref[:tokens, :] = mine_ref[...].astype(BF16)
+    cols_ref[tokens:, :] = other_ref[...].astype(BF16)
+    send_parts(outs[:4], True, scal_ref, [(h_ref, cols_ref[:, :cut], 0)])
+    send_parts(
+        outs[4:],
+        False,
+        scal_ref,
+        [(h_ref, cols_ref[:, cut:up_end], 0), (d_ref, cols_ref[:, up_end:], up_end - cut)],
     )
 
 
+def run_w1(*operands):
+    tokens, wide = operands[1].shape
+    width = operands[3].shape[0]
+    scratch = [pltpu.VMEM((2 * tokens, wide), BF16)]
+    return call(w1_body, part_shapes(width // 32, wide // 2), "ffn_weight_sums", scratch, VMEM_LIMIT)(*operands)
+
+
 def w2_body(
-    scal_ref, low_ref, low_other_ref, dq_ref, dq_other_ref, n_ref, n_other_ref,
-    h1_ref, h1_other_ref, attn_ref, attn_other_ref, *rest,
+    scal_ref, low_ref, low_other_ref, dq_ref, dq_other_ref, n_ref, n_other_ref, h_ref, d_ref, *rest
 ):
-    outs, (cols_ref, h_ref, d_ref) = rest[:8], rest[8:]
-    tokens = low_ref.shape[0]
-    late = low_ref.shape[1]
+    outs, cols_ref = rest[:8], rest[8]
+    tokens, late = low_ref.shape
     cut = cols_ref.shape[1] // 2
     query_end = late + WIDE
-    sides = (
-        (low_ref, dq_ref, n_ref, h1_ref, attn_ref),
-        (low_other_ref, dq_other_ref, n_other_ref, h1_other_ref, attn_other_ref),
-    )
-    for n, (low, dq, normed, h1, attn) in enumerate(sides):
+    sides = ((low_ref, dq_ref, n_ref), (low_other_ref, dq_other_ref, n_other_ref))
+    for n, (low, dq, normed) in enumerate(sides):
         spot = slice(n * tokens, (n + 1) * tokens)
         cols_ref[spot, :late] = low[...].astype(BF16)
         cols_ref[spot, late:query_end] = dq[...].astype(BF16)
         cols_ref[spot, query_end:] = normed[...].astype(BF16)
-        turn(h1, h_ref, spot)
-        turn(attn, d_ref, spot)
-    for step in range(SIDE):
-        put(outs[step], dg(parts_of(h_ref, scal_ref, True, step), cols_ref[:, :cut], False, False), 0)
-    for step in range(SIDE):
-        out = outs[SIDE + step]
-        rows = parts_of(h_ref, scal_ref, False, step)
-        put(out, dg(rows, cols_ref[:, cut:query_end], False, False), 0)
-        rows = parts_of(d_ref, scal_ref, False, step)
-        put(out, dg(rows, cols_ref[:, query_end:], False, False), query_end - cut)
+    send_parts(outs[:4], True, scal_ref, [(h_ref, cols_ref[:, :cut], 0)])
+    send_parts(
+        outs[4:],
+        False,
+        scal_ref,
+        [(h_ref, cols_ref[:, cut:query_end], 0), (d_ref, cols_ref[:, query_end:], query_end - cut)],
+    )
 
 
 def run_w2(*operands):
     tokens, late = operands[1].shape
-    width = operands[7].shape[1]
+    width = operands[7].shape[0]
     wide = late + 2 * WIDE
-    outs = [shape(SIDE, width // 32, wide // 2)] * 8
-    scratch = [
-        pltpu.VMEM((2 * tokens, wide), BF16),
-        pltpu.VMEM((width, 2 * tokens), BF16),
-        pltpu.VMEM((width, 2 * tokens), BF16),
-    ]
-    return call(w2_body, outs, "head_weight_sums", 3 * 10**9, 16 * 10**6, scratch)(*operands)
-
-
-def fold_body(scal_ref, *refs):
-    first, second, outs = refs[:4], refs[4:8], refs[8:]
-    for group, place, target in ((first, scal_ref[3], outs[:4]), (second, scal_ref[4], outs[4:])):
+    scratch = [pltpu.VMEM((2 * tokens, wide), BF16)]
+    return call(
+        w2_body, part_shapes(width // 32, wide // 2), "head_weight_sums", scratch, VMEM_LIMIT
+    )(*operands)
+
+
+def relay_body(scal_ref, *refs):
+    ins, outs = refs[:6], refs[6:]
+    for n in range(2):
+        held_ref, on_ref, back_ref = ins[3 * n : 3 * n + 3]
+        outs[2 * n][...] = held_ref[0] + on_ref[1]
+        outs[2 * n + 1][...] = held_ref[1] + back_ref[1]
+
+
+def run_relay(scal, *pieces):
+    dims = pieces[0].shape[1:]
+    return call(relay_body, [shape(*dims)] * 4, "relay_sums")(scal, *pieces)
+
+
+def folded(refs, at):
+    keep_ref, on_ref, back_ref, on_2_ref, back_2_ref = refs
+    half = keep_ref.shape[2] // 2
+    low = keep_ref[at, :, :half] + on_2_ref[at] + back_ref[0, at]
+    high = keep_ref[at, :, half:] + on_ref[0, at] + back_2_ref[at]
+    return low, high
+
+
+def fold_1_body(scal_ref, *refs):
+    for n, target in enumerate(refs[10:]):
+        half = target.shape[2] // 2
+        for at in range(SIDE):
+            low, high = folded(refs[5 * n : 5 * n + 5], at)
+            target[at, :, :half] = low
+            target[at, :, half:] = high
+
+
+def run_fold_1(scal, pieces):
+    outs = [shape(*pieces[0].shape)] * 2
+    return call(fold_1_body, outs, "fold_sums")(scal, *pieces)
+
+
+def fold_2_body(scal_ref, *refs):
+    outs = refs[10:]
+    for n in range(2):
         for step in range(SIDE):
-            at = lax.rem(place + step, SIDE)
-            target[step][...] = (group[0][at] + group[1][at]) + (group[2][at] + group[3][at])
-
-
-def run_fold(scal, pieces):
-    dims = pieces[0].shape[1:]
-    return call(fold_body, [shape(*dims)] * 8, "fold_sums", 10**7, 10**7)(scal, *pieces)
-
-
-def end_1_body(scal_ref, *refs):
-    first, second, (gate_ref, up_ref, down_ref) = refs[:4], refs[4:8], refs[8:]
-    one = (first[0][...] + first[1][...]) + (first[2][...] + first[3][...])
-    two = (second[0][...] + second[1][...]) + (second[2][...] + second[3][...])
+            target = outs[SIDE * n + step]
+            half = target.shape[1] // 2
+            low, high = folded(refs[5 * n : 5 * n + 5], lax.rem(scal_ref[3 + n] + step, SIDE))
+            target[:, :half] = low
+            target[:, half:] = high
+
+
+def run_fold_2(scal, pieces):
+    outs = [shape(*pieces[0].shape[1:])] * 8
+    return call(fold_2_body, outs, "fold_parts")(scal, *pieces)
+
+
+def end_1_body(scal_ref, one_ref, two_ref, gate_ref, up_ref, down_ref):
     units = gate_ref.shape[1]
-    rest = one.shape[1] - units
-    gate_ref[...] = one[:, :units]
-    up_ref[:, :rest] = one[:, units:]
-    up_ref[:, rest:] = two[:, : units - rest]
-    down_ref[...] = two[:, units - rest :]
-
-
-def run_end_1(scal, pieces):
-    rows, wide = pieces[0].shape
+    rest = one_ref.shape[1] - units
+    gate_ref[...] = one_ref[:, :units]
+    up_ref[:, :rest] = one_ref[:, units:]
+    up_ref[:, rest:] = two_ref[:, : units - rest]
+    down_ref[...] = two_ref[:, units - rest :]
+
+
+def run_end_1(scal, one, two):
+    rows, wide = one.shape
     outs = [shape(rows, 2 * wide // 3)] * 3
-    return call(end_1_body, outs, "ffn_gradients", 10**6, 3 * 10**6)(scal, *pieces)
+    return call(end_1_body, outs, "ffn_gradients")(scal, one, two)
 
 
 def end_2_body(scal_ref, *refs):
@@ -867,7 +966,7 @@
 def run_end_2(scal, pieces):
     rows = pieces[0].shape[0]
     outs = [shape(rows, WIDE)] * 3 + [shape(rows, HW)] + [shape(rows, WIDE)] * 2
-    return call(end_2_body, outs, "head_gradients", 10**6, 3 * 10**6)(scal, *pieces)
+    return call(end_2_body, outs, "head_gradients")(scal, *pieces)
 
 
 def swap(value):
@@ -884,6 +983,24 @@
         moved[step] = shift(pieces[step], first_axis, step)
         moved[4 + step] = shift(pieces[4 + step], second_axis, step)
     return [pieces[0], moved[1], moved[2], moved[3], pieces[4], moved[5], moved[6], moved[7]]
+
+
+def step_one(pieces):
+    out = []
+    for n, axis in enumerate(("x", "y")):
+        _, on, back, _ = pieces[4 * n : 4 * n + 4]
+        out.append((shift(on, axis, 1), shift(back, axis, SIDE - 1)))
+    return out
+
+
+def step_two(pieces, came, scal):
+    relayed = run_relay(scal, pieces[3], *came[0], pieces[7], *came[1])
+    out = []
+    for n, axis in enumerate(("x", "y")):
+        on = shift(relayed[2 * n], axis, 1)
+        back = shift(relayed[2 * n + 1], axis, SIDE - 1)
+        out += [pieces[4 * n], *came[n], on, back]
+    return relayed, out
 
 
 def trade(value, axis):
@@ -906,78 +1023,86 @@
     unity = (lengths[0] > 0).astype(F32)
     gain_1 = gain_in.reshape(1, width)
     gain_2 = gain_mid.reshape(1, width)
-    w_beta_wide = jnp.pad(w_beta, ((0, 0), (0, HW - w_beta.shape[1])))
-    heads_w = (w_query, w_key, w_value, w_path, w_beta_wide)
-
-    out_half = lax.dynamic_slice_in_dim(w_out, core * (width // 2), width // 2, 1)
-    out_mine = lax.all_gather(out_half.astype(F32), "z", axis=0)
-    out_other = swap(out_mine)
-    grad_other = swap(out_grad)
+    heads_w = (w_query, w_key, w_value, w_path, w_beta.T)
 
     h1, q, k, v, w, aux, inv, kp, b, kt, tu = run_a1(scal, block_input, gain_1, *heads_w)
     both = lax.all_gather(tu, "c", axis=0)
     u_c, spread = run_s1(scal, both)
-    along_x = lax.all_gather(trade(spread, "x"), "c", axis=0)
-    t_x, u_x, spread = run_s2(scal, along_x)
-    c, sc, qt, inside = run_a2(scal, q, k, v, w, inv, kp)
-    along_y = lax.all_gather(trade(spread, "y"), "c", axis=0)
-    t_y, states = run_s3(scal, along_y, t_x, u_x, both, u_c)
+    along_x = trade(spread, "x")
+    out_half = lax.dynamic_slice_in_dim(after(w_out, spread), core * (width // 2), width // 2, 1)
+    out_mine = lax.all_gather(out_half.astype(F32), "z", axis=0)
+    grad_other = swap(after(out_grad, spread))
+    h1_other = swap(after(h1, spread))
+    along_x = after(along_x, grad_other, h1_other)
+    t_x, u_x, spread = run_s2(scal, along_x, swap(along_x))
+    along_y = trade(spread, "y")
+    c, sc, qt, inside = run_a2(scal, after(q, spread), k, v, w, inv, kp)
+    h1_turned = run_turn(scal, after(h1, spread), h1_other)
+    grad_turned = run_turn(scal, after(out_grad, spread), grad_other)
+    along_y = after(along_y, inside, h1_turned, grad_turned)
+    t_y, states = run_s3(scal, along_y, swap(along_y), t_x, u_x, both, u_c)
     states = lax.all_gather(states, "c", axis=0)
-    out_mine_low = (out_mine * unity).astype(BF16)
-    out_other_low = (out_other * unity).astype(BF16)
-    states = after(states, out_mine_low, out_other_low, inside)
     mixed, normed, spread, carried = run_a3(scal, inside, qt, states)
     normed_all = trade(spread, "z")
-    middle, sent, second_part, down_part = run_ffn(
-        scal, normed_all, out_mine_low, out_other_low, block_input, gain_2, out_grad,
-        w_gate, w_up, w_down,
-    )
+    out_mine = after(out_mine, spread)
+    out_mine_low = (out_mine * unity).astype(BF16)
+    out_other_low = (swap(out_mine) * unity).astype(BF16)
+    normed_all = after(normed_all, out_mine_low, out_other_low)
+    middle, h2 = run_middle(scal, normed_all, out_mine_low, out_other_low, block_input, gain_2)
+    sent, second_part, down_part = run_ffn(h2, out_grad, w_gate, w_up, w_down)
 
     second = trade(second_part.reshape(RANKS, PART, width), "z")
-    sent_other = swap(sent)
-    ffn_pieces = run_w1(scal, sent, sent_other, out_grad, grad_other)
+    h2_other = swap(h2)
+    h2_turned = run_turn(scal, after(h2, sent), h2_other)
+    ffn_pieces = run_w1(scal, sent, swap(sent), h2_turned, grad_turned)
     second = after(second, *ffn_pieces)
+    came = step_one(ffn_pieces)
     d_middle, attn, gain_mid_part, d_normed = run_k5(
         scal, second, middle, out_grad, gain_2, out_mine_low, out_other_low
     )
-    ffn_pieces = exchange(ffn_pieces, "x", "y")
+    attn_all = lax.all_gather(attn, "z", axis=0, tiled=True)
     d_normed = trade(d_normed, "z").reshape(tokens, WIDE)
-    block_output = middle + lax.psum(after(down_part, d_normed), "z")
-    attn_all = lax.all_gather(attn, "z", axis=0, tiled=True)
+    down_sum = lax.psum(after(down_part, d_normed), "z")
     dm, state_grad = run_b1(scal, d_normed, mixed, qt)
     pair = lax.all_gather(state_grad, "c", axis=0)
     g_1, spread = run_t1(scal, pair, both)
     g_x = trade(spread, "x")
+    came[0] = (after(came[0][0], spread), came[0][1])
+    relayed, ffn_pieces = step_two(ffn_pieces, came, scal)
+    g_x = after(g_x, *relayed)
     spread = run_t2(scal, g_x, t_x)
+    g_y = trade(spread, "y")
     dq, dk, dv, dw, dkp, xc = run_b2(
-        scal, dm, carried, q, k, v, w, aux, inv, kp, c, sc
+        scal, after(dm, spread), carried, q, k, v, w, aux, inv, kp, c, sc
     )
-    g_y = trade(spread, "y")
+    attn_turned = run_turn(scal, after(attn_all, spread), swap(attn_all))
+    ffn_pieces[0] = after(ffn_pieces[0], dq)
+    ffn_one, ffn_two = run_fold_1(scal, ffn_pieces)
+    g_y = after(g_y, dq, attn_turned, ffn_one)
     later = run_t3(scal, g_y, g_x, t_y, t_x, both, g_1)
     later = lax.all_gather(later, "c", axis=0)
-    ffn_pieces = run_fold(scal, ffn_pieces)
-    later = after(later, *ffn_pieces)
-    ffn_pieces = exchange(ffn_pieces, "y", "x")
-
-    low, first_part = run_b3(
-        scal, block_input, gain_mid_part, later, carried, k, v, w, aux, inv, kp, b, kt,
-        dq, dk, dv, dw, dkp, xc, *heads_w,
+    later = after(later, down_sum)
+    block_output = middle + down_sum
+    ffn_one = lax.psum_scatter(ffn_one, "y", scatter_dimension=0)
+    ffn_two = lax.psum_scatter(ffn_two, "x", scatter_dimension=0)
+
+    low = run_b3(scal, later, carried, k, v, w, aux, inv, kp, b, kt, dk, dv, dw, dkp, xc)
+    low_other = swap(low)
+    first_part = run_b4(scal, block_input, gain_mid_part, dq, low, *heads_w)
+    head_pieces = run_w2(
+        scal, low, low_other, dq, swap(dq), normed, swap(normed), h1_turned, attn_turned
     )
-    first = trade(first_part, "z")
-    gate_out, up_out, down_out = run_end_1(scal, ffn_pieces)
-    low_other = swap(low)
-    head_pieces = run_w2(
-        scal, low, low_other, dq, swap(dq), normed, swap(normed), h1, swap(h1),
-        attn_all, swap(attn_all),
-    )
-    head_pieces = run_fold(scal, exchange(head_pieces, "x", "y"))
-    spread, gains = run_n(scal, first, block_input, gain_1, d_middle)
+    first = trade(after(first_part, head_pieces[0]), "z")
+    relayed, head_pieces = step_two(head_pieces, step_one(head_pieces), scal)
+    spread, gains = run_n(scal, after(first, relayed[0]), block_input, gain_1, d_middle)
     input_grad = trade(spread, "z").reshape(tokens, width)
-    gains = jnp.swapaxes(gains[:2].reshape(2, 32, width // 32), 0, 1)
+    head_pieces = run_fold_2(scal, head_pieces)
+    gains = jnp.swapaxes(after(gains, head_pieces[0])[:2].reshape(2, 32, width // 32), 0, 1)
     gains = jnp.sum(trade(gains, CTX), axis=0)
     key_out, value_out, path_out, beta_out, query_out, out_out = run_end_2(
         scal, exchange(head_pieces, "y", "x")
     )
+    gate_out, up_out, down_out = run_end_1(scal, ffn_one, ffn_two)
     return (
         block_output, input_grad, gains[0], query_out, key_out, value_out, path_out,
         beta_out[:, : w_beta.shape[1]], out_out.T, gains[1], gate_out, up_out, down_out.T,

time: 454 us -> 396 us (0.87)
  blocking collectives: 90.8 us -> 49.7 us
  waiting for transfers between devices: 103 us -> 79 us
  local copies, waits for them, and re-layouts: 15.1 us -> 32.8 us
  starting transfers between devices: 75.7 us -> 66.3 us
    all_to_all x3, blocking collectives: 71.3 us -> 40.7 us  [trade(): return lax.all_to_all(value, axis, 0, 0)]
    all_gather x1, waiting for transfers between devices: 29.3 us -> 0.93 us  [local(): out_mine = lax.all_gather(out_half.astype(F32), 'z', axis=0)]
    ppermute x24 -> x22, waiting for transfers between devices: 26.4 us -> 50.2 us  [shift(): lax.ppermute(value, axis, [(i, (i + step) % SIDE) for i in range(SIDE)])]
    unnamed x61 -> x134, local copies, waits for them, and re-layouts: 11 us -> 29 us
    all_gather x2 -> x0, waiting for transfers between devices: 17.9 us -> none  [the longest x1 12.8 us: local(): along_x = lax.all_gather(trade(spread, 'x'), 'c', axis=0)]
    ppermute x24 -> x22, starting transfers between devices: 44.1 us -> 33.8 us  [shift(): lax.ppermute(value, axis, [(i, (i + step) % SIDE) for i in range(SIDE)])]
    pallas_call x20 -> x26, Pallas kernels: 112 us -> 112 us  [run(): pl.pallas_call(body, out_shape=outs, in_specs=[smem] + [vmem] * (len(oper...]
    pallas_call x1 -> x3, Pallas kernels: 19.4 us -> 19.3 us  [the longest x1 14.7 us: run_ffn(): pl.pallas_call(ffn_body, grid=(steps,), out_shape=outs, in_specs=[whole(h...]
  transfers between devices with their start and end apart: 44 -> 45, of which waited for: 16 -> 18; matrix products, arithmetic and copies ran while one was open for 3% -> 4% of each run, Pallas kernels for 24% -> 24%
where the time goes in v3:
time: 396 us; the launch traced here: 388 us
  Pallas kernels  131 us (33%)
  waiting for transfers between devices  79 us (20%)
  starting transfers between devices  66.3 us (17%)
  blocking collectives  49.7 us (13%)
  local copies, waits for them, and re-layouts  32.8 us (8%)
  between operations  14.8 us (4%)
  other arithmetic  14.2 us (4%)
    pallas_call x26, Pallas kernels, run(): pl.pallas_call(body, out_shape=outs, in_specs=[smem] + [vmem] * (len(oper...  112 us
    ppermute x22, waiting for transfers between devices, shift(): lax.ppermute(value, axis, [(i, (i + step) % SIDE) for i in range(SIDE)])  50.2 us
    all_to_all x3, blocking collectives, trade(): return lax.all_to_all(value, axis, 0, 0)  40.7 us
    ppermute x22, starting transfers between devices, shift(): lax.ppermute(value, axis, [(i, (i + step) % SIDE) for i in range(SIDE)])  33.8 us
    all_to_all x7, starting transfers between devices, trade(): return lax.all_to_all(value, axis, 0, 0)  30.1 us
    unnamed x134, local copies, waits for them, and re-layouts  29 us
    all_to_all x7, waiting for transfers between devices, trade(): return lax.all_to_all(value, axis, 0, 0)  22.2 us
    pallas_call x1, Pallas kernels, run_ffn(): pl.pallas_call(ffn_body, grid=(steps,), out_shape=outs, in_specs=[whole(h...  14.7 us
  transfers between devices with their start and end apart: 45, of which 18 were waited for; matrix products, arithmetic and copies ran while one was open for 4% of the time, Pallas kernels for 24%

profile of v3, /device:TPU:0, one launch (start us, length us, event | category | flops | bytes accessed | tf_op | source)
XLA Modules:
  0.0 388.2 jit_solution(10177970375688354363)
XLA Ops:
  9.8 11.7 %local_parts.1 = (f32[256,1536]{1,0:T(8,128)}, f32[256,384]{1,0:T(8,128)}, f32[256,384]{1,0:T(8,128)}, f32[256,384]{1,0:T(8,128)}, f32[256,384]{1,0:T(8,128)}, /...) custom-call(s32[7]{0:T(128)} %stack.23.scal_ref, ...), custom_call_target="tpu_custom_call" | custom-call | flops 10000 | bytes 10000 | tf_op jit(solution)/shard_map/local_parts/pallas_call | solution.py:237
  27.9 16.8 %all_to_all.50.mine_ref = f32[4,2,3,64,128]{4,3,2,1,0:T(8,128)S(1)} all-to-all(f32[4,2,3,64,128]{4,3,2,1,0:T(8,128)S(1)} %get-tuple-element.128), channel_id=1, replica_groups=mesh['y'=4,'x'=4,'c'=2,'z'=4] {'x'}, dimensions={0} | all-to-all | bytes 1572864 | tf_op jit(solution)/shard_map/all_to_all | solution.py:1007
  49.4 4.9 %all-to-all-start.1 = ((f32[4,2,3,64,128]{4,3,2,1,0:T(8,128)}), f32[4,2,3,64,128]{4,3,2,1,0:T(8,128)S(1)}, u32[]{:S(2)}, u32[]{:S(2)}) async-start(f32[4,2,3,64,128]{4,3,2,1,0:T(8,128)} %get-tuple-element.133), calls=%async_computation.1 | async-start | bytes 1572864 | tf_op jit(solution)/shard_map/all_to_all | solution.py:1007
  54.3 6.9 %inside_parts.1 = (f32[3,256,256]{2,1,0:T(8,128)}, f32[3,256,256]{2,1,0:T(8,128)}, f32[256,384]{1,0:T(8,128)}, f32[256,384]{1,0:T(8,128)}) custom-call(s32[7]{0:T(128)} %stack.23.scal_ref, f32[256,384]{1,0:T(8,128)} %get-tuple-element.134.q_ref, f32[256,384]{1,0:T(8,128)} %get-tuple-element.135.k_ref, f32[256,384]{1,0:T(8,128)} %get-tuple-element.136.v_ref, ...), custom_call_target="tpu_custom_call" | custom-call | flops 10000 | bytes 10000 | tf_op jit(solution)/shard_map/inside_parts/pallas_call | solution.py:237
  82.8 4.5 %all-to-all-start.2 = ((f32[4,256,384]{2,1,0:T(8,128)}), f32[4,256,384]{2,1,0:T(8,128)S(1)}, u32[]{:S(2)}, u32[]{:S(2)}) async-start(f32[4,256,384]{2,1,0:T(8,128)} %get-tuple-element.149), calls=%async_computation.2 | async-start | bytes 3145728 | tf_op jit(solution)/shard_map/all_to_all | solution.py:1007
  88.0 4.2 %multiply_convert_fusion.1.out_mine_ref = bf16[4,384,768]{2,1,0:T(8,128)(2,1)} fusion(f32[4,384,768]{2,1,0:T(8,128)} %bitcast.40, f32[]{:T(128)} %bitcast.9), kind=kLoop, calls=%fused_computation.1 | loop fusion | flops 2359296 | bytes 7077892 | tf_op jit(solution)/shard_map/convert_element_type | solution.py:1048
  96.3 12.2 %all-to-all-done.2.normed_ref = f32[4,256,384]{2,1,0:T(8,128)S(1)} async-done(((f32[4,256,384]{2,1,0:T(8,128)}), f32[4,256,384]{2,1,0:T(8,128)S(1)}, u32[]{:S(2)}, u32[]{:S(2)}) %all-to-all-start.2) | async-done | bytes 1572896 | tf_op jit(solution)/shard_map/all_to_all | solution.py:1007
  109.7 6.9 %middle.1 = (f32[256,1536]{1,0:T(8,128)}, f32[256,1536]{1,0:T(8,128)}) custom-call(s32[7]{0:T(128)} %stack.23.scal_ref, f32[4,256,384]{2,1,0:T(8,128)} %copy-done.57, bf16[4,384,768]{2,1,0:T(8,128)(2,1)} %multiply_convert_fusion.1.out_mine_ref, bf16[4,384,768]{2,1,0:T(8,128)(2,1)} %multiply_convert_fusion.out_other_ref, f32[256,1536]{1,0:T(8,128)} %x_ref.7, ...), custom_call_target="tpu_custom_call" | custom-call | flops 10000 | bytes 10000 | tf_op jit(solution)/shard_map/middle/pallas_call | solution.py:237
  116.6 14.7 %feed_forward.1 = (f32[256,3072]{1,0:T(8,128)}, f32[256,1536]{1,0:T(8,128)}, f32[256,1536]{1,0:T(8,128)}) custom-call(f32[256,1536]{1,0:T(8,128)} %get-tuple-element.158.h_ref.mine_ref, f32[256,1536]{1,0:T(8,128)} %grad_ref.3, bf16[1536,1024]{1,0:T(8,128)(2,1)} %gate_ref.1, bf16[1536,1024]{1,0:T(8,128)(2,1)} %up_ref.1, bf16[1024,1536]{1,0:T(8,128)(2,1)} %down_ref.1), custom_call_target="tpu_custom_call" | custom-call | flops 10000 | bytes 10000 | tf_op jit(solution)/shard_map/feed_forward/pallas_call | solution.py:685
  131.8 4.3 %all-to-all-start.3 = ((f32[4,64,1536]{2,1,0:T(8,128)}), f32[4,64,1536]{2,1,0:T(8,128)}, u32[]{:S(2)}, u32[]{:S(2)}) async-start(f32[4,64,1536]{2,1,0:T(8,128)} %bitcast.42), calls=%async_computation.3 | async-start | bytes 3145728 | tf_op jit(solution)/shard_map/all_to_all | solution.py:1007
  142.5 9.9 %ffn_weight_sums.1 = (f32[4,48,1536]{2,1,0:T(8,128)}, f32[2,4,48,768]{3,2,1,0:T(8,128)}, f32[2,4,48,768]{3,2,1,0:T(8,128)}, f32[2,4,48,768]{3,2,1,0:T(8,128)}, f...) custom-call(s32[7]{0:T(128)} %stack.23.scal_ref, ...), custom_call_target="tpu_custom_call" | custom-call | flops 10000 | bytes 10000 | tf_op jit(solution)/shard_map/ffn_weight_sums/pallas_call | solution.py:237
  152.4 5.0 %all-to-all-done.3.second_ref = f32[4,64,1536]{2,1,0:T(8,128)} async-done(((f32[4,64,1536]{2,1,0:T(8,128)}), f32[4,64,1536]{2,1,0:T(8,128)}, u32[]{:S(2)}, u32[]{:S(2)}) %all-to-all-start.3) | async-done | bytes 1572896 | tf_op jit(solution)/shard_map/all_to_all | solution.py:1007
  185.0 15.9 %collective-permute-done.7.refs_1_ = f32[2,4,48,768]{3,2,1,0:T(8,128)S(1)} collective-permute-done((f32[2,4,48,768]{3,2,1,0:T(8,128)}, f32[2,4,48,768]{3,2,1,0:T(8,128)S(1)}, u32[]{:S(2)}, u32[]{:S(2)}) %collective-permute-start.7) | collective-permute-done | bytes 1179680 | tf_op jit(solution)/shard_map/ppermute | solution.py:977
  214.4 12.0 %all_to_all.51.g_ref.gx_ref = f32[4,3,64,128]{3,2,1,0:T(8,128)S(1)} all-to-all(f32[4,3,64,128]{3,2,1,0:T(8,128)S(1)} %get-tuple-element.174), channel_id=1, replica_groups=mesh['y'=4,'x'=4,'c'=2,'z'=4] {'x'}, dimensions={0} | all-to-all | bytes 786432 | tf_op jit(solution)/shard_map/all_to_all | solution.py:1007
  228.8 9.5 %inside_gradients.1 = (f32[256,384]{1,0:T(8,128)}, f32[256,384]{1,0:T(8,128)}, f32[256,384]{1,0:T(8,128)}, f32[256,384]{1,0:T(8,128)}, f32[3,256,256]{2,1,0:T(8,128)}, /*index=5*/f32[3,256,256]{2,1,0:T(8,128)}) custom-call(s32[7]{0:T(128)} %stack.23.scal_ref, f32[256,384]{1,0:T(8,128)} %copy-done.29, f32[3,128,128]{2,1,0:T(8,128)} %copy-done.20, ...), custom_call_target="tpu_custom_call" | custom-call | flops 10000 | bytes 10000 | tf_op jit(solution)/shard_map/inside_gradients/pallas_call | solution.py:237
  261.4 9.9 %late_gradients.1.low_ref = f32[256,1280]{1,0:T(8,128)} custom-call(s32[7]{0:T(128)} %stack.23.scal_ref, f32[2,2,3,64,128]{4,3,2,1,0:T(8,128)} %bitcast.41, f32[3,128,128]{2,1,0:T(8,128)} %copy-done.20, f32[256,384]{1,0:T(8,128)} %get-tuple-element.135.k_ref, f32[256,384]{1,0:T(8,128)} %get-tuple-element.136.v_ref, f32[256,384]{1,0:T(8,128)} %get-tuple-element.137.w_ref, ...), custom_call_target="tpu_custom_call" | custom-call | flops 10000 | bytes 10000 | tf_op jit(solution)/shard_map/late_gradients/pallas_call | solution.py:237
  272.3 6.7 %first_norm_part.1 = f32[4,72,1536]{2,1,0:T(8,128)} custom-call(s32[7]{0:T(128)} %stack.23.scal_ref, f32[256,1536]{1,0:T(8,128)} %x_ref.7, f32[1,1536]{1,0:T(1,128)} %copy-done.49, f32[256,384]{1,0:T(8,128)} %get-tuple-element.186.dq_ref, f32[256,1280]{1,0:T(8,128)} %late_gradients.1.low_ref, bf16[1536,384]{1,0:T(8,128)(2,1)} %wq_ref.3, ...), custom_call_target="tpu_custom_call" | custom-call | flops 10000 | bytes 10000 | tf_op jit(solution)/shard_map/first_norm_part/pallas_call | solution.py:237
  281.0 7.5 %head_weight_sums.1 = (f32[4,48,1024]{2,1,0:T(8,128)}, f32[2,4,48,512]{3,2,1,0:T(8,128)}, f32[2,4,48,512]{3,2,1,0:T(8,128)}, f32[2,4,48,512]{3,2,1,0:T(8,128)}, ...) custom-call(s32[7]{0:T(128)} %stack.23.scal_ref, ...), custom_call_target="tpu_custom_call" | custom-call | flops 10000 | bytes 10000 | tf_op jit(solution)/shard_map/head_weight_sums/pallas_call | solution.py:237
  288.5 4.2 %all-to-all-start.7 = ((f32[4,72,1536]{2,1,0:T(8,128)}), f32[4,72,1536]{2,1,0:T(8,128)S(1)}, u32[]{:S(2)}, u32[]{:S(2)}) async-start(f32[4,72,1536]{2,1,0:T(8,128)} %first_norm_part.1), calls=%async_computation.7 | async-start | bytes 3538944 | tf_op jit(solution)/shard_map/all_to_all | solution.py:1007
  299.2 15.8 %collective-permute-done.19.refs_1_ = f32[2,4,48,512]{3,2,1,0:T(8,128)S(1)} collective-permute-done((f32[2,4,48,512]{3,2,1,0:T(8,128)}, f32[2,4,48,512]{3,2,1,0:T(8,128)S(1)}, u32[]{:S(2)}, u32[]{:S(2)}) %collective-permute-start.19) | collective-permute-done | bytes 786464 | tf_op jit(solution)/shard_map/ppermute | solution.py:977
  323.7 4.4 %collective-permute-done.23.refs_3_ = f32[4,48,512]{2,1,0:T(8,128)S(1)} collective-permute-done((f32[4,48,512]{2,1,0:T(8,128)S(1)}, f32[4,48,512]{2,1,0:T(8,128)S(1)}, u32[]{:S(2)}, u32[]{:S(2)}) %collective-permute-start.23) | collective-permute-done | bytes 393248 | tf_op jit(solution)/shard_map/ppermute | solution.py:977
  338.1 11.9 %all_to_all.52 = f32[32,2,48]{2,1,0:T(2,128)} all-to-all(f32[32,2,48]{2,1,0:T(2,128)S(1)} %bitcast.43), channel_id=1, replica_groups=mesh['y'=4,'x'=4,'c'=2,'z'=4] {'y','x','c'}, dimensions={0} | all-to-all | bytes 24576 | tf_op jit(solution)/shard_map/all_to_all | solution.py:1007
  350.0 4.5 %all-to-all-start.8 = ((f32[4,64,1536]{2,1,0:T(8,128)}), f32[4,64,1536]{2,1,0:T(8,128)}, u32[]{:S(2)}, u32[]{:S(2)}) async-start(f32[4,64,1536]{2,1,0:T(8,128)} %copy-done.9), calls=%async_computation.8 | async-start | bytes 3145728 | tf_op jit(solution)/shard_map/all_to_all | solution.py:1007
  369.7 4.1 %collective-permute-done.29.refs_3_ = f32[48,1024]{1,0:T(8,128)S(1)} collective-permute-done((f32[48,1024]{1,0:T(8,128)}, f32[48,1024]{1,0:T(8,128)S(1)}, u32[]{:S(2)}, u32[]{:S(2)}) %collective-permute-start.29) | collective-permute-done | bytes 196640 | tf_op jit(solution)/shard_map/ppermute | solution.py:977
  (253 shorter events, 164.8 us)
Async XLA Ops:
  7.2 75.6 %all-gather.10.cloned.1.call-start = ((), (), s32[]{:S(2)}) async-start(), calls=%async_computation.16 | async-start | bytes 5898240 | tf_op jit(solution)/shard_map/all_gather | solution.py:1033
  27.3 17.4 %collective-permute-start = (f32[256,1536]{1,0:T(8,128)S(1)}, f32[256,1536]{1,0:T(8,128)S(1)}, u32[]{:S(2)}, u32[]{:S(2)}) collective-permute-start(f32[256,1536]{1,0:T(8,128)S(1)} %copy-done.3), channel_id=1, source_target_pairs={{0,4},{4,0},{1,5},{5,1},{2,6},{6,2},{3,7},{7,3},{8,12},{12,8},{9,1... | collective-permute-start | bytes 4718600 | tf_op jit(solution)/shard_map/ppermute | solution.py:973
  49.4 19.1 %all-to-all-start.1 = ((f32[4,2,3,64,128]{4,3,2,1,0:T(8,128)}), f32[4,2,3,64,128]{4,3,2,1,0:T(8,128)S(1)}, u32[]{:S(2)}, u32[]{:S(2)}) async-start(f32[4,2,3,64,128]{4,3,2,1,0:T(8,128)} %get-tuple-element.133), calls=%async_computation.1 | async-start | bytes 1572864 | tf_op jit(solution)/shard_map/all_to_all | solution.py:1007
  82.8 25.8 %all-to-all-start.2 = ((f32[4,256,384]{2,1,0:T(8,128)}), f32[4,256,384]{2,1,0:T(8,128)S(1)}, u32[]{:S(2)}, u32[]{:S(2)}) async-start(f32[4,256,384]{2,1,0:T(8,128)} %get-tuple-element.149), calls=%async_computation.2 | async-start | bytes 3145728 | tf_op jit(solution)/shard_map/all_to_all | solution.py:1007
  131.8 25.6 %all-to-all-start.3 = ((f32[4,64,1536]{2,1,0:T(8,128)}), f32[4,64,1536]{2,1,0:T(8,128)}, u32[]{:S(2)}, u32[]{:S(2)}) async-start(f32[4,64,1536]{2,1,0:T(8,128)} %bitcast.42), calls=%async_computation.3 | async-start | bytes 3145728 | tf_op jit(solution)/shard_map/all_to_all | solution.py:1007
  136.1 78.3 %all-gather.8.cloned.1.call-start = ((), (), s32[]{:S(2)}) async-start(), calls=%async_computation.13 | async-start | bytes 1966080 | tf_op jit(solution)/shard_map/all_gather | solution.py:1063
  172.2 89.2 %all-reduce.2.cloned.1.call-start = ((), (), s32[]{:S(2)}) async-start(), calls=%async_computation.12 | async-start | bytes 3145728 | tf_op jit(solution)/shard_map/psum | solution.py:1065
  172.3 28.6 %collective-permute-start.7 = (f32[2,4,48,768]{3,2,1,0:T(8,128)}, f32[2,4,48,768]{3,2,1,0:T(8,128)S(1)}, u32[]{:S(2)}, u32[]{:S(2)}) collective-permute-start(f32[2,4,48,768]{3,2,1,0:T(8,128)} %get-tuple-element.160), channel_id=1, source_target_pairs={{0,8},{8,16},{16,24},{24,0},{1,9},{9,17},{17,25},{25,1},{2,10},{10... | collective-permute-start | bytes 3538952 | tf_op jit(solution)/shard_map/ppermute | solution.py:977
  173.3 27.6 %collective-permute-start.8 = (f32[2,4,48,768]{3,2,1,0:T(8,128)}, f32[2,4,48,768]{3,2,1,0:T(8,128)}, u32[]{:S(2)}, u32[]{:S(2)}) collective-permute-start(f32[2,4,48,768]{3,2,1,0:T(8,128)} %get-tuple-element.161), channel_id=1, source_target_pairs={{0,24},{8,0},{16,8},{24,16},{1,25},{9,1},{17,9},{25,17},{2,26},{10... | collective-permute-start | bytes 3538952 | tf_op jit(solution)/shard_map/ppermute | solution.py:977
  175.6 28.3 %collective-permute-start.9 = (f32[2,4,48,768]{3,2,1,0:T(8,128)}, f32[2,4,48,768]{3,2,1,0:T(8,128)}, u32[]{:S(2)}, u32[]{:S(2)}) collective-permute-start(f32[2,4,48,768]{3,2,1,0:T(8,128)} %get-tuple-element.164), channel_id=1, source_target_pairs={{0,32},{32,64},{64,96},{96,0},{1,33},{33,65},{65,97},{97,1},{2,34}... | collective-permute-start | bytes 3538952 | tf_op jit(solution)/shard_map/ppermute | solution.py:977
  177.6 26.6 %collective-permute-start.10 = (f32[2,4,48,768]{3,2,1,0:T(8,128)}, f32[2,4,48,768]{3,2,1,0:T(8,128)}, u32[]{:S(2)}, u32[]{:S(2)}) collective-permute-start(f32[2,4,48,768]{3,2,1,0:T(8,128)} %get-tuple-element.165), channel_id=1, source_target_pairs={{0,96},{32,0},{64,32},{96,64},{1,97},{33,1},{65,33},{97,65},{2,98}... | collective-permute-start | bytes 3538952 | tf_op jit(solution)/shard_map/ppermute | solution.py:977
  180.0 177.8 %reduce-scatter.3.cloned.1.call-start = ((), (), s32[]{:S(2)}) async-start(), calls=%async_computation.14 | async-start | bytes 1474560 | tf_op jit(solution)/shard_map/reduce_scatter | solution.py:1086
  207.9 30.5 %collective-permute-start.12 = (f32[4,48,768]{2,1,0:T(8,128)}, f32[4,48,768]{2,1,0:T(8,128)}, u32[]{:S(2)}, u32[]{:S(2)}) collective-permute-start(f32[4,48,768]{2,1,0:T(8,128)} %get-tuple-element.176), channel_id=1, source_target_pairs={{0,8},{8,16},{16,24},{24,0},{1,9},{9,17},{17,25},{25,1},{2,10},{10... | collective-permute-start | bytes 1769480 | tf_op jit(solution)/shard_map/ppermute | solution.py:977
  207.9 30.5 %collective-permute-start.13 = (f32[4,48,768]{2,1,0:T(8,128)}, f32[4,48,768]{2,1,0:T(8,128)}, u32[]{:S(2)}, u32[]{:S(2)}) collective-permute-start(f32[4,48,768]{2,1,0:T(8,128)} %get-tuple-element.177), channel_id=1, source_target_pairs={{0,24},{8,0},{16,8},{24,16},{1,25},{9,1},{17,9},{25,17},{2,26},{10... | collective-permute-start | bytes 1769480 | tf_op jit(solution)/shard_map/ppermute | solution.py:977
  211.1 27.2 %collective-permute-start.14 = (f32[4,48,768]{2,1,0:T(8,128)}, f32[4,48,768]{2,1,0:T(8,128)}, u32[]{:S(2)}, u32[]{:S(2)}) collective-permute-start(f32[4,48,768]{2,1,0:T(8,128)} %get-tuple-element.178), channel_id=1, source_target_pairs={{0,32},{32,64},{64,96},{96,0},{1,33},{33,65},{65,97},{97,1},{2,34}... | collective-permute-start | bytes 1769480 | tf_op jit(solution)/shard_map/ppermute | solution.py:977
  212.7 25.7 %collective-permute-start.15 = (f32[4,48,768]{2,1,0:T(8,128)}, f32[4,48,768]{2,1,0:T(8,128)}, u32[]{:S(2)}, u32[]{:S(2)}) collective-permute-start(f32[4,48,768]{2,1,0:T(8,128)} %get-tuple-element.179), channel_id=1, source_target_pairs={{0,96},{32,0},{64,32},{96,64},{1,97},{33,1},{65,33},{97,65},{2,98}... | collective-permute-start | bytes 1769480 | tf_op jit(solution)/shard_map/ppermute | solution.py:977
  214.4 33.0 %collective-permute-start.11 = (f32[256,1536]{1,0:T(8,128)}, f32[256,1536]{1,0:T(8,128)}, u32[]{:S(2)}, u32[]{:S(2)}) collective-permute-start(f32[256,1536]{1,0:T(8,128)} %all-gather.8.cloned.1.call-done.mine_ref), channel_id=1, source_target_pairs={{0,4},{4,0},{1,5},{5,1},{2,6},{6,2},{3,7},{7,3},{8,12},{12,8},{9,1... | collective-permute-start | bytes 4718600 | tf_op jit(solution)/shard_map/ppermute | solution.py:973
  247.3 110.5 %reduce-scatter.5.cloned.1.call-start = ((), (), s32[]{:S(2)}) async-start(), calls=%async_computation.15 | async-start | bytes 1474560 | tf_op jit(solution)/shard_map/reduce_scatter | solution.py:1087
  288.5 46.6 %all-to-all-start.7 = ((f32[4,72,1536]{2,1,0:T(8,128)}), f32[4,72,1536]{2,1,0:T(8,128)S(1)}, u32[]{:S(2)}, u32[]{:S(2)}) async-start(f32[4,72,1536]{2,1,0:T(8,128)} %first_norm_part.1), calls=%async_computation.7 | async-start | bytes 3538944 | tf_op jit(solution)/shard_map/all_to_all | solution.py:1007
  292.7 22.2 %collective-permute-start.19 = (f32[2,4,48,512]{3,2,1,0:T(8,128)}, f32[2,4,48,512]{3,2,1,0:T(8,128)S(1)}, u32[]{:S(2)}, u32[]{:S(2)}) collective-permute-start(f32[2,4,48,512]{3,2,1,0:T(8,128)} %get-tuple-element.206), channel_id=1, source_target_pairs={{0,8},{8,16},{16,24},{24,0},{1,9},{9,17},{17,25},{25,1},{2,10},{10... | collective-permute-start | bytes 2359304 | tf_op jit(solution)/shard_map/ppermute | solution.py:977
  294.0 21.0 %collective-permute-start.20 = (f32[2,4,48,512]{3,2,1,0:T(8,128)}, f32[2,4,48,512]{3,2,1,0:T(8,128)S(1)}, u32[]{:S(2)}, u32[]{:S(2)}) collective-permute-start(f32[2,4,48,512]{3,2,1,0:T(8,128)} %get-tuple-element.207), channel_id=1, source_target_pairs={{0,24},{8,0},{16,8},{24,16},{1,25},{9,1},{17,9},{25,17},{2,26},{10... | collective-permute-start | bytes 2359304 | tf_op jit(solution)/shard_map/ppermute | solution.py:977
  296.0 20.4 %collective-permute-start.21 = (f32[2,4,48,512]{3,2,1,0:T(8,128)}, f32[2,4,48,512]{3,2,1,0:T(8,128)S(1)}, u32[]{:S(2)}, u32[]{:S(2)}) collective-permute-start(f32[2,4,48,512]{3,2,1,0:T(8,128)} %get-tuple-element.209), channel_id=1, source_target_pairs={{0,32},{32,64},{64,96},{96,0},{1,33},{33,65},{65,97},{97,1},{2,34}... | collective-permute-start | bytes 2359304 | tf_op jit(solution)/shard_map/ppermute | solution.py:977
  296.5 19.9 %collective-permute-start.22 = (f32[2,4,48,512]{3,2,1,0:T(8,128)}, f32[2,4,48,512]{3,2,1,0:T(8,128)S(1)}, u32[]{:S(2)}, u32[]{:S(2)}) collective-permute-start(f32[2,4,48,512]{3,2,1,0:T(8,128)} %get-tuple-element.210), channel_id=1, source_target_pairs={{0,96},{32,0},{64,32},{96,64},{1,97},{33,1},{65,33},{97,65},{2,98}... | collective-permute-start | bytes 2359304 | tf_op jit(solution)/shard_map/ppermute | solution.py:977
  350.0 28.5 %all-to-all-start.8 = ((f32[4,64,1536]{2,1,0:T(8,128)}), f32[4,64,1536]{2,1,0:T(8,128)}, u32[]{:S(2)}, u32[]{:S(2)}) async-start(f32[4,64,1536]{2,1,0:T(8,128)} %copy-done.9), calls=%async_computation.8 | async-start | bytes 3145728 | tf_op jit(solution)/shard_map/all_to_all | solution.py:1007
  (87 other events, 718.5 us)
Sparse Core Ops, SparseCore 0:
  27.4 55.3 all-gather.9
  168.8 25.4 all-gather.7
  196.6 50.6 all-reduce.1
  249.6 24.0 reduce-scatter.2
  276.0 25.0 reduce-scatter.4
